TPU v7x, 256 devices: a whole 4x4x8 slice. The times are simulated.
256 devices in a mesh: pop: 32 (over y, z_lo, core), tp: 8 (over z_hi, x).
Axes of the slice: x: 4, y: 4, z: 8 (z_hi: 2, z_lo: 4; z = z_hi * 4 + z_lo), core: 2. Of those that a mesh axis runs over, the one named last changes fastest.
Arguments:
- gate_left: bfloat16 [256, 4, 8192], P(('pop', 'tp')), may hold values from -6 to 6
- up_left: bfloat16 [256, 4, 8192], P(('pop', 'tp')), may hold values from -6 to 6
- gate_right: bfloat16 [256, 4, 28672], P('pop', None, 'tp'), may hold values from -6 to 6
- up_right: bfloat16 [256, 4, 28672], P('pop', None, 'tp'), may hold values from -6 to 6
- fitness_order: int32 [256], P(('pop', 'tp')), may hold values from 0 to 255, each once
- member_scale: float32 [256], P(('pop', 'tp')), may hold values from 0.5 to 2
Outputs:
- gate_grad: bfloat16 [8192, 28672], P('pop', 'tp')
- up_grad: bfloat16 [8192, 28672], P('pop', 'tp')
Inputs may be any that keep to these rules, and one draw needn't show every extreme that they name: `fitness_order`: each of 0 to 255 appears once.
All inputs are finite; a program needn't handle non-finite values.
Results may differ from a plain program's by a relative error of at most 0.0049.
Values may be sent and summed in bfloat16 or wider, within the bound.
No kernel may reach another device: no remote copies, remote signals or barrier semaphores. Data moves between devices by JAX's collectives and lax.ppermute only.
A program may use at most 128 MiB of HBM per device.

v0:
```python
import math

import jax
import jax.numpy as jnp
from jax import lax
from jax.sharding import PartitionSpec as P


def weigh(left, coef):
    return (coef[:, None, None] * left.astype(jnp.float32)).astype(jnp.bfloat16)


def contract(left, right):
    return lax.dot_general(
        left, right, (((0, 1), (0, 1)), ((), ())), preferred_element_type=jnp.float32
    )


def shards(gate_left, up_left, gate_right, up_right, fitness_order, member_scale):
    pop_count = lax.axis_size("pop")
    tp_count = lax.axis_size("tp")
    local_count = fitness_order.shape[0]
    total = local_count * pop_count * tp_count
    centered = (2 * fitness_order - (total - 1)).astype(jnp.float32)
    coef = centered * member_scale / ((total - 1) * math.sqrt(total * gate_left.shape[1]))
    grouped = (
        lax.all_gather(gate_left, "tp", axis=0, tiled=True),
        lax.all_gather(up_left, "tp", axis=0, tiled=True),
    )
    gate_rows, up_rows = (
        lax.all_to_all(grouped[0], "pop", split_axis=2, concat_axis=0, tiled=True),
        lax.all_to_all(grouped[1], "pop", split_axis=2, concat_axis=0, tiled=True),
    )
    all_coef = lax.all_gather(coef, ("pop", "tp"), axis=0, tiled=True)
    gate_rows = weigh(gate_rows, all_coef)
    up_rows = weigh(up_rows, all_coef)

    def add_part(rows, piece):
        return contract(rows, piece)

    gate_sum = add_part(gate_rows, lax.all_gather(gate_right, "pop", axis=0, tiled=True))
    up_sum = add_part(up_rows, lax.all_gather(up_right, "pop", axis=0, tiled=True))
    return (gate_sum.astype(jnp.bfloat16), up_sum.astype(jnp.bfloat16))


def solution(mesh):
    in_specs = (
        P(("pop", "tp"), None, None),
        P(("pop", "tp"), None, None),
        P("pop", None, "tp"),
        P("pop", None, "tp"),
        P(("pop", "tp")),
        P(("pop", "tp")),
    )
    out_specs = (P("pop", "tp"), P("pop", "tp"))
    return jax.shard_map(shards, mesh=mesh, in_specs=in_specs, out_specs=out_specs, check_vma=False)
```

profile of v0, /device:TPU:1, one launch (start us, length us, event | category | flops | bytes accessed | tf_op | source)
XLA Modules:
  0.0 309.3 jit_solution(12631340301411213424)
XLA Ops:
  7.2 0.0 all-gather.3.cloned.1.call-start
  7.2 1.7 copy.47
  8.9 0.0 all-gather.5.cloned.1.call-start
  8.9 1.7 copy.52
  10.7 42.7 %all_gather.16 = bf16[8,4,8192]{2,1,0:T(4,128)(2,1)S(1)} all-gather(bf16[1,4,8192]{2,1,0:T(4,128)(2,1)} %param.6), channel_id=1, replica_groups=mesh['pop'=32,'tp'=8] {'tp'}, dimensions={0}, use_global_device_ids=true | all-gather | bytes 589824 | tf_op jit(solution)/shard_map/all_gather | solution.py:27
  53.4 8.3 %copy.44 = bf16[8,4,8192]{0,1,2:T(4,128)(2,1)} copy(bf16[8,4,8192]{2,1,0:T(4,128)(2,1)S(1)} %all_gather.16) | data formatting | bytes 1048576 | tf_op jit(solution)/shard_map/all_gather | solution.py:27
  61.7 11.3 %reshape.21 = bf16[32,2,4096]{2,1,0:T(2,128)(2,1)} reshape(bf16[8192,4,8]{2,1,0:T(4,128)(2,1)} %bitcast.46) | data formatting | bytes 1048576
  72.9 13.0 %all-to-all-start = ((bf16[32,2,4096]{2,1,0:T(2,128)(2,1)}), bf16[32,2,4096]{2,1,0:T(2,128)(2,1)S(1)}, u32[]{:S(2)}, u32[]{:S(2)}) async-start(bf16[32,2,4096]{2,1,0:T(2,128)(2,1)} %reshape.21), calls=%async_computation | async-start | bytes 1048576 | tf_op jit(solution)/shard_map/all_to_all | solution.py:31
  86.0 47.2 %all_gather.18 = bf16[8,4,8192]{2,1,0:T(4,128)(2,1)S(1)} all-gather(bf16[1,4,8192]{2,1,0:T(4,128)(2,1)S(1)} %copy-done), channel_id=1, replica_groups=mesh['pop'=32,'tp'=8] {'tp'}, dimensions={0}, use_global_device_ids=true | all-gather | bytes 589824 | tf_op jit(solution)/shard_map/all_gather | solution.py:28
  133.2 8.3 %copy.49 = bf16[8,4,8192]{0,1,2:T(4,128)(2,1)} copy(bf16[8,4,8192]{2,1,0:T(4,128)(2,1)S(1)} %all_gather.18) | data formatting | bytes 1048576 | tf_op jit(solution)/shard_map/all_gather | solution.py:28
  141.5 11.3 %reshape.23 = bf16[32,2,4096]{2,1,0:T(2,128)(2,1)} reshape(bf16[8192,4,8]{2,1,0:T(4,128)(2,1)} %bitcast.47) | data formatting | bytes 1048576
  152.8 16.8 %all-to-all-start.1 = ((bf16[32,2,4096]{2,1,0:T(2,128)(2,1)}), bf16[32,2,4096]{2,1,0:T(2,128)(2,1)S(1)}, u32[]{:S(2)}, u32[]{:S(2)}) async-start(bf16[32,2,4096]{2,1,0:T(2,128)(2,1)} %reshape.23), calls=%async_computation.1 | async-start | bytes 1048576 | tf_op jit(solution)/shard_map/all_to_all | solution.py:32
  170.9 0.1 multiply_dynamic-update-slice_fusion
  171.0 75.5 %all-reduce = f32[256]{0:T(256)S(1)} all-reduce(f32[256]{0:T(256)S(1)} %multiply_dynamic-update-slice_fusion), channel_id=1, replica_groups=mesh['pop'=32,'tp'=8] {'pop','tp'}, use_global_device_ids=true, to_apply=%add | all-reduce | flops 256 | bytes 2048
  246.5 10.9 %reshape.22 = bf16[8192,4,8]{2,1,0:T(4,128)(2,1)} reshape(bf16[32,2,4096]{2,1,0:T(2,128)(2,1)S(1)} %all-to-all-done) | data formatting | bytes 1048576
  257.4 9.7 %copy.45 = bf16[8,4,8192]{2,0,1:T(8,128)(2,1)S(1)} copy(bf16[8,4,8192]{0,1,2:T(4,128)(2,1)} %bitcast.48) | data formatting | bytes 1048576 | tf_op jit(solution)/shard_map/all_to_all | solution.py:31
  267.1 0.1 convert_element_type.56
  267.2 0.3 copy.65
  267.6 10.9 %reshape.24 = bf16[8192,4,8]{2,1,0:T(4,128)(2,1)} reshape(bf16[32,2,4096]{2,1,0:T(2,128)(2,1)S(1)} %all-to-all-done.1) | data formatting | bytes 1048576
  278.5 9.7 %copy.50 = bf16[8,4,8192]{2,0,1:T(8,128)(2,1)S(1)} copy(bf16[8,4,8192]{0,1,2:T(4,128)(2,1)} %bitcast.49) | data formatting | bytes 1048576 | tf_op jit(solution)/shard_map/all_to_all | solution.py:32
  288.2 0.1 convert_element_type.57
  288.3 0.3 copy.64
  288.7 6.9 %fusion = bf16[256,3584]{1,0:T(8,128)(2,1)} fusion(bf16[256,4,3584]{2,0,1:T(8,128)(2,1)} %all-gather.3.cloned.1.call-done, f32[32,8,4,256]{3,0,1,2:T(8,128)S(1)} %bitcast.50, f32[256]{0:T(256)S(1)} %all-reduce), kind=kOutput, calls=%fused_computation.2 | convolution fusion | flops 1880489984 | bytes 10224640 | tf_op jit(solution)/shard_map/dot_general | solution.py:14
  295.6 6.9 %fusion.1 = bf16[256,3584]{1,0:T(8,128)(2,1)} fusion(bf16[256,4,3584]{2,0,1:T(8,128)(2,1)} %all-gather.5.cloned.1.call-done, f32[32,8,4,256]{3,0,1,2:T(8,128)S(1)} %bitcast.51, f32[256]{0:T(256)S(1)} %all-reduce), kind=kOutput, calls=%fused_computation.3 | convolution fusion | flops 1880489984 | bytes 10224640 | tf_op jit(solution)/shard_map/dot_general | solution.py:14
  (9 shorter events, 0.1 us)
Async XLA Ops:
  7.2 281.5 %all-gather.3.cloned.1.call-start = ((), (), s32[]{:S(2)}) async-start(), calls=%async_computation.2 | async-start | bytes 7569408 | tf_op jit(solution)/shard_map/all_gather | solution.py:41
  8.9 286.7 %all-gather.5.cloned.1.call-start = ((), (), s32[]{:S(2)}) async-start(), calls=%async_computation.3 | async-start | bytes 7569408 | tf_op jit(solution)/shard_map/all_gather | solution.py:42
  53.4 32.6 %copy-start = (bf16[1,4,8192]{2,1,0:T(4,128)(2,1)S(1)}, bf16[1,4,8192]{2,1,0:T(4,128)(2,1)}, u32[]{:S(2)}) copy-start(bf16[1,4,8192]{2,1,0:T(4,128)(2,1)} %param.7) | copy-start | bytes 196612
  72.9 79.9 %all-to-all-start = ((bf16[32,2,4096]{2,1,0:T(2,128)(2,1)}), bf16[32,2,4096]{2,1,0:T(2,128)(2,1)S(1)}, u32[]{:S(2)}, u32[]{:S(2)}) async-start(bf16[32,2,4096]{2,1,0:T(2,128)(2,1)} %reshape.21), calls=%async_computation | async-start | bytes 1048576 | tf_op jit(solution)/shard_map/all_to_all | solution.py:31
  152.8 114.7 %all-to-all-start.1 = ((bf16[32,2,4096]{2,1,0:T(2,128)(2,1)}), bf16[32,2,4096]{2,1,0:T(2,128)(2,1)S(1)}, u32[]{:S(2)}, u32[]{:S(2)}) async-start(bf16[32,2,4096]{2,1,0:T(2,128)(2,1)} %reshape.23), calls=%async_computation.1 | async-start | bytes 1048576 | tf_op jit(solution)/shard_map/all_to_all | solution.py:32
Sparse Core Ops, SparseCore 0:
  9.8 73.9 all-gather.2
  85.6 70.7 all-gather.4
where the time goes:
time: 311 us; the launch traced here: 309 us
  blocking collectives  165 us (53%)
  local copies, waits for them, and re-layouts  84.4 us (27%)
  starting transfers between devices  29.9 us (10%)
  between operations  15.4 us (5%)
  matrix products  13.8 us (4%)
    unnamed x1, blocking collectives  75.5 us
    unnamed x11, local copies, waits for them, and re-layouts  48.4 us
    all_gather x1, blocking collectives, shards(): lax.all_gather(up_left, 'tp', axis=0, tiled=True)  47.2 us
    all_gather x1, blocking collectives, shards(): lax.all_gather(gate_left, 'tp', axis=0, tiled=True)  42.7 us
    all_to_all x1, starting transfers between devices, shards(): lax.all_to_all(grouped[1], 'pop', split_axis=2, concat_axis=0, tiled=True)  16.8 us
    dot_general x2, matrix products, contract(): lax.dot_general(left, right, (((0, 1), (0, 1)), ((), ())), preferred_elem...  13.8 us
    all_to_all x1, starting transfers between devices, shards(): lax.all_to_all(grouped[0], 'pop', split_axis=2, concat_axis=0, tiled=True)  13 us
    all_to_all x1, local copies, waits for them, and re-layouts, shards(): lax.all_to_all(grouped[0], 'pop', split_axis=2, concat_axis=0, tiled=True)  9.73 us
  transfers between devices with their start and end apart: 4, of which 0 were waited for; matrix products, arithmetic and copies ran while one was open for 29% of the time, Pallas kernels for 0%

commit v1 on v0

v1 whole, which is shorter than its diff:
```python
import functools
import math

import jax
import jax.numpy as jnp
from jax import lax
from jax.experimental import pallas as pl
from jax.experimental.pallas import tpu as pltpu
from jax.sharding import Mesh, PartitionSpec as P

Y, Z, C, H, X = 4, 4, 2, 2, 4
FIRST = 512


def shift(x, axis, by):
    n = lax.axis_size(axis)
    return lax.ppermute(x, axis, [(i, (i + by) % n) for i in range(n)])


def spread(x):
    half = x.shape[0] // 2
    up, down = shift(x, "y", 1), shift(x, "y", -1)
    return up, down, shift(up[:half], "y", 1), shift(down[half:], "y", -1)


def left_kernel(place_ref, left_ref, out_ref):
    y, z = place_ref[0], place_ref[1]
    for d in range(Z):
        parts = []
        for j in (0, 1, Y - 1, 2):
            chip = lax.rem(y + Y - j, Y) * Z + lax.rem(z + Z - d, Z)
            parts += [left_ref[x, h, chip].astype(jnp.float32) for h in range(H) for x in range(X)]
        out_ref[d] = jnp.concatenate(parts, axis=0).T.astype(out_ref.dtype)


def arrange_left(place, left):
    rows = left.shape[-1]
    depth = Y * H * X * left.shape[3]
    return pl.pallas_call(
        left_kernel,
        out_shape=jax.ShapeDtypeStruct((Z, rows, depth), left.dtype),
        in_specs=[pl.BlockSpec(memory_space=pltpu.SMEM), pl.BlockSpec(memory_space=pltpu.VMEM)],
        out_specs=pl.BlockSpec(memory_space=pltpu.VMEM),
        name="arrange_left",
    )(place, left)


def mul_kernel(groups, width, core_ref, left_ref, *refs):
    pieces, (keep_ref, send_ref) = refs[:-2], refs[-2:]
    rows = keep_ref.shape[0]
    mine = pl.multiple_of(core_ref[0] * rows, rows)
    other = pl.multiple_of((1 - core_ref[0]) * rows, rows)

    def step(i, _):
        at = pl.multiple_of(i * width, width)
        keep = jnp.zeros((rows, width), jnp.float32)
        send = jnp.zeros((rows, width), jnp.float32)
        for d, group in enumerate(groups):
            part = []
            for piece, row, count, offset in group:
                part.append(pieces[piece][pl.ds(row, count), pl.ds(pl.multiple_of(at + offset, 128), width)])
            right = jnp.concatenate(part, axis=0)
            keep += jnp.dot(left_ref[d, pl.ds(mine, rows)], right, preferred_element_type=jnp.float32)
            send += jnp.dot(left_ref[d, pl.ds(other, rows)], right, preferred_element_type=jnp.float32)
        keep_ref[:, pl.ds(at, width)] = keep.astype(keep_ref.dtype)
        send_ref[:, pl.ds(at, width)] = send.astype(send_ref.dtype)
        return _

    lax.fori_loop(0, keep_ref.shape[1] // width, step, None)


def multiply(core, left, pieces, groups, columns, name):
    rows = left.shape[1] // 2
    shape = jax.ShapeDtypeStruct((rows, columns), left.dtype)
    vmem = pl.BlockSpec(memory_space=pltpu.VMEM)
    return pl.pallas_call(
        functools.partial(mul_kernel, groups, 256),
        out_shape=(shape, shape),
        in_specs=[pl.BlockSpec(memory_space=pltpu.SMEM)] + [vmem] * (1 + len(pieces)),
        out_specs=(vmem, vmem),
        compiler_params=pltpu.CompilerParams(vmem_limit_bytes=24 << 20),
        name=name,
    )(core, left, *pieces)


def join_kernel(core_ref, keep_a, keep_b, got_a, got_b, gate_ref, up_ref, sems):
    cut = keep_a.shape[1]

    def put(gate, up):
        copies = []
        for out, (a, b) in ((gate_ref, gate), (up_ref, up)):
            copies.append(pltpu.make_async_copy(a, out.at[:, pl.ds(0, cut)], sems.at[len(copies)]))
            copies.append(pltpu.make_async_copy(b, out.at[:, pl.ds(cut, b.shape[1])], sems.at[len(copies)]))
        for copy in copies:
            copy.start()
        for copy in copies:
            copy.wait()

    @pl.when(core_ref[0] == 0)
    def _():
        put((keep_a, keep_b), (got_a, got_b))

    @pl.when(core_ref[0] == 1)
    def _():
        put((got_a, got_b), (keep_a, keep_b))


def join(core, keep_a, keep_b, got_a, got_b):
    rows, columns = keep_a.shape[0], keep_a.shape[1] + keep_b.shape[1]
    shape = jax.ShapeDtypeStruct((rows, columns), keep_a.dtype)
    anywhere = pl.BlockSpec(memory_space=pl.ANY)
    return pl.pallas_call(
        join_kernel,
        out_shape=(shape, shape),
        in_specs=[pl.BlockSpec(memory_space=pltpu.SMEM)] + [anywhere] * 4,
        out_specs=(anywhere, anywhere),
        scratch_shapes=[pltpu.SemaphoreType.DMA((4,))],
        compiler_params=pltpu.CompilerParams(vmem_limit_bytes=16 << 20),
        name="join",
    )(core, keep_a, keep_b, got_a, got_b)


def weigh(left, coef):
    return (coef[:, None, None] * left.astype(jnp.float32)).astype(jnp.bfloat16)


def shards(gate_left, up_left, gate_right, up_right, fitness_order, member_scale):
    core = lax.axis_index("c")
    first = core == 0
    place = jnp.stack([lax.axis_index("y"), lax.axis_index("z")]).astype(jnp.int32)
    core_at = core.reshape(1).astype(jnp.int32)
    total = Y * Z * C * H * X
    rank, columns = gate_right.shape[1:]

    mine = jnp.where(first, gate_right, up_right)
    got = shift(jnp.where(first, up_right, gate_right), "c", 1)
    own = jnp.concatenate([jnp.where(first, mine, got), jnp.where(first, got, mine)], axis=1)
    own = own.reshape(-1, columns)

    centered = (2 * fitness_order - (total - 1)).astype(jnp.float32)
    coef = centered * member_scale / ((total - 1) * math.sqrt(total * rank))
    gate_w, up_w = weigh(gate_left, coef)[0], weigh(up_left, coef)[0]
    left_mine = jnp.where(first, gate_w, up_w)
    left_got = shift(jnp.where(first, up_w, gate_w), "c", 1)
    left = jnp.concatenate([jnp.where(first, left_mine, left_got), jnp.where(first, left_got, left_mine)], axis=0)
    left = left.reshape(C * rank, Y * Z, -1).transpose(1, 0, 2)
    left = jnp.concatenate([left, left], axis=0)
    left = lax.all_to_all(left, ("h", "y", "z"), split_axis=0, concat_axis=0, tiled=True)
    left = lax.all_gather(left, "x", axis=0, tiled=False)
    left = left.reshape(X, H, Y * Z, C * rank, -1)
    left = arrange_left(place, left)

    n = own.shape[0]
    half = n // 2
    y0 = spread(own)
    z1 = shift(own[:, FIRST:], "z", 1)
    z2 = shift(z1, "z", 1)
    z3 = shift(z2, "z", 1)
    y1 = spread(z1)
    z23 = jnp.concatenate([z2[:half], z3[:half], z2[half:], z3[half:]], axis=0)
    y23 = spread(z23)
    a0 = jnp.concatenate([own[:, :FIRST]] + [part[:, :FIRST] for part in y0], axis=0)
    a1 = shift(a0, "z", 1)
    a2 = shift(a1, "z", 1)
    a3 = shift(a2, "z", 1)

    a_groups = [[(d, 0, Y * n, 0)] for d in range(Z)]
    keep_a, send_a = multiply(core_at, left, [a0, a1, a2, a3], a_groups, FIRST, "multiply_a")
    got_a = shift(send_a, "c", 1)
    pieces = [own, *y0, z1, *y1, z23, *y23]
    b_groups = [
        [(0, 0, n, FIRST), (1, 0, n, FIRST), (2, 0, n, FIRST), (3, 0, half, FIRST), (4, 0, half, FIRST)],
        [(5, 0, n, 0), (6, 0, n, 0), (7, 0, n, 0), (8, 0, half, 0), (9, 0, half, 0)],
    ]
    for k in (0, 1):
        low, high = k * half, (k + 2) * half
        group = []
        for piece in (10, 11, 12):
            group += [(piece, low, half, 0), (piece, high, half, 0)]
        group += [(13, low, half, 0), (14, low, half, 0)]
        b_groups.append(group)
    keep_b, send_b = multiply(core_at, left, pieces, b_groups, columns - FIRST, "multiply_b")
    got_b = shift(send_b, "c", 1)
    return tuple(join(core_at, keep_a, keep_b, got_a, got_b))


def solution(mesh):
    fine = Mesh(mesh.devices.reshape(Y, Z, C, H, X), ("y", "z", "c", "h", "x"))
    pop, tp = ("y", "z", "c"), ("h", "x")
    in_specs = (
        P(pop + tp, None, None),
        P(pop + tp, None, None),
        P(pop, None, tp),
        P(pop, None, tp),
        P(pop + tp),
        P(pop + tp),
    )
    out_specs = (P(pop, tp), P(pop, tp))
    return jax.shard_map(shards, mesh=fine, in_specs=in_specs, out_specs=out_specs, check_vma=False)
```

time: 311 us -> 166 us (0.53)
  blocking collectives: 165 us -> 0 us
  waiting for transfers between devices: 0.06 us -> 81.6 us
  local copies, waits for them, and re-layouts: 84.4 us -> 14.5 us
  matrix products: 13.8 us -> 0 us
  Pallas kernels: 0 us -> 12.2 us
  starting transfers between devices: 29.9 us -> 36.2 us
  other arithmetic: 0.24 us -> 5.58 us
    all_gather x2 -> x0, blocking collectives: 90 us -> none  [the longest x1 47.2 us: shards(): lax.all_gather(up_left, 'tp', axis=0, tiled=True)]
    unnamed x1 -> x0, blocking collectives: 75.5 us -> none
    ppermute x0 -> x22, waiting for transfers between devices: none -> 70.9 us  [shift(): return lax.ppermute(x, axis, [(i, (i + by) % n) for i in range(n)])]
    unnamed x11 -> x20, local copies, waits for them, and re-layouts: 48.4 us -> 7.21 us
    ppermute x0 -> x22, starting transfers between devices: none -> 25.9 us  [shift(): return lax.ppermute(x, axis, [(i, (i + by) % n) for i in range(n)])]
    all_to_all x2 -> x1, starting transfers between devices: 29.8 us -> 10.2 us  [shards(): lax.all_to_all(left, ('h', 'y', 'z'), split_axis=0, concat_axis=0, tiled=...]
    all_to_all x2 -> x0, local copies, waits for them, and re-layouts: 19.5 us -> none  [the longest x1 9.73 us: shards(): lax.all_to_all(grouped[0], 'pop', split_axis=2, concat_axis=0, tiled=True)]
    all_gather x2 -> x0, local copies, waits for them, and re-layouts: 16.6 us -> none  [the longest x1 8.29 us: shards(): lax.all_gather(gate_left, 'tp', axis=0, tiled=True)]
  transfers between devices with their start and end apart: 4 -> 24, of which waited for: 0 -> 11; matrix products, arithmetic and copies ran while one was open for 29% -> 7% of each run, Pallas kernels for 0% -> 2%
where the time goes in v1:
time: 166 us
  waiting for transfers between devices  81.6 us (49%)
  starting transfers between devices  36.2 us (22%)
  between operations  15.5 us (9%)
  local copies, waits for them, and re-layouts  14.5 us (9%)
  Pallas kernels  12.2 us (7%)
  other arithmetic  5.58 us (3%)
    ppermute x22, waiting for transfers between devices, shift(): return lax.ppermute(x, axis, [(i, (i + by) % n) for i in range(n)])  70.9 us
    ppermute x22, starting transfers between devices, shift(): return lax.ppermute(x, axis, [(i, (i + by) % n) for i in range(n)])  25.9 us
    all_to_all x1, waiting for transfers between devices, shards(): lax.all_to_all(left, ('h', 'y', 'z'), split_axis=0, concat_axis=0, tiled=...  10.7 us
    all_to_all x1, starting transfers between devices, shards(): lax.all_to_all(left, ('h', 'y', 'z'), split_axis=0, concat_axis=0, tiled=...  10.2 us
    pallas_call x2, Pallas kernels, multiply(): pl.pallas_call(functools.partial(mul_kernel, groups, 256), out_shape=(sha...  7.77 us
    unnamed x20, local copies, waits for them, and re-layouts  7.21 us
    slice x6, local copies, waits for them, and re-layouts, spread(): return (up, down, shift(up[:half], 'y', 1), shift(down[half:], 'y', -1))  6.47 us
  transfers between devices with their start and end apart: 24, of which 11 were waited for; matrix products, arithmetic and copies ran while one was open for 7% of the time, Pallas kernels for 2%

profile of v1, /device:TPU:1, one launch (start us, length us, event | category | flops | bytes accessed | tf_op | source)
XLA Modules:
  0.0 165.6 jit_solution(10073122325339062094)
XLA Ops:
  9.4 3.3 %collective-permute-start = (bf16[4,8192]{1,0:T(4,128)(2,1)S(1)}, bf16[4,8192]{1,0:T(4,128)(2,1)S(1)}, u32[]{:S(2)}, u32[]{:S(2)}) collective-permute-start(bf16[4,8192]{1,0:T(4,128)(2,1)S(1)} %select_bitcast_fusion), channel_id=1, source_target_pairs={{0,8},{8,0},{1,9},{9,1},{2,10},{10,2},{3,11},{11,3},{4,12},{12,4},... | collective-permute-start | bytes 196616 | tf_op jit(solution)/shard_map/ppermute | solution.py:17
  17.4 10.2 %all-to-all-start = ((bf16[32,8,512]{2,1,0:T(8,128)(2,1)}), bf16[32,8,512]{2,1,0:T(8,128)(2,1)S(1)}, u32[]{:S(2)}, u32[]{:S(2)}) async-start(bf16[32,8,512]{2,1,0:T(8,128)(2,1)} %pad_maximum_fusion.1), calls=%async_computation | async-start | bytes 524288 | tf_op jit(solution)/shard_map/all_to_all | solution.py:148
  27.7 1.3 collective-permute-done.9.refs_5_
  29.0 10.7 %all-to-all-done = bf16[32,8,512]{2,1,0:T(8,128)(2,1)S(1)} async-done(((bf16[32,8,512]{2,1,0:T(8,128)(2,1)}), bf16[32,8,512]{2,1,0:T(8,128)(2,1)S(1)}, u32[]{:S(2)}, u32[]{:S(2)}) %all-to-all-start) | async-done | bytes 262176 | tf_op jit(solution)/shard_map/all_to_all | solution.py:148
  40.4 4.3 %collective-permute-done.14 = bf16[64,3072]{1,0:T(8,128)(2,1)S(1)} collective-permute-done((bf16[64,3072]{1,0:T(8,128)(2,1)S(1)}, bf16[64,3072]{1,0:T(8,128)(2,1)S(1)}, u32[]{:S(2)}, u32[]{:S(2)}) %collective-permute-start.14) | collective-permute-done | bytes 393248 | tf_op jit(solution)/shard_map/ppermute | solution.py:17
  44.8 10.8 %collective-permute-done.15 = bf16[64,3072]{1,0:T(8,128)(2,1)S(1)} collective-permute-done((bf16[64,3072]{1,0:T(8,128)(2,1)S(1)}, bf16[64,3072]{1,0:T(8,128)(2,1)S(1)}, u32[]{:S(2)}, u32[]{:S(2)}) %collective-permute-start.15) | collective-permute-done | bytes 393248 | tf_op jit(solution)/shard_map/ppermute | solution.py:17
  55.7 1.3 collective-permute-start.16
  57.0 1.4 collective-permute-start.17
  58.5 2.6 %collective-permute-start.3 = (bf16[64,3584]{1,0:T(8,128)(2,1)S(1)}, bf16[64,3584]{1,0:T(8,128)(2,1)S(1)}, u32[]{:S(2)}, u32[]{:S(2)}) collective-permute-start(bf16[64,3584]{1,0:T(8,128)(2,1)S(1)} %maximum_bitcast_fusion.refs_0_), channel_id=1, source_target_pairs={{0,192},{64,0},{128,64},{192,128},{1,193},{65,1},{129,65},{193,129... | collective-permute-start | bytes 1376264 | tf_op jit(solution)/shard_map/ppermute | solution.py:17
  61.1 22.2 %collective-permute-done.2.refs_1_ = bf16[64,3584]{1,0:T(8,128)(2,1)S(1)} collective-permute-done((bf16[64,3584]{1,0:T(8,128)(2,1)S(1)}, bf16[64,3584]{1,0:T(8,128)(2,1)S(1)}, u32[]{:S(2)}, u32[]{:S(2)}) %collective-permute-start.2) | collective-permute-done | bytes 458784 | tf_op jit(solution)/shard_map/ppermute | solution.py:17
  88.0 2.5 %collective-permute-start.5 = (bf16[32,3584]{1,0:T(8,128)(2,1)}, bf16[32,3584]{1,0:T(8,128)(2,1)}, u32[]{:S(2)}, u32[]{:S(2)}) collective-permute-start(bf16[32,3584]{1,0:T(8,128)(2,1)} %slice.69), channel_id=1, source_target_pairs={{0,192},{64,0},{128,64},{192,128},{1,193},{65,1},{129,65},{193,129... | collective-permute-start | bytes 688136 | tf_op jit(solution)/shard_map/ppermute | solution.py:17
  92.0 2.7 %collective-permute-start.19 = (bf16[64,3072]{1,0:T(8,128)(2,1)}, bf16[64,3072]{1,0:T(8,128)(2,1)}, u32[]{:S(2)}, u32[]{:S(2)}) collective-permute-start(bf16[64,3072]{1,0:T(8,128)(2,1)} %slice.79), channel_id=1, source_target_pairs={{0,192},{64,0},{128,64},{192,128},{1,193},{65,1},{129,65},{193,129... | collective-permute-start | bytes 1179656 | tf_op jit(solution)/shard_map/ppermute | solution.py:17
  94.7 1.6 slice.72
  96.3 1.6 slice.73
  98.7 2.7 %collective-permute-start.13 = (bf16[32,3072]{1,0:T(8,128)(2,1)}, bf16[32,3072]{1,0:T(8,128)(2,1)}, u32[]{:S(2)}, u32[]{:S(2)}) collective-permute-start(bf16[32,3072]{1,0:T(8,128)(2,1)} %slice.73), channel_id=1, source_target_pairs={{0,192},{64,0},{128,64},{192,128},{1,193},{65,1},{129,65},{193,129... | collective-permute-start | bytes 589832 | tf_op jit(solution)/shard_map/ppermute | solution.py:17
  102.2 2.6 %arrange_left.1.left_ref = bf16[4,512,256]{2,1,0:T(8,128)(2,1)} custom-call(s32[2]{0:T(128)} %pad_add_fusion.place_ref, bf16[4,2,16,8,512]{4,3,2,1,0:T(8,128)(2,1)} %bitcast.23), custom_call_target="tpu_custom_call" | custom-call | tf_op jit(solution)/shard_map/arrange_left/pallas_call | solution.py:39
  104.7 4.2 %collective-permute-done.12.refs_8_ = bf16[32,3072]{1,0:T(8,128)(2,1)} collective-permute-done((bf16[32,3072]{1,0:T(8,128)(2,1)}, bf16[32,3072]{1,0:T(8,128)(2,1)}, u32[]{:S(2)}, u32[]{:S(2)}) %collective-permute-start.12) | collective-permute-done | bytes 196640 | tf_op jit(solution)/shard_map/ppermute | solution.py:17
  113.1 6.9 %multiply_b.1 = (bf16[256,3072]{1,0:T(8,128)(2,1)S(1)}, bf16[256,3072]{1,0:T(8,128)(2,1)S(1)}) custom-call(s32[1]{0:T(128)} %bitcast.core_ref, bf16[4,512,256]{2,1,0:T(8,128)(2,1)S(1)} %copy-done, bf16[64,3584]{1,0:T(8,128)(2,1)S(1)} %maximum_bitcast_fusion.refs_0_, bf16[64,3584]{1,0:T(8,128)(2,1)S(1)} %copy-done.2, ...), custom_call_target="tpu_custom_call" | custom-call | tf_op jit(solution)/shard_map/multiply_b/pallas_call | solution.py:76
  120.0 4.9 %collective-permute-start.21 = (bf16[256,3072]{1,0:T(8,128)(2,1)S(1)}, bf16[256,3072]{1,0:T(8,128)(2,1)S(1)}, u32[]{:S(2)}, u32[]{:S(2)}) collective-permute-start(bf16[256,3072]{1,0:T(8,128)(2,1)S(1)} %get-tuple-element.9), channel_id=1, source_target_pairs={{0,8},{8,0},{1,9},{9,1},{2,10},{10,2},{3,11},{11,3},{4,12},{12,4},... | collective-permute-start | bytes 4718600 | tf_op jit(solution)/shard_map/ppermute | solution.py:17
  125.7 9.7 %collective-permute-done.6.refs_1_ = bf16[256,512]{1,0:T(8,128)(2,1)S(1)} collective-permute-done((bf16[256,512]{1,0:T(8,128)(2,1)S(1)}, bf16[256,512]{1,0:T(8,128)(2,1)S(1)}, u32[]{:S(2)}, u32[]{:S(2)}) %collective-permute-start.6) | collective-permute-done | bytes 262176 | tf_op jit(solution)/shard_map/ppermute | solution.py:17
  135.4 8.8 %collective-permute-done.7.refs_2_ = bf16[256,512]{1,0:T(8,128)(2,1)S(1)} collective-permute-done((bf16[256,512]{1,0:T(8,128)(2,1)S(1)}, bf16[256,512]{1,0:T(8,128)(2,1)S(1)}, u32[]{:S(2)}, u32[]{:S(2)}) %collective-permute-start.7) | collective-permute-done | bytes 262176 | tf_op jit(solution)/shard_map/ppermute | solution.py:17
  144.2 7.9 %collective-permute-done.8.refs_3_ = bf16[256,512]{1,0:T(8,128)(2,1)S(1)} collective-permute-done((bf16[256,512]{1,0:T(8,128)(2,1)S(1)}, bf16[256,512]{1,0:T(8,128)(2,1)S(1)}, u32[]{:S(2)}, u32[]{:S(2)}) %collective-permute-start.8) | collective-permute-done | bytes 262176 | tf_op jit(solution)/shard_map/ppermute | solution.py:17
  153.0 2.7 %collective-permute-start.20 = (bf16[256,512]{1,0:T(8,128)(2,1)S(1)}, bf16[256,512]{1,0:T(8,128)(2,1)S(1)}, u32[]{:S(2)}, u32[]{:S(2)}) collective-permute-start(bf16[256,512]{1,0:T(8,128)(2,1)S(1)} %get-tuple-element.8), channel_id=1, source_target_pairs={{0,8},{8,0},{1,9},{9,1},{2,10},{10,2},{3,11},{11,3},{4,12},{12,4},... | collective-permute-start | bytes 786440 | tf_op jit(solution)/shard_map/ppermute | solution.py:17
  156.8 1.9 %join.1 = (bf16[256,3584]{1,0:T(8,128)(2,1)}, bf16[256,3584]{1,0:T(8,128)(2,1)}) custom-call(s32[1]{0:T(128)} %bitcast.core_ref, bf16[256,512]{1,0:T(8,128)(2,1)S(1)} %get-tuple-element.6.keep_a, bf16[256,3072]{1,0:T(8,128)(2,1)S(1)} %get-tuple-element.7.keep_b, bf16[256,512]{1,0:T(8,128)(2,1)S(1)} %collective-permute-done.20.got_a, ...), custom_call_target="tpu_custom_call" | custom-call | tf_op jit(solution)/shard_map/join/pallas_call | solution.py:112
  (68 shorter events, 21.3 us)
Async XLA Ops:
  9.4 4.4 %collective-permute-start = (bf16[4,8192]{1,0:T(4,128)(2,1)S(1)}, bf16[4,8192]{1,0:T(4,128)(2,1)S(1)}, u32[]{:S(2)}, u32[]{:S(2)}) collective-permute-start(bf16[4,8192]{1,0:T(4,128)(2,1)S(1)} %select_bitcast_fusion), channel_id=1, source_target_pairs={{0,8},{8,0},{1,9},{9,1},{2,10},{10,2},{3,11},{11,3},{4,12},{12,4},... | collective-permute-start | bytes 196616 | tf_op jit(solution)/shard_map/ppermute | solution.py:17
  13.7 1.6 collective-permute-start.1
  16.5 12.5 %collective-permute-start.9 = (bf16[64,3072]{1,0:T(8,128)(2,1)S(1)}, bf16[64,3072]{1,0:T(8,128)(2,1)S(1)}, u32[]{:S(2)}, u32[]{:S(2)}) collective-permute-start(bf16[64,3072]{1,0:T(8,128)(2,1)S(1)} %slice.71), channel_id=1, source_target_pairs={{0,16},{16,32},{32,48},{48,0},{1,17},{17,33},{33,49},{49,1},{2,18}... | collective-permute-start | bytes 1179656 | tf_op jit(solution)/shard_map/ppermute | solution.py:17
  17.4 22.3 %all-to-all-start = ((bf16[32,8,512]{2,1,0:T(8,128)(2,1)}), bf16[32,8,512]{2,1,0:T(8,128)(2,1)S(1)}, u32[]{:S(2)}, u32[]{:S(2)}) async-start(bf16[32,8,512]{2,1,0:T(8,128)(2,1)} %pad_maximum_fusion.1), calls=%async_computation | async-start | bytes 524288 | tf_op jit(solution)/shard_map/all_to_all | solution.py:148
  27.6 74.6 %all-gather.3.cloned.1.call-start = ((), (), s32[]{:S(2)}) async-start(), calls=%async_computation.1 | async-start | bytes 1310720 | tf_op jit(solution)/shard_map/all_gather | solution.py:149
  29.0 15.8 %collective-permute-start.14 = (bf16[64,3072]{1,0:T(8,128)(2,1)S(1)}, bf16[64,3072]{1,0:T(8,128)(2,1)S(1)}, u32[]{:S(2)}, u32[]{:S(2)}) collective-permute-start(bf16[64,3072]{1,0:T(8,128)(2,1)S(1)} %collective-permute-done.9.refs_5_), channel_id=1, source_target_pairs={{0,16},{16,32},{32,48},{48,0},{1,17},{17,33},{33,49},{49,1},{2,18}... | collective-permute-start | bytes 1179656 | tf_op jit(solution)/shard_map/ppermute | solution.py:17
  44.7 10.8 %collective-permute-start.15 = (bf16[64,3072]{1,0:T(8,128)(2,1)S(1)}, bf16[64,3072]{1,0:T(8,128)(2,1)S(1)}, u32[]{:S(2)}, u32[]{:S(2)}) collective-permute-start(bf16[64,3072]{1,0:T(8,128)(2,1)S(1)} %collective-permute-done.14), channel_id=1, source_target_pairs={{0,16},{16,32},{32,48},{48,0},{1,17},{17,33},{33,49},{49,1},{2,18}... | collective-permute-start | bytes 1179656 | tf_op jit(solution)/shard_map/ppermute | solution.py:17
  55.7 32.3 %collective-permute-start.16 = (bf16[128,3072]{1,0:T(8,128)(2,1)S(1)}, bf16[128,3072]{1,0:T(8,128)(2,1)S(1)}, u32[]{:S(2)}, u32[]{:S(2)}) collective-permute-start(bf16[128,3072]{1,0:T(8,128)(2,1)S(1)} %pad_maximum_fusion.refs_10_), channel_id=1, source_target_pairs={{0,64},{64,128},{128,192},{192,0},{1,65},{65,129},{129,193},{193,1... | collective-permute-start | bytes 2359304 | tf_op jit(solution)/shard_map/ppermute | solution.py:17
  57.0 34.2 %collective-permute-start.17 = (bf16[128,3072]{1,0:T(8,128)(2,1)S(1)}, bf16[128,3072]{1,0:T(8,128)(2,1)S(1)}, u32[]{:S(2)}, u32[]{:S(2)}) collective-permute-start(bf16[128,3072]{1,0:T(8,128)(2,1)S(1)} %pad_maximum_fusion.refs_10_), channel_id=1, source_target_pairs={{0,192},{64,0},{128,64},{192,128},{1,193},{65,1},{129,65},{193,129... | collective-permute-start | bytes 2359304 | tf_op jit(solution)/shard_map/ppermute | solution.py:17
  58.4 24.9 %collective-permute-start.2 = (bf16[64,3584]{1,0:T(8,128)(2,1)S(1)}, bf16[64,3584]{1,0:T(8,128)(2,1)S(1)}, u32[]{:S(2)}, u32[]{:S(2)}) collective-permute-start(bf16[64,3584]{1,0:T(8,128)(2,1)S(1)} %maximum_bitcast_fusion.refs_0_), channel_id=1, source_target_pairs={{0,64},{64,128},{128,192},{192,0},{1,65},{65,129},{129,193},{193,1... | collective-permute-start | bytes 1376264 | tf_op jit(solution)/shard_map/ppermute | solution.py:17
  58.5 27.8 %collective-permute-start.3 = (bf16[64,3584]{1,0:T(8,128)(2,1)S(1)}, bf16[64,3584]{1,0:T(8,128)(2,1)S(1)}, u32[]{:S(2)}, u32[]{:S(2)}) collective-permute-start(bf16[64,3584]{1,0:T(8,128)(2,1)S(1)} %maximum_bitcast_fusion.refs_0_), channel_id=1, source_target_pairs={{0,192},{64,0},{128,64},{192,128},{1,193},{65,1},{129,65},{193,129... | collective-permute-start | bytes 1376264 | tf_op jit(solution)/shard_map/ppermute | solution.py:17
  61.1 30.9 %collective-permute-start.10 = (bf16[64,3072]{1,0:T(8,128)(2,1)}, bf16[64,3072]{1,0:T(8,128)(2,1)}, u32[]{:S(2)}, u32[]{:S(2)}) collective-permute-start(bf16[64,3072]{1,0:T(8,128)(2,1)} %copy-done.3), channel_id=1, source_target_pairs={{0,64},{64,128},{128,192},{192,0},{1,65},{65,129},{129,193},{193,1... | collective-permute-start | bytes 1179656 | tf_op jit(solution)/shard_map/ppermute | solution.py:17
  84.1 12.2 %collective-permute-start.11 = (bf16[64,3072]{1,0:T(8,128)(2,1)}, bf16[64,3072]{1,0:T(8,128)(2,1)}, u32[]{:S(2)}, u32[]{:S(2)}) collective-permute-start(bf16[64,3072]{1,0:T(8,128)(2,1)} %copy-done.3), channel_id=1, source_target_pairs={{0,192},{64,0},{128,64},{192,128},{1,193},{65,1},{129,65},{193,129... | collective-permute-start | bytes 1179656 | tf_op jit(solution)/shard_map/ppermute | solution.py:17
  86.3 11.6 %collective-permute-start.4 = (bf16[32,3584]{1,0:T(8,128)(2,1)S(1)}, bf16[32,3584]{1,0:T(8,128)(2,1)S(1)}, u32[]{:S(2)}, u32[]{:S(2)}) collective-permute-start(bf16[32,3584]{1,0:T(8,128)(2,1)S(1)} %slice.67), channel_id=1, source_target_pairs={{0,64},{64,128},{128,192},{192,0},{1,65},{65,129},{129,193},{193,1... | collective-permute-start | bytes 688136 | tf_op jit(solution)/shard_map/ppermute | solution.py:17
  88.0 16.8 %collective-permute-start.5 = (bf16[32,3584]{1,0:T(8,128)(2,1)}, bf16[32,3584]{1,0:T(8,128)(2,1)}, u32[]{:S(2)}, u32[]{:S(2)}) collective-permute-start(bf16[32,3584]{1,0:T(8,128)(2,1)} %slice.69), channel_id=1, source_target_pairs={{0,192},{64,0},{128,64},{192,128},{1,193},{65,1},{129,65},{193,129... | collective-permute-start | bytes 688136 | tf_op jit(solution)/shard_map/ppermute | solution.py:17
  91.2 17.7 %collective-permute-start.18 = (bf16[64,3072]{1,0:T(8,128)(2,1)}, bf16[64,3072]{1,0:T(8,128)(2,1)}, u32[]{:S(2)}, u32[]{:S(2)}) collective-permute-start(bf16[64,3072]{1,0:T(8,128)(2,1)} %slice.78), channel_id=1, source_target_pairs={{0,64},{64,128},{128,192},{192,0},{1,65},{65,129},{129,193},{193,1... | collective-permute-start | bytes 1179656 | tf_op jit(solution)/shard_map/ppermute | solution.py:17
  92.0 17.0 %collective-permute-start.19 = (bf16[64,3072]{1,0:T(8,128)(2,1)}, bf16[64,3072]{1,0:T(8,128)(2,1)}, u32[]{:S(2)}, u32[]{:S(2)}) collective-permute-start(bf16[64,3072]{1,0:T(8,128)(2,1)} %slice.79), channel_id=1, source_target_pairs={{0,192},{64,0},{128,64},{192,128},{1,193},{65,1},{129,65},{193,129... | collective-permute-start | bytes 1179656 | tf_op jit(solution)/shard_map/ppermute | solution.py:17
  96.3 12.6 %collective-permute-start.12 = (bf16[32,3072]{1,0:T(8,128)(2,1)}, bf16[32,3072]{1,0:T(8,128)(2,1)}, u32[]{:S(2)}, u32[]{:S(2)}) collective-permute-start(bf16[32,3072]{1,0:T(8,128)(2,1)} %slice.72), channel_id=1, source_target_pairs={{0,64},{64,128},{128,192},{192,0},{1,65},{65,129},{129,193},{193,1... | collective-permute-start | bytes 589832 | tf_op jit(solution)/shard_map/ppermute | solution.py:17
  98.7 10.3 %collective-permute-start.13 = (bf16[32,3072]{1,0:T(8,128)(2,1)}, bf16[32,3072]{1,0:T(8,128)(2,1)}, u32[]{:S(2)}, u32[]{:S(2)}) collective-permute-start(bf16[32,3072]{1,0:T(8,128)(2,1)} %slice.73), channel_id=1, source_target_pairs={{0,192},{64,0},{128,64},{192,128},{1,193},{65,1},{129,65},{193,129... | collective-permute-start | bytes 589832 | tf_op jit(solution)/shard_map/ppermute | solution.py:17
  120.0 36.8 %collective-permute-start.21 = (bf16[256,3072]{1,0:T(8,128)(2,1)S(1)}, bf16[256,3072]{1,0:T(8,128)(2,1)S(1)}, u32[]{:S(2)}, u32[]{:S(2)}) collective-permute-start(bf16[256,3072]{1,0:T(8,128)(2,1)S(1)} %get-tuple-element.9), channel_id=1, source_target_pairs={{0,8},{8,0},{1,9},{9,1},{2,10},{10,2},{3,11},{11,3},{4,12},{12,4},... | collective-permute-start | bytes 4718600 | tf_op jit(solution)/shard_map/ppermute | solution.py:17
  125.7 9.7 %collective-permute-start.6 = (bf16[256,512]{1,0:T(8,128)(2,1)S(1)}, bf16[256,512]{1,0:T(8,128)(2,1)S(1)}, u32[]{:S(2)}, u32[]{:S(2)}) collective-permute-start(bf16[256,512]{1,0:T(8,128)(2,1)S(1)} %slice_dynamic-update-slice_fusion.3.refs_0_), channel_id=1, source_target_pairs={{0,16},{16,32},{32,48},{48,0},{1,17},{17,33},{33,49},{49,1},{2,18}... | collective-permute-start | bytes 786440 | tf_op jit(solution)/shard_map/ppermute | solution.py:17
  135.4 8.8 %collective-permute-start.7 = (bf16[256,512]{1,0:T(8,128)(2,1)S(1)}, bf16[256,512]{1,0:T(8,128)(2,1)S(1)}, u32[]{:S(2)}, u32[]{:S(2)}) collective-permute-start(bf16[256,512]{1,0:T(8,128)(2,1)S(1)} %collective-permute-done.6.refs_1_), channel_id=1, source_target_pairs={{0,16},{16,32},{32,48},{48,0},{1,17},{17,33},{33,49},{49,1},{2,18}... | collective-permute-start | bytes 786440 | tf_op jit(solution)/shard_map/ppermute | solution.py:17
  144.2 7.9 %collective-permute-start.8 = (bf16[256,512]{1,0:T(8,128)(2,1)S(1)}, bf16[256,512]{1,0:T(8,128)(2,1)S(1)}, u32[]{:S(2)}, u32[]{:S(2)}) collective-permute-start(bf16[256,512]{1,0:T(8,128)(2,1)S(1)} %collective-permute-done.7.refs_2_), channel_id=1, source_target_pairs={{0,16},{16,32},{32,48},{48,0},{1,17},{17,33},{33,49},{49,1},{2,18}... | collective-permute-start | bytes 786440 | tf_op jit(solution)/shard_map/ppermute | solution.py:17
  153.0 3.9 %collective-permute-start.20 = (bf16[256,512]{1,0:T(8,128)(2,1)S(1)}, bf16[256,512]{1,0:T(8,128)(2,1)S(1)}, u32[]{:S(2)}, u32[]{:S(2)}) collective-permute-start(bf16[256,512]{1,0:T(8,128)(2,1)S(1)} %get-tuple-element.8), channel_id=1, source_target_pairs={{0,8},{8,0},{1,9},{9,1},{2,10},{10,2},{3,11},{11,3},{4,12},{12,4},... | collective-permute-start | bytes 786440 | tf_op jit(solution)/shard_map/ppermute | solution.py:17
  (8 other events, 33.0 us)
Sparse Core Ops, SparseCore 0:
  40.6 27.8 all-gather.2

commit v2 on v0

v2 whole, which is shorter than its diff:
```python
import functools
import math

import jax
import jax.numpy as jnp
from jax import lax
from jax.experimental import pallas as pl
from jax.experimental.pallas import tpu as pltpu
from jax.sharding import Mesh, PartitionSpec as P

Y, Z, C, H, X = 4, 4, 2, 2, 4
FIRST = 0


def shift(x, axis, by):
    n = lax.axis_size(axis)
    return lax.ppermute(x, axis, [(i, (i + by) % n) for i in range(n)])


def left_kernel(place_ref, *refs):
    *left_refs, first_ref, second_ref, last_ref, held = refs
    x, y, z, h = place_ref[0], place_ref[1], place_ref[2], place_ref[3]
    for r, left_ref in enumerate(left_refs):
        held[r] = left_ref[...].astype(held.dtype)
    size = H * X * held.shape[3]
    for d in range(Z):
        parts = []
        for from_y in (0, 1, Y - 1, 2):
            chip = lax.rem(y + Y - from_y, Y) * Z + lax.rem(z + Z - d, Z)
            for at_h in range(H):
                for at_x in range(X):
                    parts.append(held[lax.rem(x + X - at_x, X), lax.rem(h + at_h, H), chip])
        block = jnp.concatenate(parts, axis=0).T.astype(first_ref.dtype)
        if d < Z // 2:
            first_ref[:, d * Y * size : (d + 1) * Y * size] = block
        elif d < Z - 1:
            second_ref[:, (d - Z // 2) * Y * size : (d - Z // 2 + 1) * Y * size] = block
        else:
            second_ref[:, (d - Z // 2) * Y * size :] = block[:, : (Y - 1) * size]
            last_ref[...] = block[:, (Y - 1) * size :]


def arrange_left(place, lefts):
    rows = lefts[0].shape[-1]
    size = H * X * lefts[0].shape[2]
    vmem = pl.BlockSpec(memory_space=pltpu.VMEM)
    return pl.pallas_call(
        left_kernel,
        out_shape=(
            jax.ShapeDtypeStruct((rows, Y * Z * size // 2), lefts[0].dtype),
            jax.ShapeDtypeStruct((rows, (Y * Z // 2 - 1) * size), lefts[0].dtype),
            jax.ShapeDtypeStruct((rows, size), lefts[0].dtype),
        ),
        in_specs=[pl.BlockSpec(memory_space=pltpu.SMEM)] + [vmem] * X,
        out_specs=(vmem, vmem, vmem),
        scratch_shapes=[pltpu.VMEM((X,) + lefts[0].shape, jnp.float32)],
        compiler_params=pltpu.CompilerParams(vmem_limit_bytes=8 << 20),
        cost_estimate=pl.CostEstimate(flops=0, bytes_accessed=6 << 20, transcendentals=0),
        name="arrange_left",
    )(place, *lefts)


def part_kernel(ranges, width, left_ref, *refs):
    *arrays, out_ref, held, sems = refs
    total_ref = arrays.pop() if len(arrays) > len({which for which, _, _ in ranges}) else None
    columns = out_ref.shape[1]
    cuts = (0, columns // (2 * width) * width, columns)

    def copies(side):
        found, at = [], 0
        part = pl.ds(cuts[side], cuts[side + 1] - cuts[side])
        for which, row, count in ranges:
            source, target = arrays[which].at[pl.ds(row, count), part], held.at[pl.ds(at, count), part]
            found.append(pltpu.make_async_copy(source, target, sems.at[side, len(found)]))
            at += count
        return found

    for side in (0, 1):
        for copy in copies(side):
            copy.start()
    for side in (0, 1):
        for copy in copies(side):
            copy.wait()

        def step(i, _):
            at = pl.ds(pl.multiple_of(i * width, width), width)
            product = jnp.dot(left_ref[...], held[:, at], preferred_element_type=jnp.float32)
            out_ref[:, at] = product if total_ref is None else total_ref[:, at] + product
            return _

        lax.fori_loop(cuts[side] // width, cuts[side + 1] // width, step, None)


def multiply_part(left, pieces, total, name):
    arrays, ranges = [], []
    for array, row, count in pieces:
        known = [k for k, other in enumerate(arrays) if other is array]
        if not known:
            arrays.append(array)
        ranges.append((known[0] if known else len(arrays) - 1, row, count))
    rows, depth = left.shape
    columns = arrays[0].shape[1]
    vmem = pl.BlockSpec(memory_space=pltpu.VMEM)
    totals = [] if total is None else [total]
    return pl.pallas_call(
        functools.partial(part_kernel, ranges, 256),
        out_shape=jax.ShapeDtypeStruct((rows, columns), jnp.float32),
        in_specs=[vmem] + [pl.BlockSpec(memory_space=pl.ANY)] * len(arrays) + [vmem] * len(totals),
        out_specs=vmem,
        scratch_shapes=[
            pltpu.VMEM((depth, columns), left.dtype),
            pltpu.SemaphoreType.DMA((2, len(ranges))),
        ],
        input_output_aliases={1 + len(arrays): 0} if totals else {},
        compiler_params=pltpu.CompilerParams(vmem_limit_bytes=24 << 20),
        cost_estimate=pl.CostEstimate(
            flops=4 * rows * columns * depth, bytes_accessed=12 << 20, transcendentals=0
        ),
        name=name,
    )(left, *arrays, *totals)


def last_kernel(cut, width, core_ref, left_ref, total_ref, *refs):
    *right_refs, keep_ref, send_ref = refs
    rows, columns = keep_ref.shape
    mine = pl.multiple_of(core_ref[0] * rows, rows)
    other = pl.multiple_of((1 - core_ref[0]) * rows, rows)

    def step(i, _):
        at = pl.ds(pl.multiple_of(i * width, width), width)
        from_at = pl.ds(pl.multiple_of(cut + i * width, width), width)
        right = jnp.concatenate([ref[:, from_at] for ref in right_refs], axis=0)
        for out_ref, row in ((send_ref, other), (keep_ref, mine)):
            total = total_ref[pl.ds(row, rows), from_at]
            total += jnp.dot(left_ref[pl.ds(row, rows)], right, preferred_element_type=jnp.float32)
            out_ref[:, at] = total.astype(out_ref.dtype)
        return _

    lax.fori_loop(0, columns // width, step, None)


def multiply_last(core, left, total, last, cut, end, name):
    rows, columns = total.shape[0] // 2, end - cut
    shape = jax.ShapeDtypeStruct((rows, columns), left.dtype)
    vmem = pl.BlockSpec(memory_space=pltpu.VMEM)
    return pl.pallas_call(
        functools.partial(last_kernel, cut, 256),
        out_shape=(shape, shape),
        in_specs=[pl.BlockSpec(memory_space=pltpu.SMEM)] + [vmem] * (2 + len(last)),
        out_specs=(vmem, vmem),
        compiler_params=pltpu.CompilerParams(vmem_limit_bytes=14 << 20),
        cost_estimate=pl.CostEstimate(flops=1024 * rows * columns, bytes_accessed=6 << 20, transcendentals=0),
        name=name,
    )(core, left, total, *last)


def join_kernel(core_ref, keep_0, keep_1, got_0, got_1, gate_ref, up_ref, sems):
    def put(gate, up):
        copies = []
        for out, halves in ((gate_ref, gate), (up_ref, up)):
            for half, at in zip(halves, (0, halves[0].shape[1])):
                to = out.at[:, pl.ds(at, half.shape[1])]
                copies.append(pltpu.make_async_copy(half, to, sems.at[len(copies)]))
        for copy in copies:
            copy.start()
        for copy in copies:
            copy.wait()

    @pl.when(core_ref[0] == 0)
    def _():
        put((keep_0, keep_1), (got_0, got_1))

    @pl.when(core_ref[0] == 1)
    def _():
        put((got_0, got_1), (keep_0, keep_1))


def join(core, *halves):
    rows, columns = halves[0].shape[0], halves[0].shape[1] + halves[1].shape[1]
    shape = jax.ShapeDtypeStruct((rows, columns), halves[0].dtype)
    anywhere = pl.BlockSpec(memory_space=pl.ANY)
    return pl.pallas_call(
        join_kernel,
        out_shape=(shape, shape),
        in_specs=[pl.BlockSpec(memory_space=pltpu.SMEM)] + [anywhere] * 4,
        out_specs=(anywhere, anywhere),
        scratch_shapes=[pltpu.SemaphoreType.DMA((4,))],
        compiler_params=pltpu.CompilerParams(vmem_limit_bytes=4 << 20),
        name="join",
    )(core, *halves)


def weigh(left, coef):
    return (coef[:, None, None] * left.astype(jnp.float32)).astype(jnp.bfloat16)


def shards(gate_left, up_left, gate_right, up_right, fitness_order, member_scale):
    y, z, core = lax.axis_index("y"), lax.axis_index("z"), lax.axis_index("c")
    first = core == 0
    place = jnp.stack([lax.axis_index("x"), y, z, lax.axis_index("h")]).astype(jnp.int32)
    token = core.reshape(1).astype(jnp.int32)
    total = Y * Z * C * H * X
    rank, columns = gate_right.shape[1:]

    def event(*arrived):
        nonlocal token
        *arrived, token = lax.optimization_barrier((*arrived, token))
        return arrived

    gate_got, up_got = shift(gate_right, "c", 1), shift(up_right, "c", 1)
    own = jnp.concatenate([jnp.where(first, gate_right, up_got), jnp.where(first, gate_got, up_right)], axis=1)
    own = own.reshape(-1, columns)

    centered = (2 * fitness_order - (total - 1)).astype(jnp.float32)
    coef = centered * member_scale / ((total - 1) * math.sqrt(total * rank))
    gate_w, up_w = weigh(gate_left, coef)[0], weigh(up_left, coef)[0]
    left_mine = jnp.where(first, gate_w, up_w)
    left_got = shift(jnp.where(first, up_w, gate_w), "c", 1)
    left = jnp.concatenate([jnp.where(first, left_mine, left_got), jnp.where(first, left_got, left_mine)], axis=0)

    def deal(block, axis, at, size):
        width = block.shape[-1] // size
        parts = []
        for by in range(size):
            start = lax.rem(at + by, size) * width
            part = lax.dynamic_slice_in_dim(block, start, width, axis=block.ndim - 1)
            parts.append(shift(part, axis, by) if by else part)
        return parts

    n = own.shape[0]
    half = n // 2

    def both(block, up=None, down=None):
        if up is None:
            return shift(block, "y", 1), shift(block, "y", -1)
        up = jnp.concatenate([block, up[:half]], axis=0)
        down = jnp.concatenate([block, down[half:n]], axis=0)
        return shift(up, "y", 1), shift(down, "y", -1)

    left = left.reshape(C * rank, Y * Z, -1).transpose(1, 0, 2)
    left = lax.all_to_all(left, ("y", "z"), split_axis=0, concat_axis=0, tiled=True)
    own, place = event(own, place)
    up0, down0 = both(own)
    z1 = shift(own, "z", 1)
    up0, down0, z1, left = event(up0, down0, z1, left)

    up1, down1 = both(z1, up0, down0)
    z2 = shift(z1, "z", 1)
    left_h = shift(left, "h", 1)
    up1, down1, z2, left, left_h = event(up1, down1, z2, left, left_h)

    up2, down2 = both(z2, up1, down1)
    z3 = shift(z2, "z", 1)
    left = jnp.stack([left, left_h])
    left_1, left_3 = shift(left, "x", 1), shift(left, "x", 3)
    up2, down2, z3, left, left_1, left_3 = event(up2, down2, z3, left, left_1, left_3)

    up3, down3 = both(z3, up2, down2)
    left_0, left_1, left_2 = arrange_left(place, [left, left_1, shift(left, "x", 2), left_3])

    def slot(block, up, down, up_next, down_next):
        return [(block, 0, n), (up, 0, n), (down, 0, n), (up_next, n, half), (down_next, n, half)]

    total = multiply_part(left_0, slot(own, up0, down0, up1, down1) + slot(z1, up1, down1, up2, down2), None, "multiply_0")
    up3, down3, total = event(up3, down3, total)

    up4, down4 = shift(up3[:half], "y", 1), shift(down3[half:n], "y", -1)
    pieces = slot(z2, up2, down2, up3, down3) + [(z3, 0, n), (up3, 0, n), (down3, 0, n)]
    total = multiply_part(left_1, pieces, total, "multiply_1")
    up4, down4, total = event(up4, down4, total)
    cut = columns // 2
    keep_0, send_0 = multiply_last(token, left_2, total, [up4, down4], 0, cut, "multiply_2")
    got_0 = shift(send_0, "c", 1)
    keep_1, send_1 = multiply_last(token, left_2, total, [up4, down4], cut, columns, "multiply_3")
    got_1 = shift(send_1, "c", 1)
    return tuple(join(token, keep_0, keep_1, got_0, got_1))


def solution(mesh):
    fine = Mesh(mesh.devices.reshape(Y, Z, C, H, X), ("y", "z", "c", "h", "x"))
    pop, tp = ("y", "z", "c"), ("h", "x")
    in_specs = (
        P(pop + tp, None, None),
        P(pop + tp, None, None),
        P(pop, None, tp),
        P(pop, None, tp),
        P(pop + tp),
        P(pop + tp),
    )
    out_specs = (P(pop, tp), P(pop, tp))
    return jax.shard_map(shards, mesh=fine, in_specs=in_specs, out_specs=out_specs, check_vma=False)
```

time: 311 us -> 103 us (0.33)
  blocking collectives: 165 us -> 15.3 us
  local copies, waits for them, and re-layouts: 84.4 us -> 0.14 us
  waiting for transfers between devices: 0.06 us -> 31.9 us
  Pallas kernels: 0 us -> 16.1 us
  matrix products: 13.8 us -> 0 us
  between operations: 15.4 us -> 2.38 us
  starting transfers between devices: 29.9 us -> 33.4 us
  other arithmetic: 0.24 us -> 3.56 us
    all_gather x2 -> x0, blocking collectives: 90 us -> none  [the longest x1 47.2 us: shards(): lax.all_gather(up_left, 'tp', axis=0, tiled=True)]
    unnamed x1 -> x0, blocking collectives: 75.5 us -> none
    unnamed x11 -> x2, local copies, waits for them, and re-layouts: 48.4 us -> 0.01 us
    ppermute x0 -> x22, starting transfers between devices: none -> 33.4 us  [shift(): return lax.ppermute(x, axis, [(i, (i + by) % n) for i in range(n)])]
    ppermute x0 -> x22, waiting for transfers between devices: none -> 31.9 us  [shift(): return lax.ppermute(x, axis, [(i, (i + by) % n) for i in range(n)])]
    all_to_all x2 -> x0, starting transfers between devices: 29.8 us -> none  [the longest x1 16.8 us: shards(): lax.all_to_all(grouped[1], 'pop', split_axis=2, concat_axis=0, tiled=True)]
    all_to_all x2 -> x0, local copies, waits for them, and re-layouts: 19.5 us -> none  [the longest x1 9.73 us: shards(): lax.all_to_all(grouped[0], 'pop', split_axis=2, concat_axis=0, tiled=True)]
    all_gather x2 -> x0, local copies, waits for them, and re-layouts: 16.6 us -> none  [the longest x1 8.29 us: shards(): lax.all_gather(gate_left, 'tp', axis=0, tiled=True)]
  transfers between devices with their start and end apart: 4 -> 22, of which waited for: 0 -> 10; matrix products, arithmetic and copies ran while one was open for 29% -> 2% of each run, Pallas kernels for 0% -> 11%
where the time goes in v2:
time: 103 us
  starting transfers between devices  33.4 us (32%)
  waiting for transfers between devices  31.9 us (31%)
  Pallas kernels  16.1 us (16%)
  blocking collectives  15.3 us (15%)
  other arithmetic  3.56 us (3%)
  between operations  2.38 us (2%)
    ppermute x22, starting transfers between devices, shift(): return lax.ppermute(x, axis, [(i, (i + by) % n) for i in range(n)])  33.4 us
    ppermute x22, waiting for transfers between devices, shift(): return lax.ppermute(x, axis, [(i, (i + by) % n) for i in range(n)])  31.9 us
    all_to_all x1, blocking collectives, shards(): lax.all_to_all(left, ('y', 'z'), split_axis=0, concat_axis=0, tiled=True)  15.3 us
    pallas_call x2, Pallas kernels, multiply_part(): pl.pallas_call(functools.partial(part_kernel, ranges, 256), out_shape=jax...  10.3 us
    pallas_call x2, Pallas kernels, multiply_last(): pl.pallas_call(functools.partial(last_kernel, cut, 256), out_shape=(shape...  2.87 us
  transfers between devices with their start and end apart: 22, of which 10 were waited for; matrix products, arithmetic and copies ran while one was open for 2% of the time, Pallas kernels for 11%

profile of v2, /device:TPU:1, one launch (start us, length us, event | category | flops | bytes accessed | tf_op | source)
XLA Modules:
  0.0 102.9 jit_solution(5776997633545795073)
XLA Ops:
  2.9 3.3 %collective-permute-start.5 = (bf16[4,8192]{1,0:T(4,128)(2,1)S(1)}, bf16[4,8192]{1,0:T(4,128)(2,1)S(1)}, u32[]{:S(2)}, u32[]{:S(2)}) collective-permute-start(bf16[4,8192]{1,0:T(4,128)(2,1)S(1)} %select_bitcast_fusion), channel_id=1, source_target_pairs={{0,8},{8,0},{1,9},{9,1},{2,10},{10,2},{3,11},{11,3},{4,12},{12,4},... | collective-permute-start | bytes 196616 | tf_op jit(solution)/shard_map/ppermute | solution.py:17
  9.5 2.6 %collective-permute-start.3 = (bf16[64,3584]{1,0:T(8,128)(2,1)S(1)}, bf16[64,3584]{1,0:T(8,128)(2,1)S(1)}, u32[]{:S(2)}, u32[]{:S(2)}) collective-permute-start(bf16[64,3584]{1,0:T(8,128)(2,1)S(1)} %maximum_bitcast_fusion.refs_0_), channel_id=1, source_target_pairs={{0,192},{64,0},{128,64},{192,128},{1,193},{65,1},{129,65},{193,129... | collective-permute-start | bytes 1376264 | tf_op jit(solution)/shard_map/ppermute | solution.py:17
  12.2 15.3 %all_to_all.5 = bf16[16,8,512]{2,1,0:T(8,128)(2,1)S(1)} all-to-all(bf16[16,8,512]{2,1,0:T(8,128)(2,1)S(1)} %bitcast.26), channel_id=1, replica_groups=mesh['y'=4,'z'=4,'c'=2,'h'=2,'x'=4] {'y','z'}, dimensions={0} | all-to-all | bytes 262144 | tf_op jit(solution)/shard_map/all_to_all | solution.py:241
  29.2 1.0 collective-permute-start.8
  30.2 5.2 %collective-permute-start.9 = (bf16[16,8,512]{2,1,0:T(8,128)(2,1)S(1)}, bf16[16,8,512]{2,1,0:T(8,128)(2,1)S(1)}, u32[]{:S(2)}, u32[]{:S(2)}) collective-permute-start(bf16[16,8,512]{2,1,0:T(8,128)(2,1)S(1)} %all_to_all.5), channel_id=1, source_target_pairs={{0,4},{4,0},{1,5},{5,1},{2,6},{6,2},{3,7},{7,3},{8,12},{12,8},{9,1... | collective-permute-start | bytes 393224 | tf_op jit(solution)/shard_map/ppermute | solution.py:17
  35.5 12.8 %collective-permute-done.9 = bf16[16,8,512]{2,1,0:T(8,128)(2,1)S(1)} collective-permute-done((bf16[16,8,512]{2,1,0:T(8,128)(2,1)S(1)}, bf16[16,8,512]{2,1,0:T(8,128)(2,1)S(1)}, u32[]{:S(2)}, u32[]{:S(2)}) %collective-permute-start.9) | collective-permute-done | bytes 131104 | tf_op jit(solution)/shard_map/ppermute | solution.py:17
  48.4 1.8 %collective-permute-start.11 = (bf16[96,3584]{1,0:T(8,128)(2,1)S(1)}, bf16[96,3584]{1,0:T(8,128)(2,1)S(1)}, u32[]{:S(2)}, u32[]{:S(2)}) collective-permute-start(bf16[96,3584]{1,0:T(8,128)(2,1)S(1)} %get-tuple-element.76), channel_id=1, source_target_pairs={{0,192},{64,0},{128,64},{192,128},{1,193},{65,1},{129,65},{193,129... | collective-permute-start | bytes 2064392 | tf_op jit(solution)/shard_map/ppermute | solution.py:17
  50.3 2.5 %collective-permute-start.14 = (bf16[2,16,8,512]{3,2,1,0:T(8,128)(2,1)S(1)}, bf16[2,16,8,512]{3,2,1,0:T(8,128)(2,1)S(1)}, u32[]{:S(2)}, u32[]{:S(2)}) collective-permute-start(bf16[2,16,8,512]{3,2,1,0:T(8,128)(2,1)S(1)} %pad_maximum_fusion.6.refs_0_), channel_id=1, source_target_pairs={{0,3},{1,0},{2,1},{3,2},{4,7},{5,4},{6,5},{7,6},{8,11},{9,8},{10,9... | collective-permute-start | bytes 786440 | tf_op jit(solution)/shard_map/ppermute | solution.py:17
  52.8 3.3 %collective-permute-done.14.refs_3_ = bf16[2,16,8,512]{3,2,1,0:T(8,128)(2,1)S(1)} collective-permute-done((bf16[2,16,8,512]{3,2,1,0:T(8,128)(2,1)S(1)}, bf16[2,16,8,512]{3,2,1,0:T(8,128)(2,1)S(1)}, u32[]{:S(2)}, u32[]{:S(2)}) %collective-permute-start.14) | collective-permute-done | bytes 262176 | tf_op jit(solution)/shard_map/ppermute | solution.py:17
  56.1 3.4 %collective-permute-done.13.refs_1_ = bf16[2,16,8,512]{3,2,1,0:T(8,128)(2,1)S(1)} collective-permute-done((bf16[2,16,8,512]{3,2,1,0:T(8,128)(2,1)S(1)}, bf16[2,16,8,512]{3,2,1,0:T(8,128)(2,1)S(1)}, u32[]{:S(2)}, u32[]{:S(2)}) %collective-permute-start.13) | collective-permute-done | bytes 262176 | tf_op jit(solution)/shard_map/ppermute | solution.py:17
  59.5 3.2 %collective-permute-done.12.refs_5_ = bf16[64,3584]{1,0:T(8,128)(2,1)S(1)} collective-permute-done((bf16[64,3584]{1,0:T(8,128)(2,1)S(1)}, bf16[64,3584]{1,0:T(8,128)(2,1)S(1)}, u32[]{:S(2)}, u32[]{:S(2)}) %collective-permute-start.12) | collective-permute-done | bytes 458784 | tf_op jit(solution)/shard_map/ppermute | solution.py:17
  63.8 1.7 %collective-permute-start.16 = (bf16[96,3584]{1,0:T(8,128)(2,1)S(1)}, bf16[96,3584]{1,0:T(8,128)(2,1)S(1)}, u32[]{:S(2)}, u32[]{:S(2)}) collective-permute-start(bf16[96,3584]{1,0:T(8,128)(2,1)S(1)} %get-tuple-element.74), channel_id=1, source_target_pairs={{0,192},{64,0},{128,64},{192,128},{1,193},{65,1},{129,65},{193,129... | collective-permute-start | bytes 2064392 | tf_op jit(solution)/shard_map/ppermute | solution.py:17
  65.6 2.7 %collective-permute-start.17 = (bf16[2,16,8,512]{3,2,1,0:T(8,128)(2,1)S(1)}, bf16[2,16,8,512]{3,2,1,0:T(8,128)(2,1)S(1)}, u32[]{:S(2)}, u32[]{:S(2)}) collective-permute-start(bf16[2,16,8,512]{3,2,1,0:T(8,128)(2,1)S(1)} %pad_maximum_fusion.6.refs_0_), channel_id=1, source_target_pairs={{0,2},{1,3},{2,0},{3,1},{4,6},{5,7},{6,4},{7,5},{8,10},{9,11},{10,... | collective-permute-start | bytes 786440 | tf_op jit(solution)/shard_map/ppermute | solution.py:17
  68.3 4.0 %collective-permute-done.17.refs_2_ = bf16[2,16,8,512]{3,2,1,0:T(8,128)(2,1)S(1)} collective-permute-done((bf16[2,16,8,512]{3,2,1,0:T(8,128)(2,1)S(1)}, bf16[2,16,8,512]{3,2,1,0:T(8,128)(2,1)S(1)}, u32[]{:S(2)}, u32[]{:S(2)}) %collective-permute-start.17) | collective-permute-done | bytes 262176 | tf_op jit(solution)/shard_map/ppermute | solution.py:17
  72.3 1.1 %arrange_left.1 = (bf16[512,512]{1,0:T(8,128)(2,1)S(1)}, bf16[512,448]{1,0:T(8,128)(2,1)S(1)}, bf16[512,64]{1,0:T(8,128)(2,1)S(1)}) custom-call(s32[4]{0:T(128)S(1)} %pad_add_fusion.place_ref, bf16[2,16,8,512]{3,2,1,0:T(8,128)(2,1)S(1)} %pad_maximum_fusion.6.refs_0_, bf16[2,16,8,512]{3,2,1,0:T(8,128)(2,1)S(1)} %collective-permute-done.13.refs_1_, ...), custom_call_target="tpu_custom_call" | custom-call | bytes 6291456 | tf_op jit(solution)/shard_map/arrange_left/pallas_call | solution.py:47
  73.4 5.1 %multiply_0.1.refs_6_ = f32[512,3584]{1,0:T(8,128)S(1)} custom-call(bf16[512,512]{1,0:T(8,128)(2,1)S(1)} %get-tuple-element.58.left_ref, bf16[64,3584]{1,0:T(8,128)(2,1)S(1)} %maximum_bitcast_fusion.refs_0_, bf16[64,3584]{1,0:T(8,128)(2,1)S(1)} %collective-permute-done.2.refs_1_, bf16[64,3584]{1,0:T(8,128)(2,1)S(1)} %collective-permute-done.3.refs_2_, ...), custom_call_target="tpu_custom_call" | custom-call | flops 3758096384 | bytes 12582912 | tf_op jit(solution)/shard_map/multiply_0/pallas_call | solution.py:105
  79.3 2.7 %collective-permute-start.19 = (bf16[32,3584]{1,0:T(8,128)(2,1)S(1)}, bf16[32,3584]{1,0:T(8,128)(2,1)S(1)}, u32[]{:S(2)}, u32[]{:S(2)}) collective-permute-start(bf16[32,3584]{1,0:T(8,128)(2,1)S(1)} %slice.31), channel_id=1, source_target_pairs={{0,192},{64,0},{128,64},{192,128},{1,193},{65,1},{129,65},{193,129... | collective-permute-start | bytes 688136 | tf_op jit(solution)/shard_map/ppermute | solution.py:17
  81.9 5.1 %multiply_1.1.total_ref = f32[512,3584]{1,0:T(8,128)S(1)} custom-call(bf16[512,448]{1,0:T(8,128)(2,1)S(1)} %get-tuple-element.62.left_ref, bf16[64,3584]{1,0:T(8,128)(2,1)S(1)} %collective-permute-done.8.refs_0_, bf16[96,3584]{1,0:T(8,128)(2,1)S(1)} %collective-permute-done.10.refs_6_.refs_1_, ...), custom_call_target="tpu_custom_call", output_to_operand_aliasing={{}: (7, {})} | custom-call | flops 3288334336 | bytes 12582912 | tf_op jit(solution)/shard_map/multiply_1/pallas_call | solution.py:105
  87.1 1.4 %multiply_3.1 = (bf16[256,1792]{1,0:T(8,128)(2,1)S(1)}, bf16[256,1792]{1,0:T(8,128)(2,1)S(1)}) custom-call(s32[1]{0:T(128)} %bitcast.5.core_ref, bf16[512,64]{1,0:T(8,128)(2,1)S(1)} %get-tuple-element.66.left_ref, f32[512,3584]{1,0:T(8,128)S(1)} %multiply_1.1.total_ref, bf16[32,3584]{1,0:T(8,128)(2,1)S(1)} %collective-permute-done.18.refs_0_, ...), custom_call_target="tpu_custom_call" | custom-call | flops 469762048 | bytes 6291456 | tf_op jit(solution)/shard_map/multiply_3/pallas_call | solution.py:146
  88.6 1.4 %multiply_2.1 = (bf16[256,1792]{1,0:T(8,128)(2,1)S(1)}, bf16[256,1792]{1,0:T(8,128)(2,1)S(1)}) custom-call(s32[1]{0:T(128)} %bitcast.5.core_ref, bf16[512,64]{1,0:T(8,128)(2,1)S(1)} %get-tuple-element.66.left_ref, f32[512,3584]{1,0:T(8,128)S(1)} %multiply_1.1.total_ref, bf16[32,3584]{1,0:T(8,128)(2,1)S(1)} %collective-permute-done.18.refs_0_, ...), custom_call_target="tpu_custom_call" | custom-call | flops 469762048 | bytes 6291456 | tf_op jit(solution)/shard_map/multiply_2/pallas_call | solution.py:146
  90.0 7.5 %collective-permute-start.21 = (bf16[256,1792]{1,0:T(8,128)(2,1)S(1)}, bf16[256,1792]{1,0:T(8,128)(2,1)S(1)}, u32[]{:S(2)}, u32[]{:S(2)}) collective-permute-start(bf16[256,1792]{1,0:T(8,128)(2,1)S(1)} %get-tuple-element.73), channel_id=1, source_target_pairs={{0,8},{8,0},{1,9},{9,1},{2,10},{10,2},{3,11},{11,3},{4,12},{12,4},... | collective-permute-start | bytes 2752520 | tf_op jit(solution)/shard_map/ppermute | solution.py:17
  97.6 2.0 %collective-permute-done.21.got_1 = bf16[256,1792]{1,0:T(8,128)(2,1)S(1)} collective-permute-done((bf16[256,1792]{1,0:T(8,128)(2,1)S(1)}, bf16[256,1792]{1,0:T(8,128)(2,1)S(1)}, u32[]{:S(2)}, u32[]{:S(2)}) %collective-permute-start.21) | collective-permute-done | bytes 917536 | tf_op jit(solution)/shard_map/ppermute | solution.py:17
  99.6 1.3 %collective-permute-done.20.got_0 = bf16[256,1792]{1,0:T(8,128)(2,1)S(1)} collective-permute-done((bf16[256,1792]{1,0:T(8,128)(2,1)S(1)}, bf16[256,1792]{1,0:T(8,128)(2,1)S(1)}, u32[]{:S(2)}, u32[]{:S(2)}) %collective-permute-start.20) | collective-permute-done | bytes 917536 | tf_op jit(solution)/shard_map/ppermute | solution.py:17
  100.9 1.9 %join.1 = (bf16[256,3584]{1,0:T(8,128)(2,1)}, bf16[256,3584]{1,0:T(8,128)(2,1)}) custom-call(s32[1]{0:T(128)} %bitcast.5.core_ref, bf16[256,1792]{1,0:T(8,128)(2,1)S(1)} %get-tuple-element.70.keep_0, bf16[256,1792]{1,0:T(8,128)(2,1)S(1)} %get-tuple-element.71.keep_1, bf16[256,1792]{1,0:T(8,128)(2,1)S(1)} %collective-permute-done.20.got_0, ...), custom_call_target="tpu_custom_call" | custom-call | tf_op jit(solution)/shard_map/join/pallas_call | solution.py:182
  (48 shorter events, 7.9 us)
Async XLA Ops:
  0.6 8.5 %copy-start = (bf16[8,4,3584]{2,1,0:T(4,128)(2,1)S(1)}, bf16[8,4,3584]{2,1,0:T(4,128)(2,1)}, u32[]{:S(2)}) copy-start(bf16[8,4,3584]{2,1,0:T(4,128)(2,1)} %param.8) | copy-start | bytes 688132
  2.9 4.2 %collective-permute-start.5 = (bf16[4,8192]{1,0:T(4,128)(2,1)S(1)}, bf16[4,8192]{1,0:T(4,128)(2,1)S(1)}, u32[]{:S(2)}, u32[]{:S(2)}) collective-permute-start(bf16[4,8192]{1,0:T(4,128)(2,1)S(1)} %select_bitcast_fusion), channel_id=1, source_target_pairs={{0,8},{8,0},{1,9},{9,1},{2,10},{10,2},{3,11},{11,3},{4,12},{12,4},... | collective-permute-start | bytes 196616 | tf_op jit(solution)/shard_map/ppermute | solution.py:17
  6.2 1.9 %collective-permute-start.1 = (bf16[8,4,3584]{2,1,0:T(4,128)(2,1)}, bf16[8,4,3584]{2,1,0:T(4,128)(2,1)S(1)}, u32[]{:S(2)}, u32[]{:S(2)}) collective-permute-start(bf16[8,4,3584]{2,1,0:T(4,128)(2,1)} %param.8), channel_id=1, source_target_pairs={{0,8},{8,0},{1,9},{9,1},{2,10},{10,2},{3,11},{11,3},{4,12},{12,4},... | collective-permute-start | bytes 688136 | tf_op jit(solution)/shard_map/ppermute | solution.py:17
  6.3 2.8 %collective-permute-start = (bf16[8,4,3584]{2,1,0:T(4,128)(2,1)}, bf16[8,4,3584]{2,1,0:T(4,128)(2,1)S(1)}, u32[]{:S(2)}, u32[]{:S(2)}) collective-permute-start(bf16[8,4,3584]{2,1,0:T(4,128)(2,1)} %param.9), channel_id=1, source_target_pairs={{0,8},{8,0},{1,9},{9,1},{2,10},{10,2},{3,11},{11,3},{4,12},{12,4},... | collective-permute-start | bytes 688136 | tf_op jit(solution)/shard_map/ppermute | solution.py:17
  9.4 18.1 %collective-permute-start.4 = (bf16[64,3584]{1,0:T(8,128)(2,1)S(1)}, bf16[64,3584]{1,0:T(8,128)(2,1)S(1)}, u32[]{:S(2)}, u32[]{:S(2)}) collective-permute-start(bf16[64,3584]{1,0:T(8,128)(2,1)S(1)} %maximum_bitcast_fusion.refs_0_), channel_id=1, source_target_pairs={{0,16},{16,32},{32,48},{48,0},{1,17},{17,33},{33,49},{49,1},{2,18}... | collective-permute-start | bytes 1376264 | tf_op jit(solution)/shard_map/ppermute | solution.py:17
  9.5 18.0 %collective-permute-start.3 = (bf16[64,3584]{1,0:T(8,128)(2,1)S(1)}, bf16[64,3584]{1,0:T(8,128)(2,1)S(1)}, u32[]{:S(2)}, u32[]{:S(2)}) collective-permute-start(bf16[64,3584]{1,0:T(8,128)(2,1)S(1)} %maximum_bitcast_fusion.refs_0_), channel_id=1, source_target_pairs={{0,192},{64,0},{128,64},{192,128},{1,193},{65,1},{129,65},{193,129... | collective-permute-start | bytes 1376264 | tf_op jit(solution)/shard_map/ppermute | solution.py:17
  12.1 15.4 %collective-permute-start.2 = (bf16[64,3584]{1,0:T(8,128)(2,1)S(1)}, bf16[64,3584]{1,0:T(8,128)(2,1)S(1)}, u32[]{:S(2)}, u32[]{:S(2)}) collective-permute-start(bf16[64,3584]{1,0:T(8,128)(2,1)S(1)} %maximum_bitcast_fusion.refs_0_), channel_id=1, source_target_pairs={{0,64},{64,128},{128,192},{192,0},{1,65},{65,129},{129,193},{193,1... | collective-permute-start | bytes 1376264 | tf_op jit(solution)/shard_map/ppermute | solution.py:17
  27.7 20.6 %collective-permute-start.7 = (bf16[96,3584]{1,0:T(8,128)(2,1)S(1)}, bf16[96,3584]{1,0:T(8,128)(2,1)S(1)}, u32[]{:S(2)}, u32[]{:S(2)}) collective-permute-start(bf16[96,3584]{1,0:T(8,128)(2,1)S(1)} %get-tuple-element.78), channel_id=1, source_target_pairs={{0,192},{64,0},{128,64},{192,128},{1,193},{65,1},{129,65},{193,129... | collective-permute-start | bytes 2064392 | tf_op jit(solution)/shard_map/ppermute | solution.py:17
  28.3 20.0 %collective-permute-start.6 = (bf16[96,3584]{1,0:T(8,128)(2,1)S(1)}, bf16[96,3584]{1,0:T(8,128)(2,1)S(1)}, u32[]{:S(2)}, u32[]{:S(2)}) collective-permute-start(bf16[96,3584]{1,0:T(8,128)(2,1)S(1)} %get-tuple-element.79), channel_id=1, source_target_pairs={{0,64},{64,128},{128,192},{192,0},{1,65},{65,129},{129,193},{193,1... | collective-permute-start | bytes 2064392 | tf_op jit(solution)/shard_map/ppermute | solution.py:17
  29.2 19.1 %collective-permute-start.8 = (bf16[64,3584]{1,0:T(8,128)(2,1)S(1)}, bf16[64,3584]{1,0:T(8,128)(2,1)S(1)}, u32[]{:S(2)}, u32[]{:S(2)}) collective-permute-start(bf16[64,3584]{1,0:T(8,128)(2,1)S(1)} %collective-permute-done.4.refs_5_), channel_id=1, source_target_pairs={{0,16},{16,32},{32,48},{48,0},{1,17},{17,33},{33,49},{49,1},{2,18}... | collective-permute-start | bytes 1376264 | tf_op jit(solution)/shard_map/ppermute | solution.py:17
  30.2 18.0 %collective-permute-start.9 = (bf16[16,8,512]{2,1,0:T(8,128)(2,1)S(1)}, bf16[16,8,512]{2,1,0:T(8,128)(2,1)S(1)}, u32[]{:S(2)}, u32[]{:S(2)}) collective-permute-start(bf16[16,8,512]{2,1,0:T(8,128)(2,1)S(1)} %all_to_all.5), channel_id=1, source_target_pairs={{0,4},{4,0},{1,5},{5,1},{2,6},{6,2},{3,7},{7,3},{8,12},{12,8},{9,1... | collective-permute-start | bytes 393224 | tf_op jit(solution)/shard_map/ppermute | solution.py:17
  48.4 14.3 %collective-permute-start.11 = (bf16[96,3584]{1,0:T(8,128)(2,1)S(1)}, bf16[96,3584]{1,0:T(8,128)(2,1)S(1)}, u32[]{:S(2)}, u32[]{:S(2)}) collective-permute-start(bf16[96,3584]{1,0:T(8,128)(2,1)S(1)} %get-tuple-element.76), channel_id=1, source_target_pairs={{0,192},{64,0},{128,64},{192,128},{1,193},{65,1},{129,65},{193,129... | collective-permute-start | bytes 2064392 | tf_op jit(solution)/shard_map/ppermute | solution.py:17
  50.3 13.4 %collective-permute-start.10 = (bf16[96,3584]{1,0:T(8,128)(2,1)S(1)}, bf16[96,3584]{1,0:T(8,128)(2,1)S(1)}, u32[]{:S(2)}, u32[]{:S(2)}) collective-permute-start(bf16[96,3584]{1,0:T(8,128)(2,1)S(1)} %get-tuple-element.77), channel_id=1, source_target_pairs={{0,64},{64,128},{128,192},{192,0},{1,65},{65,129},{129,193},{193,1... | collective-permute-start | bytes 2064392 | tf_op jit(solution)/shard_map/ppermute | solution.py:17
  50.3 12.4 %collective-permute-start.12 = (bf16[64,3584]{1,0:T(8,128)(2,1)S(1)}, bf16[64,3584]{1,0:T(8,128)(2,1)S(1)}, u32[]{:S(2)}, u32[]{:S(2)}) collective-permute-start(bf16[64,3584]{1,0:T(8,128)(2,1)S(1)} %collective-permute-done.8.refs_0_), channel_id=1, source_target_pairs={{0,16},{16,32},{32,48},{48,0},{1,17},{17,33},{33,49},{49,1},{2,18}... | collective-permute-start | bytes 1376264 | tf_op jit(solution)/shard_map/ppermute | solution.py:17
  50.3 5.8 %collective-permute-start.14 = (bf16[2,16,8,512]{3,2,1,0:T(8,128)(2,1)S(1)}, bf16[2,16,8,512]{3,2,1,0:T(8,128)(2,1)S(1)}, u32[]{:S(2)}, u32[]{:S(2)}) collective-permute-start(bf16[2,16,8,512]{3,2,1,0:T(8,128)(2,1)S(1)} %pad_maximum_fusion.6.refs_0_), channel_id=1, source_target_pairs={{0,3},{1,0},{2,1},{3,2},{4,7},{5,4},{6,5},{7,6},{8,11},{9,8},{10,9... | collective-permute-start | bytes 786440 | tf_op jit(solution)/shard_map/ppermute | solution.py:17
  52.8 6.7 %collective-permute-start.13 = (bf16[2,16,8,512]{3,2,1,0:T(8,128)(2,1)S(1)}, bf16[2,16,8,512]{3,2,1,0:T(8,128)(2,1)S(1)}, u32[]{:S(2)}, u32[]{:S(2)}) collective-permute-start(bf16[2,16,8,512]{3,2,1,0:T(8,128)(2,1)S(1)} %pad_maximum_fusion.6.refs_0_), channel_id=1, source_target_pairs={{0,1},{1,2},{2,3},{3,0},{4,5},{5,6},{6,7},{7,4},{8,9},{9,10},{10,1... | collective-permute-start | bytes 786440 | tf_op jit(solution)/shard_map/ppermute | solution.py:17
  63.8 14.7 %collective-permute-start.16 = (bf16[96,3584]{1,0:T(8,128)(2,1)S(1)}, bf16[96,3584]{1,0:T(8,128)(2,1)S(1)}, u32[]{:S(2)}, u32[]{:S(2)}) collective-permute-start(bf16[96,3584]{1,0:T(8,128)(2,1)S(1)} %get-tuple-element.74), channel_id=1, source_target_pairs={{0,192},{64,0},{128,64},{192,128},{1,193},{65,1},{129,65},{193,129... | collective-permute-start | bytes 2064392 | tf_op jit(solution)/shard_map/ppermute | solution.py:17
  65.5 13.6 %collective-permute-start.15 = (bf16[96,3584]{1,0:T(8,128)(2,1)S(1)}, bf16[96,3584]{1,0:T(8,128)(2,1)S(1)}, u32[]{:S(2)}, u32[]{:S(2)}) collective-permute-start(bf16[96,3584]{1,0:T(8,128)(2,1)S(1)} %get-tuple-element.75), channel_id=1, source_target_pairs={{0,64},{64,128},{128,192},{192,0},{1,65},{65,129},{129,193},{193,1... | collective-permute-start | bytes 2064392 | tf_op jit(solution)/shard_map/ppermute | solution.py:17
  65.6 6.7 %collective-permute-start.17 = (bf16[2,16,8,512]{3,2,1,0:T(8,128)(2,1)S(1)}, bf16[2,16,8,512]{3,2,1,0:T(8,128)(2,1)S(1)}, u32[]{:S(2)}, u32[]{:S(2)}) collective-permute-start(bf16[2,16,8,512]{3,2,1,0:T(8,128)(2,1)S(1)} %pad_maximum_fusion.6.refs_0_), channel_id=1, source_target_pairs={{0,2},{1,3},{2,0},{3,1},{4,6},{5,7},{6,4},{7,5},{8,10},{9,11},{10,... | collective-permute-start | bytes 786440 | tf_op jit(solution)/shard_map/ppermute | solution.py:17
  79.2 7.9 %collective-permute-start.18 = (bf16[32,3584]{1,0:T(8,128)(2,1)S(1)}, bf16[32,3584]{1,0:T(8,128)(2,1)S(1)}, u32[]{:S(2)}, u32[]{:S(2)}) collective-permute-start(bf16[32,3584]{1,0:T(8,128)(2,1)S(1)} %slice.30), channel_id=1, source_target_pairs={{0,64},{64,128},{128,192},{192,0},{1,65},{65,129},{129,193},{193,1... | collective-permute-start | bytes 688136 | tf_op jit(solution)/shard_map/ppermute | solution.py:17
  79.3 7.8 %collective-permute-start.19 = (bf16[32,3584]{1,0:T(8,128)(2,1)S(1)}, bf16[32,3584]{1,0:T(8,128)(2,1)S(1)}, u32[]{:S(2)}, u32[]{:S(2)}) collective-permute-start(bf16[32,3584]{1,0:T(8,128)(2,1)S(1)} %slice.31), channel_id=1, source_target_pairs={{0,192},{64,0},{128,64},{192,128},{1,193},{65,1},{129,65},{193,129... | collective-permute-start | bytes 688136 | tf_op jit(solution)/shard_map/ppermute | solution.py:17
  90.0 9.6 %collective-permute-start.21 = (bf16[256,1792]{1,0:T(8,128)(2,1)S(1)}, bf16[256,1792]{1,0:T(8,128)(2,1)S(1)}, u32[]{:S(2)}, u32[]{:S(2)}) collective-permute-start(bf16[256,1792]{1,0:T(8,128)(2,1)S(1)} %get-tuple-element.73), channel_id=1, source_target_pairs={{0,8},{8,0},{1,9},{9,1},{2,10},{10,2},{3,11},{11,3},{4,12},{12,4},... | collective-permute-start | bytes 2752520 | tf_op jit(solution)/shard_map/ppermute | solution.py:17
  97.5 3.4 %collective-permute-start.20 = (bf16[256,1792]{1,0:T(8,128)(2,1)S(1)}, bf16[256,1792]{1,0:T(8,128)(2,1)S(1)}, u32[]{:S(2)}, u32[]{:S(2)}) collective-permute-start(bf16[256,1792]{1,0:T(8,128)(2,1)S(1)} %get-tuple-element.72), channel_id=1, source_target_pairs={{0,8},{8,0},{1,9},{9,1},{2,10},{10,2},{3,11},{11,3},{4,12},{12,4},... | collective-permute-start | bytes 2752520 | tf_op jit(solution)/shard_map/ppermute | solution.py:17

commit v3 on v2

--- a/solution.py
+++ b/solution.py
@@ -88,7 +88,7 @@
             out_ref[:, at] = product if total_ref is None else total_ref[:, at] + product
             return _
 
-        lax.fori_loop(cuts[side] // width, cuts[side + 1] // width, step, None)
+        lax.fori_loop(cuts[side] // width, cuts[side + 1] // width, step, None, unroll=True)
 
 
 def multiply_part(left, pieces, total, name):
@@ -136,7 +136,7 @@
             out_ref[:, at] = total.astype(out_ref.dtype)
         return _
 
-    lax.fori_loop(0, columns // width, step, None)
+    lax.fori_loop(0, columns // width, step, None, unroll=True)
 
 
 def multiply_last(core, left, total, last, cut, end, name):
@@ -154,40 +154,42 @@
     )(core, left, total, *last)
 
 
-def join_kernel(core_ref, keep_0, keep_1, got_0, got_1, gate_ref, up_ref, sems):
-    def put(gate, up):
+def put_kernel(got, core_ref, half_0, half_1, *refs):
+    gate_ref, up_ref, sems = refs[-3:]
+
+    def put(out):
         copies = []
-        for out, halves in ((gate_ref, gate), (up_ref, up)):
-            for half, at in zip(halves, (0, halves[0].shape[1])):
-                to = out.at[:, pl.ds(at, half.shape[1])]
-                copies.append(pltpu.make_async_copy(half, to, sems.at[len(copies)]))
+        for k, (half, at) in enumerate(((half_0, 0), (half_1, half_0.shape[1]))):
+            copies.append(pltpu.make_async_copy(half, out.at[:, pl.ds(at, half.shape[1])], sems.at[k]))
         for copy in copies:
             copy.start()
         for copy in copies:
             copy.wait()
 
-    @pl.when(core_ref[0] == 0)
+    @pl.when(core_ref[0] == got)
     def _():
-        put((keep_0, keep_1), (got_0, got_1))
-
-    @pl.when(core_ref[0] == 1)
+        put(gate_ref)
+
+    @pl.when(core_ref[0] == 1 - got)
     def _():
-        put((got_0, got_1), (keep_0, keep_1))
-
-
-def join(core, *halves):
-    rows, columns = halves[0].shape[0], halves[0].shape[1] + halves[1].shape[1]
-    shape = jax.ShapeDtypeStruct((rows, columns), halves[0].dtype)
+        put(up_ref)
+
+
+def put(core, half_0, half_1, outs, got):
+    rows, columns = half_0.shape[0], half_0.shape[1] + half_1.shape[1]
+    shape = jax.ShapeDtypeStruct((rows, columns), half_0.dtype)
     anywhere = pl.BlockSpec(memory_space=pl.ANY)
     return pl.pallas_call(
-        join_kernel,
+        functools.partial(put_kernel, got),
         out_shape=(shape, shape),
-        in_specs=[pl.BlockSpec(memory_space=pltpu.SMEM)] + [anywhere] * 4,
+        in_specs=[pl.BlockSpec(memory_space=pltpu.SMEM)] + [anywhere] * (2 + len(outs)),
         out_specs=(anywhere, anywhere),
-        scratch_shapes=[pltpu.SemaphoreType.DMA((4,))],
+        scratch_shapes=[pltpu.SemaphoreType.DMA((2,))],
+        input_output_aliases={3 + k: k for k in range(len(outs))},
         compiler_params=pltpu.CompilerParams(vmem_limit_bytes=4 << 20),
-        name="join",
-    )(core, *halves)
+        cost_estimate=pl.CostEstimate(flops=0, bytes_accessed=4 << 20, transcendentals=0),
+        name="put_got" if got else "put_keep",
+    )(core, half_0, half_1, *outs)
 
 
 def weigh(left, coef):
@@ -208,14 +210,14 @@
         return arrived
 
     gate_got, up_got = shift(gate_right, "c", 1), shift(up_right, "c", 1)
-    own = jnp.concatenate([jnp.where(first, gate_right, up_got), jnp.where(first, gate_got, up_right)], axis=1)
-    own = own.reshape(-1, columns)
-
     centered = (2 * fitness_order - (total - 1)).astype(jnp.float32)
     coef = centered * member_scale / ((total - 1) * math.sqrt(total * rank))
     gate_w, up_w = weigh(gate_left, coef)[0], weigh(up_left, coef)[0]
-    left_mine = jnp.where(first, gate_w, up_w)
-    left_got = shift(jnp.where(first, up_w, gate_w), "c", 1)
+    left_mine, left_send = jnp.where(first, gate_w, up_w), jnp.where(first, up_w, gate_w)
+    gate_got, up_got, left_mine, left_send, place = event(gate_got, up_got, left_mine, left_send, place)
+    own = jnp.concatenate([jnp.where(first, gate_right, up_got), jnp.where(first, gate_got, up_right)], axis=1)
+    own = own.reshape(-1, columns)
+    left_got = shift(left_send, "c", 1)
     left = jnp.concatenate([jnp.where(first, left_mine, left_got), jnp.where(first, left_got, left_mine)], axis=0)
 
     def deal(block, axis, at, size):
@@ -231,21 +233,27 @@
     half = n // 2
 
     def both(block, up=None, down=None):
-        if up is None:
-            return shift(block, "y", 1), shift(block, "y", -1)
-        up = jnp.concatenate([block, up[:half]], axis=0)
-        down = jnp.concatenate([block, down[half:n]], axis=0)
+        if up is not None:
+            up, down = join(block, up, down)
+        else:
+            up = down = block
         return shift(up, "y", 1), shift(down, "y", -1)
+
+    def join(block, up, down):
+        return jnp.concatenate([block, up[:half]], axis=0), jnp.concatenate([block, down[half:n]], axis=0)
 
     left = left.reshape(C * rank, Y * Z, -1).transpose(1, 0, 2)
     left = lax.all_to_all(left, ("y", "z"), split_axis=0, concat_axis=0, tiled=True)
-    own, place = event(own, place)
+    own, = event(own)
     up0, down0 = both(own)
     z1 = shift(own, "z", 1)
-    up0, down0, z1, left = event(up0, down0, z1, left)
-
-    up1, down1 = both(z1, up0, down0)
+    up0, down0, z1 = event(up0, down0, z1)
+
+    up1, down1 = join(z1, up0, down0)
+    up1 = shift(up1, "y", 1)
     z2 = shift(z1, "z", 1)
+    left, down1 = event(left, down1)
+    down1 = shift(down1, "y", -1)
     left_h = shift(left, "h", 1)
     up1, down1, z2, left, left_h = event(up1, down1, z2, left, left_h)
 
@@ -272,8 +280,10 @@
     keep_0, send_0 = multiply_last(token, left_2, total, [up4, down4], 0, cut, "multiply_2")
     got_0 = shift(send_0, "c", 1)
     keep_1, send_1 = multiply_last(token, left_2, total, [up4, down4], cut, columns, "multiply_3")
+    got_0, send_1 = event(got_0, send_1)
     got_1 = shift(send_1, "c", 1)
-    return tuple(join(token, keep_0, keep_1, got_0, got_1))
+    outs = put(token, keep_0, keep_1, [], 0)
+    return tuple(put(token, got_0, got_1, outs, 1))
 
 
 def solution(mesh):

time: 103 us -> 97.9 us (0.950)
  blocking collectives: 15.3 us -> 0 us
  starting transfers between devices: 33.4 us -> 41.8 us
  waiting for transfers between devices: 31.9 us -> 38.2 us
  Pallas kernels: 16.1 us -> 11.9 us
    all_to_all x1 -> x0, blocking collectives: 15.3 us -> none  [shards(): lax.all_to_all(left, ('y', 'z'), split_axis=0, concat_axis=0, tiled=True)]
    all_to_all x0 -> x1, starting transfers between devices: none -> 6.76 us  [shards(): lax.all_to_all(left, ('y', 'z'), split_axis=0, concat_axis=0, tiled=True)]
    ppermute x22, waiting for transfers between devices: 31.9 us -> 36.3 us  [shift(): return lax.ppermute(x, axis, [(i, (i + by) % n) for i in range(n)])]
    pallas_call x2, Pallas kernels: 10.3 us -> 7.05 us  [multiply_part(): pl.pallas_call(functools.partial(part_kernel, ranges, 256), out_shape=jax...]
    all_to_all x0 -> x1, waiting for transfers between devices: none -> 1.92 us  [shards(): lax.all_to_all(left, ('y', 'z'), split_axis=0, concat_axis=0, tiled=True)]
    ppermute x22, starting transfers between devices: 33.4 us -> 35.1 us  [shift(): return lax.ppermute(x, axis, [(i, (i + by) % n) for i in range(n)])]
    pallas_call x2, Pallas kernels: 2.87 us -> 1.23 us  [multiply_last(): pl.pallas_call(functools.partial(last_kernel, cut, 256), out_shape=(shape...]
    pallas_call x1 -> x2, Pallas kernels: 1.86 us -> 2.48 us  [put(): pl.pallas_call(functools.partial(put_kernel, got), out_shape=(shape, shap...]
  transfers between devices with their start and end apart: 22 -> 23, of which waited for: 10 -> 13; matrix products, arithmetic and copies ran while one was open for 2% -> 3% of each run, Pallas kernels for 11% -> 10%
where the time goes in v3:
time: 97.9 us; the launch traced here: 97.7 us
  starting transfers between devices  41.8 us (43%)
  waiting for transfers between devices  38.2 us (39%)
  Pallas kernels  11.9 us (12%)
  other arithmetic  3.33 us (3%)
  between operations  2.29 us (2%)
    ppermute x22, waiting for transfers between devices, shift(): return lax.ppermute(x, axis, [(i, (i + by) % n) for i in range(n)])  36.3 us
    ppermute x22, starting transfers between devices, shift(): return lax.ppermute(x, axis, [(i, (i + by) % n) for i in range(n)])  35.1 us
    pallas_call x2, Pallas kernels, multiply_part(): pl.pallas_call(functools.partial(part_kernel, ranges, 256), out_shape=jax...  7.05 us
    all_to_all x1, starting transfers between devices, shards(): lax.all_to_all(left, ('y', 'z'), split_axis=0, concat_axis=0, tiled=True)  6.76 us
    pallas_call x2, Pallas kernels, put(): pl.pallas_call(functools.partial(put_kernel, got), out_shape=(shape, shap...  2.48 us
  transfers between devices with their start and end apart: 23, of which 13 were waited for; matrix products, arithmetic and copies ran while one was open for 3% of the time, Pallas kernels for 10%

profile of v3, /device:TPU:1, one launch (start us, length us, event | category | flops | bytes accessed | tf_op | source)
XLA Modules:
  0.0 97.7 jit_solution(12632182949222982229)
XLA Ops:
  0.6 3.3 %collective-permute-start = (bf16[8,4,3584]{2,1,0:T(4,128)(2,1)}, bf16[8,4,3584]{2,1,0:T(4,128)(2,1)S(1)}, u32[]{:S(2)}, u32[]{:S(2)}) collective-permute-start(bf16[8,4,3584]{2,1,0:T(4,128)(2,1)} %param.8), channel_id=1, source_target_pairs={{0,8},{8,0},{1,9},{9,1},{2,10},{10,2},{3,11},{11,3},{4,12},{12,4},... | collective-permute-start | bytes 688136 | tf_op jit(solution)/shard_map/ppermute | solution.py:17
  8.2 2.6 %collective-permute-start.3 = (bf16[64,3584]{1,0:T(8,128)(2,1)S(1)}, bf16[64,3584]{1,0:T(8,128)(2,1)S(1)}, u32[]{:S(2)}, u32[]{:S(2)}) collective-permute-start(bf16[64,3584]{1,0:T(8,128)(2,1)S(1)} %maximum_bitcast_fusion.refs_0_), channel_id=1, source_target_pairs={{0,192},{64,0},{128,64},{192,128},{1,193},{65,1},{129,65},{193,129... | collective-permute-start | bytes 1376264 | tf_op jit(solution)/shard_map/ppermute | solution.py:17
  11.6 6.8 %all-to-all-start = ((bf16[16,8,512]{2,1,0:T(8,128)(2,1)}), bf16[16,8,512]{2,1,0:T(8,128)(2,1)S(1)}, u32[]{:S(2)}, u32[]{:S(2)}) async-start(bf16[16,8,512]{2,1,0:T(8,128)(2,1)} %bitcast.10), calls=%async_computation | async-start | bytes 262144 | tf_op jit(solution)/shard_map/all_to_all | solution.py:246
  18.4 3.7 %collective-permute-done.4.refs_5_ = bf16[64,3584]{1,0:T(8,128)(2,1)S(1)} collective-permute-done((bf16[64,3584]{1,0:T(8,128)(2,1)S(1)}, bf16[64,3584]{1,0:T(8,128)(2,1)S(1)}, u32[]{:S(2)}, u32[]{:S(2)}) %collective-permute-start.4) | collective-permute-done | bytes 458784 | tf_op jit(solution)/shard_map/ppermute | solution.py:17
  22.1 1.5 %collective-permute-done.2.refs_1_ = bf16[64,3584]{1,0:T(8,128)(2,1)S(1)} collective-permute-done((bf16[64,3584]{1,0:T(8,128)(2,1)S(1)}, bf16[64,3584]{1,0:T(8,128)(2,1)S(1)}, u32[]{:S(2)}, u32[]{:S(2)}) %collective-permute-start.2) | collective-permute-done | bytes 458784 | tf_op jit(solution)/shard_map/ppermute | solution.py:17
  23.7 1.9 %all-to-all-done = bf16[16,8,512]{2,1,0:T(8,128)(2,1)S(1)} async-done(((bf16[16,8,512]{2,1,0:T(8,128)(2,1)}), bf16[16,8,512]{2,1,0:T(8,128)(2,1)S(1)}, u32[]{:S(2)}, u32[]{:S(2)}) %all-to-all-start) | async-done | bytes 131104 | tf_op jit(solution)/shard_map/all_to_all | solution.py:246
  27.7 5.5 %collective-permute-start.9 = (bf16[16,8,512]{2,1,0:T(8,128)(2,1)S(1)}, bf16[16,8,512]{2,1,0:T(8,128)(2,1)S(1)}, u32[]{:S(2)}, u32[]{:S(2)}) collective-permute-start(bf16[16,8,512]{2,1,0:T(8,128)(2,1)S(1)} %all-to-all-done), channel_id=1, source_target_pairs={{0,4},{4,0},{1,5},{5,1},{2,6},{6,2},{3,7},{7,3},{8,12},{12,8},{9,1... | collective-permute-start | bytes 393224 | tf_op jit(solution)/shard_map/ppermute | solution.py:17
  33.3 11.4 %collective-permute-done.9 = bf16[16,8,512]{2,1,0:T(8,128)(2,1)S(1)} collective-permute-done((bf16[16,8,512]{2,1,0:T(8,128)(2,1)S(1)}, bf16[16,8,512]{2,1,0:T(8,128)(2,1)S(1)}, u32[]{:S(2)}, u32[]{:S(2)}) %collective-permute-start.9) | collective-permute-done | bytes 131104 | tf_op jit(solution)/shard_map/ppermute | solution.py:17
  44.9 2.5 %collective-permute-start.11 = (bf16[96,3584]{1,0:T(8,128)(2,1)S(1)}, bf16[96,3584]{1,0:T(8,128)(2,1)S(1)}, u32[]{:S(2)}, u32[]{:S(2)}) collective-permute-start(bf16[96,3584]{1,0:T(8,128)(2,1)S(1)} %get-tuple-element.100), channel_id=1, source_target_pairs={{0,192},{64,0},{128,64},{192,128},{1,193},{65,1},{129,65},{193,129... | collective-permute-start | bytes 2064392 | tf_op jit(solution)/shard_map/ppermute | solution.py:17
  47.4 2.6 %collective-permute-start.14 = (bf16[2,16,8,512]{3,2,1,0:T(8,128)(2,1)S(1)}, bf16[2,16,8,512]{3,2,1,0:T(8,128)(2,1)S(1)}, u32[]{:S(2)}, u32[]{:S(2)}) collective-permute-start(bf16[2,16,8,512]{3,2,1,0:T(8,128)(2,1)S(1)} %pad_maximum_fusion.6.refs_0_), channel_id=1, source_target_pairs={{0,3},{1,0},{2,1},{3,2},{4,7},{5,4},{6,5},{7,6},{8,11},{9,8},{10,9... | collective-permute-start | bytes 786440 | tf_op jit(solution)/shard_map/ppermute | solution.py:17
  50.0 3.3 %collective-permute-done.14.refs_3_ = bf16[2,16,8,512]{3,2,1,0:T(8,128)(2,1)S(1)} collective-permute-done((bf16[2,16,8,512]{3,2,1,0:T(8,128)(2,1)S(1)}, bf16[2,16,8,512]{3,2,1,0:T(8,128)(2,1)S(1)}, u32[]{:S(2)}, u32[]{:S(2)}) %collective-permute-start.14) | collective-permute-done | bytes 262176 | tf_op jit(solution)/shard_map/ppermute | solution.py:17
  53.3 3.1 %collective-permute-done.13.refs_1_ = bf16[2,16,8,512]{3,2,1,0:T(8,128)(2,1)S(1)} collective-permute-done((bf16[2,16,8,512]{3,2,1,0:T(8,128)(2,1)S(1)}, bf16[2,16,8,512]{3,2,1,0:T(8,128)(2,1)S(1)}, u32[]{:S(2)}, u32[]{:S(2)}) %collective-permute-start.13) | collective-permute-done | bytes 262176 | tf_op jit(solution)/shard_map/ppermute | solution.py:17
  57.2 2.8 %collective-permute-done.10.refs_6_.refs_1_ = bf16[96,3584]{1,0:T(8,128)(2,1)S(1)} collective-permute-done((bf16[96,3584]{1,0:T(8,128)(2,1)S(1)}, bf16[96,3584]{1,0:T(8,128)(2,1)S(1)}, u32[]{:S(2)}, u32[]{:S(2)}) %collective-permute-start.10) | collective-permute-done | bytes 688160 | tf_op jit(solution)/shard_map/ppermute | solution.py:17
  60.7 1.2 %collective-permute-start.15 = (bf16[96,3584]{1,0:T(8,128)(2,1)S(1)}, bf16[96,3584]{1,0:T(8,128)(2,1)S(1)}, u32[]{:S(2)}, u32[]{:S(2)}) collective-permute-start(bf16[96,3584]{1,0:T(8,128)(2,1)S(1)} %get-tuple-element.99), channel_id=1, source_target_pairs={{0,64},{64,128},{128,192},{192,0},{1,65},{65,129},{129,193},{193,1... | collective-permute-start | bytes 2064392 | tf_op jit(solution)/shard_map/ppermute | solution.py:17
  61.9 2.7 %collective-permute-start.17 = (bf16[2,16,8,512]{3,2,1,0:T(8,128)(2,1)S(1)}, bf16[2,16,8,512]{3,2,1,0:T(8,128)(2,1)S(1)}, u32[]{:S(2)}, u32[]{:S(2)}) collective-permute-start(bf16[2,16,8,512]{3,2,1,0:T(8,128)(2,1)S(1)} %pad_maximum_fusion.6.refs_0_), channel_id=1, source_target_pairs={{0,2},{1,3},{2,0},{3,1},{4,6},{5,7},{6,4},{7,5},{8,10},{9,11},{10,... | collective-permute-start | bytes 786440 | tf_op jit(solution)/shard_map/ppermute | solution.py:17
  64.6 4.0 %collective-permute-done.17.refs_2_ = bf16[2,16,8,512]{3,2,1,0:T(8,128)(2,1)S(1)} collective-permute-done((bf16[2,16,8,512]{3,2,1,0:T(8,128)(2,1)S(1)}, bf16[2,16,8,512]{3,2,1,0:T(8,128)(2,1)S(1)}, u32[]{:S(2)}, u32[]{:S(2)}) %collective-permute-start.17) | collective-permute-done | bytes 262176 | tf_op jit(solution)/shard_map/ppermute | solution.py:17
  69.7 3.4 %multiply_0.1.refs_6_ = f32[512,3584]{1,0:T(8,128)S(1)} custom-call(bf16[512,512]{1,0:T(8,128)(2,1)S(1)} %get-tuple-element.77.left_ref, bf16[64,3584]{1,0:T(8,128)(2,1)S(1)} %maximum_bitcast_fusion.refs_0_, bf16[64,3584]{1,0:T(8,128)(2,1)S(1)} %collective-permute-done.2.refs_1_, bf16[64,3584]{1,0:T(8,128)(2,1)S(1)} %collective-permute-done.3.refs_2_, ...), custom_call_target="tpu_custom_call" | custom-call | flops 3758096384 | bytes 12582912 | tf_op jit(solution)/shard_map/multiply_0/pallas_call | solution.py:105
  74.0 2.7 %collective-permute-start.19 = (bf16[32,3584]{1,0:T(8,128)(2,1)S(1)}, bf16[32,3584]{1,0:T(8,128)(2,1)S(1)}, u32[]{:S(2)}, u32[]{:S(2)}) collective-permute-start(bf16[32,3584]{1,0:T(8,128)(2,1)S(1)} %slice.31), channel_id=1, source_target_pairs={{0,192},{64,0},{128,64},{192,128},{1,193},{65,1},{129,65},{193,129... | collective-permute-start | bytes 688136 | tf_op jit(solution)/shard_map/ppermute | solution.py:17
  76.7 3.6 %multiply_1.1.total_ref = f32[512,3584]{1,0:T(8,128)S(1)} custom-call(bf16[512,448]{1,0:T(8,128)(2,1)S(1)} %get-tuple-element.81.left_ref, bf16[64,3584]{1,0:T(8,128)(2,1)S(1)} %collective-permute-done.8.refs_0_, bf16[96,3584]{1,0:T(8,128)(2,1)S(1)} %collective-permute-done.10.refs_6_.refs_1_, ...), custom_call_target="tpu_custom_call", output_to_operand_aliasing={{}: (7, {})} | custom-call | flops 3288334336 | bytes 12582912 | tf_op jit(solution)/shard_map/multiply_1/pallas_call | solution.py:105
  80.3 2.6 %collective-permute-done.18.refs_0_ = bf16[32,3584]{1,0:T(8,128)(2,1)S(1)} collective-permute-done((bf16[32,3584]{1,0:T(8,128)(2,1)S(1)}, bf16[32,3584]{1,0:T(8,128)(2,1)S(1)}, u32[]{:S(2)}, u32[]{:S(2)}) %collective-permute-start.18) | collective-permute-done | bytes 229408 | tf_op jit(solution)/shard_map/ppermute | solution.py:17
  83.5 8.2 %collective-permute-start.20 = (bf16[256,1792]{1,0:T(8,128)(2,1)S(1)}, bf16[256,1792]{1,0:T(8,128)(2,1)S(1)}, u32[]{:S(2)}, u32[]{:S(2)}) collective-permute-start(bf16[256,1792]{1,0:T(8,128)(2,1)S(1)} %get-tuple-element.89), channel_id=1, source_target_pairs={{0,8},{8,0},{1,9},{9,1},{2,10},{10,2},{3,11},{11,3},{4,12},{12,4},... | collective-permute-start | bytes 2752520 | tf_op jit(solution)/shard_map/ppermute | solution.py:17
  92.3 1.5 %collective-permute-done.20.half_0 = bf16[256,1792]{1,0:T(8,128)(2,1)S(1)} collective-permute-done((bf16[256,1792]{1,0:T(8,128)(2,1)S(1)}, bf16[256,1792]{1,0:T(8,128)(2,1)S(1)}, u32[]{:S(2)}, u32[]{:S(2)}) %collective-permute-start.20) | collective-permute-done | bytes 917536 | tf_op jit(solution)/shard_map/ppermute | solution.py:17
  94.2 1.2 %put_keep.1 = (bf16[256,3584]{1,0:T(8,128)(2,1)}, bf16[256,3584]{1,0:T(8,128)(2,1)}) custom-call(s32[1]{0:T(128)} %bitcast.7.core_ref, bf16[256,1792]{1,0:T(8,128)(2,1)S(1)} %get-tuple-element.94.half_0, bf16[256,1792]{1,0:T(8,128)(2,1)S(1)} %get-tuple-element.95.half_1), custom_call_target="tpu_custom_call" | custom-call | bytes 4194304 | tf_op jit(solution)/shard_map/put_keep/pallas_call | solution.py:182
  96.3 1.2 %put_got.1 = (bf16[256,3584]{1,0:T(8,128)(2,1)}, bf16[256,3584]{1,0:T(8,128)(2,1)}) custom-call(s32[1]{0:T(128)} %bitcast.7.core_ref, bf16[256,1792]{1,0:T(8,128)(2,1)S(1)} %collective-permute-done.20.half_0, bf16[256,1792]{1,0:T(8,128)(2,1)S(1)} %collective-permute-done.21.half_1, ...), custom_call_target="tpu_custom_call", output_to_operand_aliasing={{0}: (3, {}), {1}: (4, {})} | custom-call | bytes 4194304 | tf_op jit(solution)/shard_map/put_got/pallas_call | solution.py:182
  (47 shorter events, 12.0 us)
Async XLA Ops:
  0.6 5.8 %collective-permute-start = (bf16[8,4,3584]{2,1,0:T(4,128)(2,1)}, bf16[8,4,3584]{2,1,0:T(4,128)(2,1)S(1)}, u32[]{:S(2)}, u32[]{:S(2)}) collective-permute-start(bf16[8,4,3584]{2,1,0:T(4,128)(2,1)} %param.8), channel_id=1, source_target_pairs={{0,8},{8,0},{1,9},{9,1},{2,10},{10,2},{3,11},{11,3},{4,12},{12,4},... | collective-permute-start | bytes 688136 | tf_op jit(solution)/shard_map/ppermute | solution.py:17
  4.0 2.4 %collective-permute-start.1 = (bf16[8,4,3584]{2,1,0:T(4,128)(2,1)}, bf16[8,4,3584]{2,1,0:T(4,128)(2,1)S(1)}, u32[]{:S(2)}, u32[]{:S(2)}) collective-permute-start(bf16[8,4,3584]{2,1,0:T(4,128)(2,1)} %param.9), channel_id=1, source_target_pairs={{0,8},{8,0},{1,9},{9,1},{2,10},{10,2},{3,11},{11,3},{4,12},{12,4},... | collective-permute-start | bytes 688136 | tf_op jit(solution)/shard_map/ppermute | solution.py:17
  6.4 4.5 %collective-permute-start.6 = (bf16[4,8192]{1,0:T(4,128)(2,1)S(1)}, bf16[4,8192]{1,0:T(4,128)(2,1)S(1)}, u32[]{:S(2)}, u32[]{:S(2)}) collective-permute-start(bf16[4,8192]{1,0:T(4,128)(2,1)S(1)} %get-tuple-element.58), channel_id=1, source_target_pairs={{0,8},{8,0},{1,9},{9,1},{2,10},{10,2},{3,11},{11,3},{4,12},{12,4},... | collective-permute-start | bytes 196616 | tf_op jit(solution)/shard_map/ppermute | solution.py:17
  8.1 14.0 %collective-permute-start.4 = (bf16[64,3584]{1,0:T(8,128)(2,1)S(1)}, bf16[64,3584]{1,0:T(8,128)(2,1)S(1)}, u32[]{:S(2)}, u32[]{:S(2)}) collective-permute-start(bf16[64,3584]{1,0:T(8,128)(2,1)S(1)} %maximum_bitcast_fusion.refs_0_), channel_id=1, source_target_pairs={{0,16},{16,32},{32,48},{48,0},{1,17},{17,33},{33,49},{49,1},{2,18}... | collective-permute-start | bytes 1376264 | tf_op jit(solution)/shard_map/ppermute | solution.py:17
  8.2 13.9 %collective-permute-start.3 = (bf16[64,3584]{1,0:T(8,128)(2,1)S(1)}, bf16[64,3584]{1,0:T(8,128)(2,1)S(1)}, u32[]{:S(2)}, u32[]{:S(2)}) collective-permute-start(bf16[64,3584]{1,0:T(8,128)(2,1)S(1)} %maximum_bitcast_fusion.refs_0_), channel_id=1, source_target_pairs={{0,192},{64,0},{128,64},{192,128},{1,193},{65,1},{129,65},{193,129... | collective-permute-start | bytes 1376264 | tf_op jit(solution)/shard_map/ppermute | solution.py:17
  10.9 12.7 %collective-permute-start.2 = (bf16[64,3584]{1,0:T(8,128)(2,1)S(1)}, bf16[64,3584]{1,0:T(8,128)(2,1)S(1)}, u32[]{:S(2)}, u32[]{:S(2)}) collective-permute-start(bf16[64,3584]{1,0:T(8,128)(2,1)S(1)} %maximum_bitcast_fusion.refs_0_), channel_id=1, source_target_pairs={{0,64},{64,128},{128,192},{192,0},{1,65},{65,129},{129,193},{193,1... | collective-permute-start | bytes 1376264 | tf_op jit(solution)/shard_map/ppermute | solution.py:17
  11.6 14.0 %all-to-all-start = ((bf16[16,8,512]{2,1,0:T(8,128)(2,1)}), bf16[16,8,512]{2,1,0:T(8,128)(2,1)S(1)}, u32[]{:S(2)}, u32[]{:S(2)}) async-start(bf16[16,8,512]{2,1,0:T(8,128)(2,1)} %bitcast.10), calls=%async_computation | async-start | bytes 262144 | tf_op jit(solution)/shard_map/all_to_all | solution.py:246
  25.7 19.1 %collective-permute-start.7 = (bf16[96,3584]{1,0:T(8,128)(2,1)S(1)}, bf16[96,3584]{1,0:T(8,128)(2,1)S(1)}, u32[]{:S(2)}, u32[]{:S(2)}) collective-permute-start(bf16[96,3584]{1,0:T(8,128)(2,1)S(1)} %get-tuple-element.61), channel_id=1, source_target_pairs={{0,192},{64,0},{128,64},{192,128},{1,193},{65,1},{129,65},{193,129... | collective-permute-start | bytes 2064392 | tf_op jit(solution)/shard_map/ppermute | solution.py:17
  26.5 18.2 %collective-permute-start.5 = (bf16[96,3584]{1,0:T(8,128)(2,1)S(1)}, bf16[96,3584]{1,0:T(8,128)(2,1)S(1)}, u32[]{:S(2)}, u32[]{:S(2)}) collective-permute-start(bf16[96,3584]{1,0:T(8,128)(2,1)S(1)} %get-tuple-element.103), channel_id=1, source_target_pairs={{0,64},{64,128},{128,192},{192,0},{1,65},{65,129},{129,193},{193,1... | collective-permute-start | bytes 2064392 | tf_op jit(solution)/shard_map/ppermute | solution.py:17
  27.1 17.6 %collective-permute-start.8 = (bf16[64,3584]{1,0:T(8,128)(2,1)S(1)}, bf16[64,3584]{1,0:T(8,128)(2,1)S(1)}, u32[]{:S(2)}, u32[]{:S(2)}) collective-permute-start(bf16[64,3584]{1,0:T(8,128)(2,1)S(1)} %collective-permute-done.4.refs_5_), channel_id=1, source_target_pairs={{0,16},{16,32},{32,48},{48,0},{1,17},{17,33},{33,49},{49,1},{2,18}... | collective-permute-start | bytes 1376264 | tf_op jit(solution)/shard_map/ppermute | solution.py:17
  27.7 17.0 %collective-permute-start.9 = (bf16[16,8,512]{2,1,0:T(8,128)(2,1)S(1)}, bf16[16,8,512]{2,1,0:T(8,128)(2,1)S(1)}, u32[]{:S(2)}, u32[]{:S(2)}) collective-permute-start(bf16[16,8,512]{2,1,0:T(8,128)(2,1)S(1)} %all-to-all-done), channel_id=1, source_target_pairs={{0,4},{4,0},{1,5},{5,1},{2,6},{6,2},{3,7},{7,3},{8,12},{12,8},{9,1... | collective-permute-start | bytes 393224 | tf_op jit(solution)/shard_map/ppermute | solution.py:17
  44.9 12.3 %collective-permute-start.11 = (bf16[96,3584]{1,0:T(8,128)(2,1)S(1)}, bf16[96,3584]{1,0:T(8,128)(2,1)S(1)}, u32[]{:S(2)}, u32[]{:S(2)}) collective-permute-start(bf16[96,3584]{1,0:T(8,128)(2,1)S(1)} %get-tuple-element.100), channel_id=1, source_target_pairs={{0,192},{64,0},{128,64},{192,128},{1,193},{65,1},{129,65},{193,129... | collective-permute-start | bytes 2064392 | tf_op jit(solution)/shard_map/ppermute | solution.py:17
  47.4 12.6 %collective-permute-start.10 = (bf16[96,3584]{1,0:T(8,128)(2,1)S(1)}, bf16[96,3584]{1,0:T(8,128)(2,1)S(1)}, u32[]{:S(2)}, u32[]{:S(2)}) collective-permute-start(bf16[96,3584]{1,0:T(8,128)(2,1)S(1)} %get-tuple-element.101), channel_id=1, source_target_pairs={{0,64},{64,128},{128,192},{192,0},{1,65},{65,129},{129,193},{193,1... | collective-permute-start | bytes 2064392 | tf_op jit(solution)/shard_map/ppermute | solution.py:17
  47.4 9.8 %collective-permute-start.12 = (bf16[64,3584]{1,0:T(8,128)(2,1)S(1)}, bf16[64,3584]{1,0:T(8,128)(2,1)S(1)}, u32[]{:S(2)}, u32[]{:S(2)}) collective-permute-start(bf16[64,3584]{1,0:T(8,128)(2,1)S(1)} %collective-permute-done.8.refs_0_), channel_id=1, source_target_pairs={{0,16},{16,32},{32,48},{48,0},{1,17},{17,33},{33,49},{49,1},{2,18}... | collective-permute-start | bytes 1376264 | tf_op jit(solution)/shard_map/ppermute | solution.py:17
  47.4 5.9 %collective-permute-start.14 = (bf16[2,16,8,512]{3,2,1,0:T(8,128)(2,1)S(1)}, bf16[2,16,8,512]{3,2,1,0:T(8,128)(2,1)S(1)}, u32[]{:S(2)}, u32[]{:S(2)}) collective-permute-start(bf16[2,16,8,512]{3,2,1,0:T(8,128)(2,1)S(1)} %pad_maximum_fusion.6.refs_0_), channel_id=1, source_target_pairs={{0,3},{1,0},{2,1},{3,2},{4,7},{5,4},{6,5},{7,6},{8,11},{9,8},{10,9... | collective-permute-start | bytes 786440 | tf_op jit(solution)/shard_map/ppermute | solution.py:17
  50.0 6.4 %collective-permute-start.13 = (bf16[2,16,8,512]{3,2,1,0:T(8,128)(2,1)S(1)}, bf16[2,16,8,512]{3,2,1,0:T(8,128)(2,1)S(1)}, u32[]{:S(2)}, u32[]{:S(2)}) collective-permute-start(bf16[2,16,8,512]{3,2,1,0:T(8,128)(2,1)S(1)} %pad_maximum_fusion.6.refs_0_), channel_id=1, source_target_pairs={{0,1},{1,2},{2,3},{3,0},{4,5},{5,6},{6,7},{7,4},{8,9},{9,10},{10,1... | collective-permute-start | bytes 786440 | tf_op jit(solution)/shard_map/ppermute | solution.py:17
  60.1 13.0 %collective-permute-start.16 = (bf16[96,3584]{1,0:T(8,128)(2,1)S(1)}, bf16[96,3584]{1,0:T(8,128)(2,1)S(1)}, u32[]{:S(2)}, u32[]{:S(2)}) collective-permute-start(bf16[96,3584]{1,0:T(8,128)(2,1)S(1)} %get-tuple-element.98), channel_id=1, source_target_pairs={{0,192},{64,0},{128,64},{192,128},{1,193},{65,1},{129,65},{193,129... | collective-permute-start | bytes 2064392 | tf_op jit(solution)/shard_map/ppermute | solution.py:17
  60.7 13.2 %collective-permute-start.15 = (bf16[96,3584]{1,0:T(8,128)(2,1)S(1)}, bf16[96,3584]{1,0:T(8,128)(2,1)S(1)}, u32[]{:S(2)}, u32[]{:S(2)}) collective-permute-start(bf16[96,3584]{1,0:T(8,128)(2,1)S(1)} %get-tuple-element.99), channel_id=1, source_target_pairs={{0,64},{64,128},{128,192},{192,0},{1,65},{65,129},{129,193},{193,1... | collective-permute-start | bytes 2064392 | tf_op jit(solution)/shard_map/ppermute | solution.py:17
  61.9 6.7 %collective-permute-start.17 = (bf16[2,16,8,512]{3,2,1,0:T(8,128)(2,1)S(1)}, bf16[2,16,8,512]{3,2,1,0:T(8,128)(2,1)S(1)}, u32[]{:S(2)}, u32[]{:S(2)}) collective-permute-start(bf16[2,16,8,512]{3,2,1,0:T(8,128)(2,1)S(1)} %pad_maximum_fusion.6.refs_0_), channel_id=1, source_target_pairs={{0,2},{1,3},{2,0},{3,1},{4,6},{5,7},{6,4},{7,5},{8,10},{9,11},{10,... | collective-permute-start | bytes 786440 | tf_op jit(solution)/shard_map/ppermute | solution.py:17
  73.9 9.0 %collective-permute-start.18 = (bf16[32,3584]{1,0:T(8,128)(2,1)S(1)}, bf16[32,3584]{1,0:T(8,128)(2,1)S(1)}, u32[]{:S(2)}, u32[]{:S(2)}) collective-permute-start(bf16[32,3584]{1,0:T(8,128)(2,1)S(1)} %slice.30), channel_id=1, source_target_pairs={{0,64},{64,128},{128,192},{192,0},{1,65},{65,129},{129,193},{193,1... | collective-permute-start | bytes 688136 | tf_op jit(solution)/shard_map/ppermute | solution.py:17
  74.0 8.9 %collective-permute-start.19 = (bf16[32,3584]{1,0:T(8,128)(2,1)S(1)}, bf16[32,3584]{1,0:T(8,128)(2,1)S(1)}, u32[]{:S(2)}, u32[]{:S(2)}) collective-permute-start(bf16[32,3584]{1,0:T(8,128)(2,1)S(1)} %slice.31), channel_id=1, source_target_pairs={{0,192},{64,0},{128,64},{192,128},{1,193},{65,1},{129,65},{193,129... | collective-permute-start | bytes 688136 | tf_op jit(solution)/shard_map/ppermute | solution.py:17
  83.5 10.3 %collective-permute-start.20 = (bf16[256,1792]{1,0:T(8,128)(2,1)S(1)}, bf16[256,1792]{1,0:T(8,128)(2,1)S(1)}, u32[]{:S(2)}, u32[]{:S(2)}) collective-permute-start(bf16[256,1792]{1,0:T(8,128)(2,1)S(1)} %get-tuple-element.89), channel_id=1, source_target_pairs={{0,8},{8,0},{1,9},{9,1},{2,10},{10,2},{3,11},{11,3},{4,12},{12,4},... | collective-permute-start | bytes 2752520 | tf_op jit(solution)/shard_map/ppermute | solution.py:17
  93.8 2.5 %collective-permute-start.21 = (bf16[256,1792]{1,0:T(8,128)(2,1)S(1)}, bf16[256,1792]{1,0:T(8,128)(2,1)S(1)}, u32[]{:S(2)}, u32[]{:S(2)}) collective-permute-start(bf16[256,1792]{1,0:T(8,128)(2,1)S(1)} %get-tuple-element.93), channel_id=1, source_target_pairs={{0,8},{8,0},{1,9},{9,1},{2,10},{10,2},{3,11},{11,3},{4,12},{12,4},... | collective-permute-start | bytes 2752520 | tf_op jit(solution)/shard_map/ppermute | solution.py:17

commit v4 on v3

--- a/solution.py
+++ b/solution.py
@@ -9,7 +9,12 @@
 from jax.sharding import Mesh, PartitionSpec as P
 
 Y, Z, C, H, X = 4, 4, 2, 2, 4
-FIRST = 0
+ORDER = (
+    ((0, 0), (0, 1), (0, 3), (0, 2)),
+    ((1, 0), (1, 1), (1, 3), (1, 2)),
+    ((2, 0), (2, 1), (2, 3), (3, 0)),
+    ((2, 2), (3, 1), (3, 3), (3, 2)),
+)
 
 
 def shift(x, axis, by):
@@ -18,26 +23,22 @@
 
 
 def left_kernel(place_ref, *refs):
-    *left_refs, first_ref, second_ref, last_ref, held = refs
+    *left_refs, out_ref, last_ref, held = refs
     x, y, z, h = place_ref[0], place_ref[1], place_ref[2], place_ref[3]
     for r, left_ref in enumerate(left_refs):
         held[r] = left_ref[...].astype(held.dtype)
-    size = H * X * held.shape[3]
-    for d in range(Z):
+    for k, order in enumerate(ORDER):
         parts = []
-        for from_y in (0, 1, Y - 1, 2):
+        for d, from_y in order:
             chip = lax.rem(y + Y - from_y, Y) * Z + lax.rem(z + Z - d, Z)
             for at_h in range(H):
                 for at_x in range(X):
                     parts.append(held[lax.rem(x + X - at_x, X), lax.rem(h + at_h, H), chip])
-        block = jnp.concatenate(parts, axis=0).T.astype(first_ref.dtype)
-        if d < Z // 2:
-            first_ref[:, d * Y * size : (d + 1) * Y * size] = block
-        elif d < Z - 1:
-            second_ref[:, (d - Z // 2) * Y * size : (d - Z // 2 + 1) * Y * size] = block
+        block = jnp.concatenate(parts, axis=0).T.astype(out_ref.dtype)
+        if k < len(ORDER) - 1:
+            out_ref[:, k * block.shape[1] : (k + 1) * block.shape[1]] = block
         else:
-            second_ref[:, (d - Z // 2) * Y * size :] = block[:, : (Y - 1) * size]
-            last_ref[...] = block[:, (Y - 1) * size :]
+            last_ref[...] = block
 
 
 def arrange_left(place, lefts):
@@ -47,12 +48,11 @@
     return pl.pallas_call(
         left_kernel,
         out_shape=(
-            jax.ShapeDtypeStruct((rows, Y * Z * size // 2), lefts[0].dtype),
-            jax.ShapeDtypeStruct((rows, (Y * Z // 2 - 1) * size), lefts[0].dtype),
-            jax.ShapeDtypeStruct((rows, size), lefts[0].dtype),
+            jax.ShapeDtypeStruct((rows, (Z - 1) * Y * size), lefts[0].dtype),
+            jax.ShapeDtypeStruct((rows, Y * size), lefts[0].dtype),
         ),
         in_specs=[pl.BlockSpec(memory_space=pltpu.SMEM)] + [vmem] * X,
-        out_specs=(vmem, vmem, vmem),
+        out_specs=(vmem, vmem),
         scratch_shapes=[pltpu.VMEM((X,) + lefts[0].shape, jnp.float32)],
         compiler_params=pltpu.CompilerParams(vmem_limit_bytes=8 << 20),
         cost_estimate=pl.CostEstimate(flops=0, bytes_accessed=6 << 20, transcendentals=0),
@@ -120,7 +120,7 @@
     )(left, *arrays, *totals)
 
 
-def last_kernel(cut, width, core_ref, left_ref, total_ref, *refs):
+def last_kernel(ranges, cut, width, core_ref, left_ref, total_ref, *refs):
     *right_refs, keep_ref, send_ref = refs
     rows, columns = keep_ref.shape
     mine = pl.multiple_of(core_ref[0] * rows, rows)
@@ -129,7 +129,7 @@
     def step(i, _):
         at = pl.ds(pl.multiple_of(i * width, width), width)
         from_at = pl.ds(pl.multiple_of(cut + i * width, width), width)
-        right = jnp.concatenate([ref[:, from_at] for ref in right_refs], axis=0)
+        right = jnp.concatenate([right_refs[k][pl.ds(row, count), from_at] for k, row, count in ranges], axis=0)
         for out_ref, row in ((send_ref, other), (keep_ref, mine)):
             total = total_ref[pl.ds(row, rows), from_at]
             total += jnp.dot(left_ref[pl.ds(row, rows)], right, preferred_element_type=jnp.float32)
@@ -139,32 +139,28 @@
     lax.fori_loop(0, columns // width, step, None, unroll=True)
 
 
-def multiply_last(core, left, total, last, cut, end, name):
+def multiply_last(core, left, total, arrays, ranges, cut, end, name):
     rows, columns = total.shape[0] // 2, end - cut
     shape = jax.ShapeDtypeStruct((rows, columns), left.dtype)
     vmem = pl.BlockSpec(memory_space=pltpu.VMEM)
     return pl.pallas_call(
-        functools.partial(last_kernel, cut, 256),
+        functools.partial(last_kernel, ranges, cut, 256),
         out_shape=(shape, shape),
-        in_specs=[pl.BlockSpec(memory_space=pltpu.SMEM)] + [vmem] * (2 + len(last)),
+        in_specs=[pl.BlockSpec(memory_space=pltpu.SMEM)] + [vmem] * (2 + len(arrays)),
         out_specs=(vmem, vmem),
         compiler_params=pltpu.CompilerParams(vmem_limit_bytes=14 << 20),
         cost_estimate=pl.CostEstimate(flops=1024 * rows * columns, bytes_accessed=6 << 20, transcendentals=0),
         name=name,
-    )(core, left, total, *last)
-
-
-def put_kernel(got, core_ref, half_0, half_1, *refs):
-    gate_ref, up_ref, sems = refs[-3:]
-
-    def put(out):
-        copies = []
-        for k, (half, at) in enumerate(((half_0, 0), (half_1, half_0.shape[1]))):
-            copies.append(pltpu.make_async_copy(half, out.at[:, pl.ds(at, half.shape[1])], sems.at[k]))
-        for copy in copies:
-            copy.start()
-        for copy in copies:
-            copy.wait()
+    )(core, left, total, *arrays)
+
+
+def put_kernel(got, at, core_ref, part_ref, *refs):
+    gate_ref, up_ref, sem = refs[-3:]
+
+    def put(out_ref):
+        copy = pltpu.make_async_copy(part_ref, out_ref.at[:, pl.ds(at, part_ref.shape[1])], sem)
+        copy.start()
+        copy.wait()
 
     @pl.when(core_ref[0] == got)
     def _():
@@ -175,21 +171,20 @@
         put(up_ref)
 
 
-def put(core, half_0, half_1, outs, got):
-    rows, columns = half_0.shape[0], half_0.shape[1] + half_1.shape[1]
-    shape = jax.ShapeDtypeStruct((rows, columns), half_0.dtype)
+def put(core, part, outs, got, at, columns):
+    shape = jax.ShapeDtypeStruct((part.shape[0], columns), part.dtype)
     anywhere = pl.BlockSpec(memory_space=pl.ANY)
     return pl.pallas_call(
-        functools.partial(put_kernel, got),
+        functools.partial(put_kernel, got, at),
         out_shape=(shape, shape),
-        in_specs=[pl.BlockSpec(memory_space=pltpu.SMEM)] + [anywhere] * (2 + len(outs)),
+        in_specs=[pl.BlockSpec(memory_space=pltpu.SMEM)] + [anywhere] * (1 + len(outs)),
         out_specs=(anywhere, anywhere),
-        scratch_shapes=[pltpu.SemaphoreType.DMA((2,))],
-        input_output_aliases={3 + k: k for k in range(len(outs))},
+        scratch_shapes=[pltpu.SemaphoreType.DMA],
+        input_output_aliases={2 + k: k for k in range(len(outs))},
         compiler_params=pltpu.CompilerParams(vmem_limit_bytes=4 << 20),
         cost_estimate=pl.CostEstimate(flops=0, bytes_accessed=4 << 20, transcendentals=0),
-        name="put_got" if got else "put_keep",
-    )(core, half_0, half_1, *outs)
+        name=f"put_{got}_{at}",
+    )(core, part, *outs)
 
 
 def weigh(left, coef):
@@ -264,26 +259,30 @@
     up2, down2, z3, left, left_1, left_3 = event(up2, down2, z3, left, left_1, left_3)
 
     up3, down3 = both(z3, up2, down2)
-    left_0, left_1, left_2 = arrange_left(place, [left, left_1, shift(left, "x", 2), left_3])
+    far3 = shift(jnp.concatenate([up1[n:], down1[n:]], axis=0), "z", 3)
+    left, left_last = arrange_left(place, [left, left_1, shift(left, "x", 2), left_3])
 
     def slot(block, up, down, up_next, down_next):
         return [(block, 0, n), (up, 0, n), (down, 0, n), (up_next, n, half), (down_next, n, half)]
 
-    total = multiply_part(left_0, slot(own, up0, down0, up1, down1) + slot(z1, up1, down1, up2, down2), None, "multiply_0")
-    up3, down3, total = event(up3, down3, total)
-
-    up4, down4 = shift(up3[:half], "y", 1), shift(down3[half:n], "y", -1)
-    pieces = slot(z2, up2, down2, up3, down3) + [(z3, 0, n), (up3, 0, n), (down3, 0, n)]
-    total = multiply_part(left_1, pieces, total, "multiply_1")
-    up4, down4, total = event(up4, down4, total)
+    pieces = slot(own, up0, down0, up1, down1) + slot(z1, up1, down1, up2, down2)
+    pieces += [(part, 0, n) for part in (z2, up2, down2, z3)]
+    total = multiply_part(left, pieces, None, "multiply_0")
+    up3, down3, far3, total = event(up3, down3, far3, total)
+
     cut = columns // 2
-    keep_0, send_0 = multiply_last(token, left_2, total, [up4, down4], 0, cut, "multiply_2")
+    lasts = [up3, down3, far3]
+    ranges = [(0, n, half), (1, n, half), (0, 0, n), (1, 0, n), (2, 0, n)]
+    keep_0, send_0 = multiply_last(token, left_last, total, lasts, ranges, 0, cut, "multiply_1")
     got_0 = shift(send_0, "c", 1)
-    keep_1, send_1 = multiply_last(token, left_2, total, [up4, down4], cut, columns, "multiply_3")
-    got_0, send_1 = event(got_0, send_1)
+    keep_1, send_1 = multiply_last(token, left_last, total, lasts, ranges, cut, columns, "multiply_2")
+    outs = put(token, keep_0, [], 0, 0, columns)
+    got_0, send_1, *outs = event(got_0, send_1, *outs)
     got_1 = shift(send_1, "c", 1)
-    outs = put(token, keep_0, keep_1, [], 0)
-    return tuple(put(token, got_0, got_1, outs, 1))
+    outs = put(token, keep_1, outs, 0, cut, columns)
+    outs = put(token, got_0, outs, 1, 0, columns)
+    got_1, *outs = event(got_1, *outs)
+    return tuple(put(token, got_1, outs, 1, cut, columns))
 
 
 def solution(mesh):

time: 97.9 us -> 90.1 us (0.920)
  waiting for transfers between devices: 38.2 us -> 29.3 us
  starting transfers between devices: 41.8 us -> 43.8 us
  Pallas kernels: 11.9 us -> 10.9 us
    ppermute x22 -> x21, waiting for transfers between devices: 36.3 us -> 27.4 us  [shift(): return lax.ppermute(x, axis, [(i, (i + by) % n) for i in range(n)])]
    pallas_call x2 -> x1, Pallas kernels: 7.05 us -> 4.9 us  [multiply_part(): pl.pallas_call(functools.partial(part_kernel, ranges, 256), out_shape=jax...]
    ppermute x22 -> x21, starting transfers between devices: 35.1 us -> 37.1 us  [shift(): return lax.ppermute(x, axis, [(i, (i + by) % n) for i in range(n)])]
    pallas_call x5 -> x7, Pallas kernels: 4.84 us -> 6.03 us  [the longest x4 3.72 us: put(): pl.pallas_call(functools.partial(put_kernel, got, at), out_shape=(shape,...]
  transfers between devices with their start and end apart: 23 -> 22, of which waited for: 13 -> 10; matrix products, arithmetic and copies ran while one was open for 3% -> 4% of each run, Pallas kernels for 10% -> 10%
where the time goes in v4:
time: 90.1 us; the launch traced here: 89.9 us
  starting transfers between devices  43.8 us (49%)
  waiting for transfers between devices  29.3 us (33%)
  Pallas kernels  10.9 us (12%)
  other arithmetic  3.36 us (4%)
  between operations  2.29 us (3%)
    ppermute x21, starting transfers between devices, shift(): return lax.ppermute(x, axis, [(i, (i + by) % n) for i in range(n)])  37.1 us
    ppermute x21, waiting for transfers between devices, shift(): return lax.ppermute(x, axis, [(i, (i + by) % n) for i in range(n)])  27.4 us
    all_to_all x1, starting transfers between devices, shards(): lax.all_to_all(left, ('y', 'z'), split_axis=0, concat_axis=0, tiled=True)  6.76 us
    pallas_call x1, Pallas kernels, multiply_part(): pl.pallas_call(functools.partial(part_kernel, ranges, 256), out_shape=jax...  4.9 us
    pallas_call x4, Pallas kernels, put(): pl.pallas_call(functools.partial(put_kernel, got, at), out_shape=(shape,...  3.72 us
    all_to_all x1, waiting for transfers between devices, shards(): lax.all_to_all(left, ('y', 'z'), split_axis=0, concat_axis=0, tiled=True)  1.92 us
  transfers between devices with their start and end apart: 22, of which 10 were waited for; matrix products, arithmetic and copies ran while one was open for 4% of the time, Pallas kernels for 10%

profile of v4, /device:TPU:1, one launch (start us, length us, event | category | flops | bytes accessed | tf_op | source)
XLA Modules:
  0.0 89.9 jit_solution(14937950943171059938)
XLA Ops:
  0.6 3.3 %collective-permute-start = (bf16[8,4,3584]{2,1,0:T(4,128)(2,1)}, bf16[8,4,3584]{2,1,0:T(4,128)(2,1)S(1)}, u32[]{:S(2)}, u32[]{:S(2)}) collective-permute-start(bf16[8,4,3584]{2,1,0:T(4,128)(2,1)} %param.8), channel_id=1, source_target_pairs={{0,8},{8,0},{1,9},{9,1},{2,10},{10,2},{3,11},{11,3},{4,12},{12,4},... | collective-permute-start | bytes 688136 | tf_op jit(solution)/shard_map/ppermute | solution.py:22
  5.4 0.9 %select_bitcast_fusion = (bf16[4,8192]{1,0:T(4,128)(2,1)S(1)}, bf16[4,8192]{1,0:T(4,128)(2,1)S(1)}) fusion(pred[]{:T(512)S(6)} %eq.3, bf16[1,4,8192]{2,1,0:T(4,128)(2,1)} %param.6, f32[]{:T(128)} %bitcast, bf16[1,4,8192]{2,1,0:T(4,128)(2,1)} %param.7), kind=kLoop, calls=%fused_computation.14 | loop fusion | flops 262144 | bytes 262149 | tf_op jit(solution)/shard_map/jit(_where)/select_n | solution.py:211
  6.9 1.0 %broadcast_select_fusion = (bf16[4,8,3584]{2,1,0:T(8,128)(2,1)S(1)}, bf16[4,8,3584]{2,1,0:T(8,128)(2,1)S(1)}) fusion(bf16[4,8,3584]{2,1,0:T(8,128)(2,1)S(1)} %bitcast.28, bf16[4,8,3584]{2,1,0:T(8,128)(2,1)} %bitcast.27, pred[]{:T(512)S(6)} %eq.3, bf16[4,8,3584]{2,1,0:T(8,128)(2,1)} %bitcast.26, bf16[4,8,3584]{2,1,0:T(8,128)(2,1)S(1)} %bitcast.29), kind=kLoop, calls=%fused_computation.9 | loop fusion | flops 229376 | bytes 1376257 | tf_op jit(solution)/shard_map/jit(_where)/select_n | solution.py:213
  8.2 2.6 %collective-permute-start.3 = (bf16[64,3584]{1,0:T(8,128)(2,1)S(1)}, bf16[64,3584]{1,0:T(8,128)(2,1)S(1)}, u32[]{:S(2)}, u32[]{:S(2)}) collective-permute-start(bf16[64,3584]{1,0:T(8,128)(2,1)S(1)} %maximum_bitcast_fusion.refs_0_), channel_id=1, source_target_pairs={{0,192},{64,0},{128,64},{192,128},{1,193},{65,1},{129,65},{193,129... | collective-permute-start | bytes 1376264 | tf_op jit(solution)/shard_map/ppermute | solution.py:22
  11.6 6.8 %all-to-all-start = ((bf16[16,8,512]{2,1,0:T(8,128)(2,1)}), bf16[16,8,512]{2,1,0:T(8,128)(2,1)S(1)}, u32[]{:S(2)}, u32[]{:S(2)}) async-start(bf16[16,8,512]{2,1,0:T(8,128)(2,1)} %bitcast.10), calls=%async_computation | async-start | bytes 262144 | tf_op jit(solution)/shard_map/all_to_all | solution.py:241
  18.4 3.7 %collective-permute-done.4.refs_5_ = bf16[64,3584]{1,0:T(8,128)(2,1)S(1)} collective-permute-done((bf16[64,3584]{1,0:T(8,128)(2,1)S(1)}, bf16[64,3584]{1,0:T(8,128)(2,1)S(1)}, u32[]{:S(2)}, u32[]{:S(2)}) %collective-permute-start.4) | collective-permute-done | bytes 458784 | tf_op jit(solution)/shard_map/ppermute | solution.py:22
  22.1 1.5 %collective-permute-done.2.refs_1_ = bf16[64,3584]{1,0:T(8,128)(2,1)S(1)} collective-permute-done((bf16[64,3584]{1,0:T(8,128)(2,1)S(1)}, bf16[64,3584]{1,0:T(8,128)(2,1)S(1)}, u32[]{:S(2)}, u32[]{:S(2)}) %collective-permute-start.2) | collective-permute-done | bytes 458784 | tf_op jit(solution)/shard_map/ppermute | solution.py:22
  23.7 1.9 %all-to-all-done = bf16[16,8,512]{2,1,0:T(8,128)(2,1)S(1)} async-done(((bf16[16,8,512]{2,1,0:T(8,128)(2,1)}), bf16[16,8,512]{2,1,0:T(8,128)(2,1)S(1)}, u32[]{:S(2)}, u32[]{:S(2)}) %all-to-all-start) | async-done | bytes 131104 | tf_op jit(solution)/shard_map/all_to_all | solution.py:241
  27.7 5.5 %collective-permute-start.9 = (bf16[16,8,512]{2,1,0:T(8,128)(2,1)S(1)}, bf16[16,8,512]{2,1,0:T(8,128)(2,1)S(1)}, u32[]{:S(2)}, u32[]{:S(2)}) collective-permute-start(bf16[16,8,512]{2,1,0:T(8,128)(2,1)S(1)} %all-to-all-done), channel_id=1, source_target_pairs={{0,4},{4,0},{1,5},{5,1},{2,6},{6,2},{3,7},{7,3},{8,12},{12,8},{9,1... | collective-permute-start | bytes 393224 | tf_op jit(solution)/shard_map/ppermute | solution.py:22
  33.3 11.4 %collective-permute-done.9 = bf16[16,8,512]{2,1,0:T(8,128)(2,1)S(1)} collective-permute-done((bf16[16,8,512]{2,1,0:T(8,128)(2,1)S(1)}, bf16[16,8,512]{2,1,0:T(8,128)(2,1)S(1)}, u32[]{:S(2)}, u32[]{:S(2)}) %collective-permute-start.9) | collective-permute-done | bytes 131104 | tf_op jit(solution)/shard_map/ppermute | solution.py:22
  44.9 2.5 %collective-permute-start.11 = (bf16[96,3584]{1,0:T(8,128)(2,1)S(1)}, bf16[96,3584]{1,0:T(8,128)(2,1)S(1)}, u32[]{:S(2)}, u32[]{:S(2)}) collective-permute-start(bf16[96,3584]{1,0:T(8,128)(2,1)S(1)} %get-tuple-element.116), channel_id=1, source_target_pairs={{0,192},{64,0},{128,64},{192,128},{1,193},{65,1},{129,65},{193,129... | collective-permute-start | bytes 2064392 | tf_op jit(solution)/shard_map/ppermute | solution.py:22
  47.4 2.6 %collective-permute-start.14 = (bf16[2,16,8,512]{3,2,1,0:T(8,128)(2,1)S(1)}, bf16[2,16,8,512]{3,2,1,0:T(8,128)(2,1)S(1)}, u32[]{:S(2)}, u32[]{:S(2)}) collective-permute-start(bf16[2,16,8,512]{3,2,1,0:T(8,128)(2,1)S(1)} %pad_maximum_fusion.7.refs_0_), channel_id=1, source_target_pairs={{0,3},{1,0},{2,1},{3,2},{4,7},{5,4},{6,5},{7,6},{8,11},{9,8},{10,9... | collective-permute-start | bytes 786440 | tf_op jit(solution)/shard_map/ppermute | solution.py:22
  50.0 3.3 %collective-permute-done.14.refs_3_ = bf16[2,16,8,512]{3,2,1,0:T(8,128)(2,1)S(1)} collective-permute-done((bf16[2,16,8,512]{3,2,1,0:T(8,128)(2,1)S(1)}, bf16[2,16,8,512]{3,2,1,0:T(8,128)(2,1)S(1)}, u32[]{:S(2)}, u32[]{:S(2)}) %collective-permute-start.14) | collective-permute-done | bytes 262176 | tf_op jit(solution)/shard_map/ppermute | solution.py:22
  53.3 3.1 %collective-permute-done.13.refs_1_ = bf16[2,16,8,512]{3,2,1,0:T(8,128)(2,1)S(1)} collective-permute-done((bf16[2,16,8,512]{3,2,1,0:T(8,128)(2,1)S(1)}, bf16[2,16,8,512]{3,2,1,0:T(8,128)(2,1)S(1)}, u32[]{:S(2)}, u32[]{:S(2)}) %collective-permute-start.13) | collective-permute-done | bytes 262176 | tf_op jit(solution)/shard_map/ppermute | solution.py:22
  57.2 2.8 %collective-permute-done.10.refs_6_ = bf16[96,3584]{1,0:T(8,128)(2,1)S(1)} collective-permute-done((bf16[96,3584]{1,0:T(8,128)(2,1)S(1)}, bf16[96,3584]{1,0:T(8,128)(2,1)S(1)}, u32[]{:S(2)}, u32[]{:S(2)}) %collective-permute-start.10) | collective-permute-done | bytes 688160 | tf_op jit(solution)/shard_map/ppermute | solution.py:22
  60.1 3.0 %collective-permute-start.18 = (bf16[2,16,8,512]{3,2,1,0:T(8,128)(2,1)S(1)}, bf16[2,16,8,512]{3,2,1,0:T(8,128)(2,1)S(1)}, u32[]{:S(2)}, u32[]{:S(2)}) collective-permute-start(bf16[2,16,8,512]{3,2,1,0:T(8,128)(2,1)S(1)} %pad_maximum_fusion.7.refs_0_), channel_id=1, source_target_pairs={{0,2},{1,3},{2,0},{3,1},{4,6},{5,7},{6,4},{7,5},{8,10},{9,11},{10,... | collective-permute-start | bytes 786440 | tf_op jit(solution)/shard_map/ppermute | solution.py:22
  63.5 1.2 %collective-permute-start.15 = (bf16[96,3584]{1,0:T(8,128)(2,1)S(1)}, bf16[96,3584]{1,0:T(8,128)(2,1)S(1)}, u32[]{:S(2)}, u32[]{:S(2)}) collective-permute-start(bf16[96,3584]{1,0:T(8,128)(2,1)S(1)} %get-tuple-element.115), channel_id=1, source_target_pairs={{0,64},{64,128},{128,192},{192,0},{1,65},{65,129},{129,193},{193,1... | collective-permute-start | bytes 2064392 | tf_op jit(solution)/shard_map/ppermute | solution.py:22
  64.8 5.2 %collective-permute-start.17 = (bf16[64,3584]{1,0:T(8,128)(2,1)S(1)}, bf16[64,3584]{1,0:T(8,128)(2,1)S(1)}, u32[]{:S(2)}, u32[]{:S(2)}) collective-permute-start(bf16[64,3584]{1,0:T(8,128)(2,1)S(1)} %pad_maximum_fusion.6), channel_id=1, source_target_pairs={{0,48},{16,0},{32,16},{48,32},{1,49},{17,1},{33,17},{49,33},{2,50}... | collective-permute-start | bytes 1376264 | tf_op jit(solution)/shard_map/ppermute | solution.py:22
  70.0 1.0 %arrange_left.1 = (bf16[512,768]{1,0:T(8,128)(2,1)S(1)}, bf16[512,256]{1,0:T(8,128)(2,1)S(1)}) custom-call(s32[4]{0:T(128)S(1)} %pad_add_fusion.place_ref, bf16[2,16,8,512]{3,2,1,0:T(8,128)(2,1)S(1)} %pad_maximum_fusion.7.refs_0_, bf16[2,16,8,512]{3,2,1,0:T(8,128)(2,1)S(1)} %collective-permute-done.13.refs_1_, ...), custom_call_target="tpu_custom_call" | custom-call | bytes 6291456 | tf_op jit(solution)/shard_map/arrange_left/pallas_call | solution.py:48
  71.0 4.9 %multiply_0.1.total_ref = f32[512,3584]{1,0:T(8,128)S(1)} custom-call(bf16[512,768]{1,0:T(8,128)(2,1)S(1)} %get-tuple-element.83.left_ref, bf16[64,3584]{1,0:T(8,128)(2,1)S(1)} %maximum_bitcast_fusion.refs_0_, bf16[64,3584]{1,0:T(8,128)(2,1)S(1)} %collective-permute-done.2.refs_1_, bf16[64,3584]{1,0:T(8,128)(2,1)S(1)} %collective-permute-done.3.refs_2_, ...), custom_call_target="tpu_custom_call" | custom-call | flops 5637144576 | bytes 12582912 | tf_op jit(solution)/shard_map/multiply_0/pallas_call | solution.py:105
  76.6 7.6 %collective-permute-start.19 = (bf16[256,1792]{1,0:T(8,128)(2,1)S(1)}, bf16[256,1792]{1,0:T(8,128)(2,1)S(1)}, u32[]{:S(2)}, u32[]{:S(2)}) collective-permute-start(bf16[256,1792]{1,0:T(8,128)(2,1)S(1)} %get-tuple-element.91), channel_id=1, source_target_pairs={{0,8},{8,0},{1,9},{9,1},{2,10},{10,2},{3,11},{11,3},{4,12},{12,4},... | collective-permute-start | bytes 2752520 | tf_op jit(solution)/shard_map/ppermute | solution.py:22
  84.2 0.9 %put_0_0.1 = (bf16[256,3584]{1,0:T(8,128)(2,1)}, bf16[256,3584]{1,0:T(8,128)(2,1)}) custom-call(s32[1]{0:T(128)} %bitcast.7.core_ref, bf16[256,1792]{1,0:T(8,128)(2,1)S(1)} %get-tuple-element.93.part_ref), custom_call_target="tpu_custom_call" | custom-call | bytes 4194304 | tf_op jit(solution)/shard_map/put_0_0/pallas_call | solution.py:177
  87.6 0.9 %put_1_0.1 = (bf16[256,3584]{1,0:T(8,128)(2,1)}, bf16[256,3584]{1,0:T(8,128)(2,1)}) custom-call(s32[1]{0:T(128)} %bitcast.7.core_ref, bf16[256,1792]{1,0:T(8,128)(2,1)S(1)} %collective-permute-done.19.part_ref, bf16[256,3584]{1,0:T(8,128)(2,1)} %get-tuple-element.102.refs_0_, ...), custom_call_target="tpu_custom_call", output_to_operand_aliasing={{0}: (2, {}), {1}: (3, {})} | custom-call | bytes 4194304 | tf_op jit(solution)/shard_map/put_1_0/pallas_call | solution.py:177
  88.8 0.9 %put_1_1792.1 = (bf16[256,3584]{1,0:T(8,128)(2,1)}, bf16[256,3584]{1,0:T(8,128)(2,1)}) custom-call(s32[1]{0:T(128)} %bitcast.7.core_ref, bf16[256,1792]{1,0:T(8,128)(2,1)S(1)} %collective-permute-done.20.part_ref, bf16[256,3584]{1,0:T(8,128)(2,1)} %get-tuple-element.108.refs_0_, ...), custom_call_target="tpu_custom_call", output_to_operand_aliasing={{0}: (2, {}), {1}: (3, {})} | custom-call | bytes 4194304 | tf_op jit(solution)/shard_map/put_1_1792/pallas_call | solution.py:177
  (45 shorter events, 8.8 us)
Async XLA Ops:
  0.6 5.8 %collective-permute-start = (bf16[8,4,3584]{2,1,0:T(4,128)(2,1)}, bf16[8,4,3584]{2,1,0:T(4,128)(2,1)S(1)}, u32[]{:S(2)}, u32[]{:S(2)}) collective-permute-start(bf16[8,4,3584]{2,1,0:T(4,128)(2,1)} %param.8), channel_id=1, source_target_pairs={{0,8},{8,0},{1,9},{9,1},{2,10},{10,2},{3,11},{11,3},{4,12},{12,4},... | collective-permute-start | bytes 688136 | tf_op jit(solution)/shard_map/ppermute | solution.py:22
  4.0 2.4 %collective-permute-start.1 = (bf16[8,4,3584]{2,1,0:T(4,128)(2,1)}, bf16[8,4,3584]{2,1,0:T(4,128)(2,1)S(1)}, u32[]{:S(2)}, u32[]{:S(2)}) collective-permute-start(bf16[8,4,3584]{2,1,0:T(4,128)(2,1)} %param.9), channel_id=1, source_target_pairs={{0,8},{8,0},{1,9},{9,1},{2,10},{10,2},{3,11},{11,3},{4,12},{12,4},... | collective-permute-start | bytes 688136 | tf_op jit(solution)/shard_map/ppermute | solution.py:22
  6.4 4.5 %collective-permute-start.6 = (bf16[4,8192]{1,0:T(4,128)(2,1)S(1)}, bf16[4,8192]{1,0:T(4,128)(2,1)S(1)}, u32[]{:S(2)}, u32[]{:S(2)}) collective-permute-start(bf16[4,8192]{1,0:T(4,128)(2,1)S(1)} %get-tuple-element.64), channel_id=1, source_target_pairs={{0,8},{8,0},{1,9},{9,1},{2,10},{10,2},{3,11},{11,3},{4,12},{12,4},... | collective-permute-start | bytes 196616 | tf_op jit(solution)/shard_map/ppermute | solution.py:22
  8.1 14.0 %collective-permute-start.4 = (bf16[64,3584]{1,0:T(8,128)(2,1)S(1)}, bf16[64,3584]{1,0:T(8,128)(2,1)S(1)}, u32[]{:S(2)}, u32[]{:S(2)}) collective-permute-start(bf16[64,3584]{1,0:T(8,128)(2,1)S(1)} %maximum_bitcast_fusion.refs_0_), channel_id=1, source_target_pairs={{0,16},{16,32},{32,48},{48,0},{1,17},{17,33},{33,49},{49,1},{2,18}... | collective-permute-start | bytes 1376264 | tf_op jit(solution)/shard_map/ppermute | solution.py:22
  8.2 13.9 %collective-permute-start.3 = (bf16[64,3584]{1,0:T(8,128)(2,1)S(1)}, bf16[64,3584]{1,0:T(8,128)(2,1)S(1)}, u32[]{:S(2)}, u32[]{:S(2)}) collective-permute-start(bf16[64,3584]{1,0:T(8,128)(2,1)S(1)} %maximum_bitcast_fusion.refs_0_), channel_id=1, source_target_pairs={{0,192},{64,0},{128,64},{192,128},{1,193},{65,1},{129,65},{193,129... | collective-permute-start | bytes 1376264 | tf_op jit(solution)/shard_map/ppermute | solution.py:22
  10.9 12.7 %collective-permute-start.2 = (bf16[64,3584]{1,0:T(8,128)(2,1)S(1)}, bf16[64,3584]{1,0:T(8,128)(2,1)S(1)}, u32[]{:S(2)}, u32[]{:S(2)}) collective-permute-start(bf16[64,3584]{1,0:T(8,128)(2,1)S(1)} %maximum_bitcast_fusion.refs_0_), channel_id=1, source_target_pairs={{0,64},{64,128},{128,192},{192,0},{1,65},{65,129},{129,193},{193,1... | collective-permute-start | bytes 1376264 | tf_op jit(solution)/shard_map/ppermute | solution.py:22
  11.6 14.0 %all-to-all-start = ((bf16[16,8,512]{2,1,0:T(8,128)(2,1)}), bf16[16,8,512]{2,1,0:T(8,128)(2,1)S(1)}, u32[]{:S(2)}, u32[]{:S(2)}) async-start(bf16[16,8,512]{2,1,0:T(8,128)(2,1)} %bitcast.10), calls=%async_computation | async-start | bytes 262144 | tf_op jit(solution)/shard_map/all_to_all | solution.py:241
  25.7 19.1 %collective-permute-start.7 = (bf16[96,3584]{1,0:T(8,128)(2,1)S(1)}, bf16[96,3584]{1,0:T(8,128)(2,1)S(1)}, u32[]{:S(2)}, u32[]{:S(2)}) collective-permute-start(bf16[96,3584]{1,0:T(8,128)(2,1)S(1)} %get-tuple-element.67), channel_id=1, source_target_pairs={{0,192},{64,0},{128,64},{192,128},{1,193},{65,1},{129,65},{193,129... | collective-permute-start | bytes 2064392 | tf_op jit(solution)/shard_map/ppermute | solution.py:22
  26.6 18.2 %collective-permute-start.5 = (bf16[96,3584]{1,0:T(8,128)(2,1)S(1)}, bf16[96,3584]{1,0:T(8,128)(2,1)S(1)}, u32[]{:S(2)}, u32[]{:S(2)}) collective-permute-start(bf16[96,3584]{1,0:T(8,128)(2,1)S(1)} %get-tuple-element.119), channel_id=1, source_target_pairs={{0,64},{64,128},{128,192},{192,0},{1,65},{65,129},{129,193},{193,1... | collective-permute-start | bytes 2064392 | tf_op jit(solution)/shard_map/ppermute | solution.py:22
  27.1 17.6 %collective-permute-start.8 = (bf16[64,3584]{1,0:T(8,128)(2,1)S(1)}, bf16[64,3584]{1,0:T(8,128)(2,1)S(1)}, u32[]{:S(2)}, u32[]{:S(2)}) collective-permute-start(bf16[64,3584]{1,0:T(8,128)(2,1)S(1)} %collective-permute-done.4.refs_5_), channel_id=1, source_target_pairs={{0,16},{16,32},{32,48},{48,0},{1,17},{17,33},{33,49},{49,1},{2,18}... | collective-permute-start | bytes 1376264 | tf_op jit(solution)/shard_map/ppermute | solution.py:22
  27.7 17.0 %collective-permute-start.9 = (bf16[16,8,512]{2,1,0:T(8,128)(2,1)S(1)}, bf16[16,8,512]{2,1,0:T(8,128)(2,1)S(1)}, u32[]{:S(2)}, u32[]{:S(2)}) collective-permute-start(bf16[16,8,512]{2,1,0:T(8,128)(2,1)S(1)} %all-to-all-done), channel_id=1, source_target_pairs={{0,4},{4,0},{1,5},{5,1},{2,6},{6,2},{3,7},{7,3},{8,12},{12,8},{9,1... | collective-permute-start | bytes 393224 | tf_op jit(solution)/shard_map/ppermute | solution.py:22
  44.9 12.3 %collective-permute-start.11 = (bf16[96,3584]{1,0:T(8,128)(2,1)S(1)}, bf16[96,3584]{1,0:T(8,128)(2,1)S(1)}, u32[]{:S(2)}, u32[]{:S(2)}) collective-permute-start(bf16[96,3584]{1,0:T(8,128)(2,1)S(1)} %get-tuple-element.116), channel_id=1, source_target_pairs={{0,192},{64,0},{128,64},{192,128},{1,193},{65,1},{129,65},{193,129... | collective-permute-start | bytes 2064392 | tf_op jit(solution)/shard_map/ppermute | solution.py:22
  47.4 12.6 %collective-permute-start.10 = (bf16[96,3584]{1,0:T(8,128)(2,1)S(1)}, bf16[96,3584]{1,0:T(8,128)(2,1)S(1)}, u32[]{:S(2)}, u32[]{:S(2)}) collective-permute-start(bf16[96,3584]{1,0:T(8,128)(2,1)S(1)} %get-tuple-element.117), channel_id=1, source_target_pairs={{0,64},{64,128},{128,192},{192,0},{1,65},{65,129},{129,193},{193,1... | collective-permute-start | bytes 2064392 | tf_op jit(solution)/shard_map/ppermute | solution.py:22
  47.4 9.8 %collective-permute-start.12 = (bf16[64,3584]{1,0:T(8,128)(2,1)S(1)}, bf16[64,3584]{1,0:T(8,128)(2,1)S(1)}, u32[]{:S(2)}, u32[]{:S(2)}) collective-permute-start(bf16[64,3584]{1,0:T(8,128)(2,1)S(1)} %collective-permute-done.8.refs_8_), channel_id=1, source_target_pairs={{0,16},{16,32},{32,48},{48,0},{1,17},{17,33},{33,49},{49,1},{2,18}... | collective-permute-start | bytes 1376264 | tf_op jit(solution)/shard_map/ppermute | solution.py:22
  47.4 5.9 %collective-permute-start.14 = (bf16[2,16,8,512]{3,2,1,0:T(8,128)(2,1)S(1)}, bf16[2,16,8,512]{3,2,1,0:T(8,128)(2,1)S(1)}, u32[]{:S(2)}, u32[]{:S(2)}) collective-permute-start(bf16[2,16,8,512]{3,2,1,0:T(8,128)(2,1)S(1)} %pad_maximum_fusion.7.refs_0_), channel_id=1, source_target_pairs={{0,3},{1,0},{2,1},{3,2},{4,7},{5,4},{6,5},{7,6},{8,11},{9,8},{10,9... | collective-permute-start | bytes 786440 | tf_op jit(solution)/shard_map/ppermute | solution.py:22
  50.0 6.4 %collective-permute-start.13 = (bf16[2,16,8,512]{3,2,1,0:T(8,128)(2,1)S(1)}, bf16[2,16,8,512]{3,2,1,0:T(8,128)(2,1)S(1)}, u32[]{:S(2)}, u32[]{:S(2)}) collective-permute-start(bf16[2,16,8,512]{3,2,1,0:T(8,128)(2,1)S(1)} %pad_maximum_fusion.7.refs_0_), channel_id=1, source_target_pairs={{0,1},{1,2},{2,3},{3,0},{4,5},{5,6},{6,7},{7,4},{8,9},{9,10},{10,1... | collective-permute-start | bytes 786440 | tf_op jit(solution)/shard_map/ppermute | solution.py:22
  60.1 9.9 %collective-permute-start.18 = (bf16[2,16,8,512]{3,2,1,0:T(8,128)(2,1)S(1)}, bf16[2,16,8,512]{3,2,1,0:T(8,128)(2,1)S(1)}, u32[]{:S(2)}, u32[]{:S(2)}) collective-permute-start(bf16[2,16,8,512]{3,2,1,0:T(8,128)(2,1)S(1)} %pad_maximum_fusion.7.refs_0_), channel_id=1, source_target_pairs={{0,2},{1,3},{2,0},{3,1},{4,6},{5,7},{6,4},{7,5},{8,10},{9,11},{10,... | collective-permute-start | bytes 786440 | tf_op jit(solution)/shard_map/ppermute | solution.py:22
  63.2 12.7 %collective-permute-start.16 = (bf16[96,3584]{1,0:T(8,128)(2,1)S(1)}, bf16[96,3584]{1,0:T(8,128)(2,1)S(1)}, u32[]{:S(2)}, u32[]{:S(2)}) collective-permute-start(bf16[96,3584]{1,0:T(8,128)(2,1)S(1)} %get-tuple-element.114), channel_id=1, source_target_pairs={{0,192},{64,0},{128,64},{192,128},{1,193},{65,1},{129,65},{193,129... | collective-permute-start | bytes 2064392 | tf_op jit(solution)/shard_map/ppermute | solution.py:22
  63.5 12.4 %collective-permute-start.15 = (bf16[96,3584]{1,0:T(8,128)(2,1)S(1)}, bf16[96,3584]{1,0:T(8,128)(2,1)S(1)}, u32[]{:S(2)}, u32[]{:S(2)}) collective-permute-start(bf16[96,3584]{1,0:T(8,128)(2,1)S(1)} %get-tuple-element.115), channel_id=1, source_target_pairs={{0,64},{64,128},{128,192},{192,0},{1,65},{65,129},{129,193},{193,1... | collective-permute-start | bytes 2064392 | tf_op jit(solution)/shard_map/ppermute | solution.py:22
  64.8 11.1 %collective-permute-start.17 = (bf16[64,3584]{1,0:T(8,128)(2,1)S(1)}, bf16[64,3584]{1,0:T(8,128)(2,1)S(1)}, u32[]{:S(2)}, u32[]{:S(2)}) collective-permute-start(bf16[64,3584]{1,0:T(8,128)(2,1)S(1)} %pad_maximum_fusion.6), channel_id=1, source_target_pairs={{0,48},{16,0},{32,16},{48,32},{1,49},{17,1},{33,17},{49,33},{2,50}... | collective-permute-start | bytes 1376264 | tf_op jit(solution)/shard_map/ppermute | solution.py:22
  76.6 9.7 %collective-permute-start.19 = (bf16[256,1792]{1,0:T(8,128)(2,1)S(1)}, bf16[256,1792]{1,0:T(8,128)(2,1)S(1)}, u32[]{:S(2)}, u32[]{:S(2)}) collective-permute-start(bf16[256,1792]{1,0:T(8,128)(2,1)S(1)} %get-tuple-element.91), channel_id=1, source_target_pairs={{0,8},{8,0},{1,9},{9,1},{2,10},{10,2},{3,11},{11,3},{4,12},{12,4},... | collective-permute-start | bytes 2752520 | tf_op jit(solution)/shard_map/ppermute | solution.py:22
  86.3 2.5 %collective-permute-start.20 = (bf16[256,1792]{1,0:T(8,128)(2,1)S(1)}, bf16[256,1792]{1,0:T(8,128)(2,1)S(1)}, u32[]{:S(2)}, u32[]{:S(2)}) collective-permute-start(bf16[256,1792]{1,0:T(8,128)(2,1)S(1)} %get-tuple-element.96), channel_id=1, source_target_pairs={{0,8},{8,0},{1,9},{9,1},{2,10},{10,2},{3,11},{11,3},{4,12},{12,4},... | collective-permute-start | bytes 2752520 | tf_op jit(solution)/shard_map/ppermute | solution.py:22

commit v5 on v4

--- a/solution.py
+++ b/solution.py
@@ -61,37 +61,15 @@
 
 
 def part_kernel(ranges, width, left_ref, *refs):
-    *arrays, out_ref, held, sems = refs
-    total_ref = arrays.pop() if len(arrays) > len({which for which, _, _ in ranges}) else None
-    columns = out_ref.shape[1]
-    cuts = (0, columns // (2 * width) * width, columns)
-
-    def copies(side):
-        found, at = [], 0
-        part = pl.ds(cuts[side], cuts[side + 1] - cuts[side])
-        for which, row, count in ranges:
-            source, target = arrays[which].at[pl.ds(row, count), part], held.at[pl.ds(at, count), part]
-            found.append(pltpu.make_async_copy(source, target, sems.at[side, len(found)]))
-            at += count
-        return found
-
-    for side in (0, 1):
-        for copy in copies(side):
-            copy.start()
-    for side in (0, 1):
-        for copy in copies(side):
-            copy.wait()
-
-        def step(i, _):
-            at = pl.ds(pl.multiple_of(i * width, width), width)
-            product = jnp.dot(left_ref[...], held[:, at], preferred_element_type=jnp.float32)
-            out_ref[:, at] = product if total_ref is None else total_ref[:, at] + product
-            return _
-
-        lax.fori_loop(cuts[side] // width, cuts[side + 1] // width, step, None, unroll=True)
-
-
-def multiply_part(left, pieces, total, name):
+    *arrays, out_ref = refs
+    left = left_ref[...]
+    for at in range(0, out_ref.shape[1], width):
+        columns = slice(at, at + width)
+        right = jnp.concatenate([arrays[which][row : row + count, columns] for which, row, count in ranges], axis=0)
+        out_ref[:, columns] = jnp.dot(left, right, preferred_element_type=jnp.float32)
+
+
+def multiply_part(left, pieces, name):
     arrays, ranges = [], []
     for array, row, count in pieces:
         known = [k for k, other in enumerate(arrays) if other is array]
@@ -101,55 +79,45 @@
     rows, depth = left.shape
     columns = arrays[0].shape[1]
     vmem = pl.BlockSpec(memory_space=pltpu.VMEM)
-    totals = [] if total is None else [total]
     return pl.pallas_call(
         functools.partial(part_kernel, ranges, 256),
         out_shape=jax.ShapeDtypeStruct((rows, columns), jnp.float32),
-        in_specs=[vmem] + [pl.BlockSpec(memory_space=pl.ANY)] * len(arrays) + [vmem] * len(totals),
+        in_specs=[vmem] * (1 + len(arrays)),
         out_specs=vmem,
-        scratch_shapes=[
-            pltpu.VMEM((depth, columns), left.dtype),
-            pltpu.SemaphoreType.DMA((2, len(ranges))),
-        ],
-        input_output_aliases={1 + len(arrays): 0} if totals else {},
         compiler_params=pltpu.CompilerParams(vmem_limit_bytes=24 << 20),
         cost_estimate=pl.CostEstimate(
-            flops=4 * rows * columns * depth, bytes_accessed=12 << 20, transcendentals=0
+            flops=2 * rows * columns * depth, bytes_accessed=1 << 20, transcendentals=0
         ),
         name=name,
-    )(left, *arrays, *totals)
-
-
-def last_kernel(ranges, cut, width, core_ref, left_ref, total_ref, *refs):
-    *right_refs, keep_ref, send_ref = refs
-    rows, columns = keep_ref.shape
-    mine = pl.multiple_of(core_ref[0] * rows, rows)
-    other = pl.multiple_of((1 - core_ref[0]) * rows, rows)
-
-    def step(i, _):
-        at = pl.ds(pl.multiple_of(i * width, width), width)
-        from_at = pl.ds(pl.multiple_of(cut + i * width, width), width)
-        right = jnp.concatenate([right_refs[k][pl.ds(row, count), from_at] for k, row, count in ranges], axis=0)
-        for out_ref, row in ((send_ref, other), (keep_ref, mine)):
-            total = total_ref[pl.ds(row, rows), from_at]
-            total += jnp.dot(left_ref[pl.ds(row, rows)], right, preferred_element_type=jnp.float32)
-            out_ref[:, at] = total.astype(out_ref.dtype)
-        return _
-
-    lax.fori_loop(0, columns // width, step, None, unroll=True)
-
-
-def multiply_last(core, left, total, arrays, ranges, cut, end, name):
-    rows, columns = total.shape[0] // 2, end - cut
-    shape = jax.ShapeDtypeStruct((rows, columns), left.dtype)
+    )(left, *arrays)
+
+
+def last_kernel(mine, ranges, width, core_ref, left_ref, total_ref, *refs):
+    right_refs, out_refs = refs[:3], refs[3:]
+    rows = out_refs[0].shape[0]
+    core = core_ref[0] if mine else 1 - core_ref[0]
+    row = pl.ds(pl.multiple_of(core * rows, rows), rows)
+    start = 0
+    for out_ref in out_refs:
+        for at in range(0, out_ref.shape[1], width):
+            from_at = slice(start + at, start + at + width)
+            right = jnp.concatenate([right_refs[k][first : first + count, from_at] for k, first, count in ranges], axis=0)
+            total = total_ref[row, from_at]
+            total += jnp.dot(left_ref[row], right, preferred_element_type=jnp.float32)
+            out_ref[:, at : at + width] = total.astype(out_ref.dtype)
+        start += out_ref.shape[1]
+
+
+def multiply_last(core, left, total, arrays, ranges, mine, cuts, name):
+    rows = total.shape[0] // 2
     vmem = pl.BlockSpec(memory_space=pltpu.VMEM)
     return pl.pallas_call(
-        functools.partial(last_kernel, ranges, cut, 256),
-        out_shape=(shape, shape),
+        functools.partial(last_kernel, mine, ranges, 256),
+        out_shape=tuple(jax.ShapeDtypeStruct((rows, cut), left.dtype) for cut in cuts),
         in_specs=[pl.BlockSpec(memory_space=pltpu.SMEM)] + [vmem] * (2 + len(arrays)),
-        out_specs=(vmem, vmem),
+        out_specs=(vmem,) * len(cuts),
         compiler_params=pltpu.CompilerParams(vmem_limit_bytes=14 << 20),
-        cost_estimate=pl.CostEstimate(flops=1024 * rows * columns, bytes_accessed=6 << 20, transcendentals=0),
+        cost_estimate=pl.CostEstimate(flops=1024 * rows * sum(cuts), bytes_accessed=6 << 20, transcendentals=0),
         name=name,
     )(core, left, total, *arrays)
 
@@ -242,7 +210,7 @@
     own, = event(own)
     up0, down0 = both(own)
     z1 = shift(own, "z", 1)
-    up0, down0, z1 = event(up0, down0, z1)
+    z1, down0, up0 = event(z1, down0, up0)
 
     up1, down1 = join(z1, up0, down0)
     up1 = shift(up1, "y", 1)
@@ -250,13 +218,13 @@
     left, down1 = event(left, down1)
     down1 = shift(down1, "y", -1)
     left_h = shift(left, "h", 1)
-    up1, down1, z2, left, left_h = event(up1, down1, z2, left, left_h)
+    z2, left, left_h, down1, up1 = event(z2, left, left_h, down1, up1)
 
     up2, down2 = both(z2, up1, down1)
     z3 = shift(z2, "z", 1)
     left = jnp.stack([left, left_h])
     left_1, left_3 = shift(left, "x", 1), shift(left, "x", 3)
-    up2, down2, z3, left, left_1, left_3 = event(up2, down2, z3, left, left_1, left_3)
+    z3, left, left_1, left_3, down2, up2 = event(z3, left, left_1, left_3, down2, up2)
 
     up3, down3 = both(z3, up2, down2)
     far3 = shift(jnp.concatenate([up1[n:], down1[n:]], axis=0), "z", 3)
@@ -267,19 +235,18 @@
 
     pieces = slot(own, up0, down0, up1, down1) + slot(z1, up1, down1, up2, down2)
     pieces += [(part, 0, n) for part in (z2, up2, down2, z3)]
-    total = multiply_part(left, pieces, None, "multiply_0")
-    up3, down3, far3, total = event(up3, down3, far3, total)
+    total = multiply_part(left, pieces, "multiply_0")
+    far3, down3, up3, total = event(far3, down3, up3, total)
 
     cut = columns // 2
     lasts = [up3, down3, far3]
     ranges = [(0, n, half), (1, n, half), (0, 0, n), (1, 0, n), (2, 0, n)]
-    keep_0, send_0 = multiply_last(token, left_last, total, lasts, ranges, 0, cut, "multiply_1")
-    got_0 = shift(send_0, "c", 1)
-    keep_1, send_1 = multiply_last(token, left_last, total, lasts, ranges, cut, columns, "multiply_2")
-    outs = put(token, keep_0, [], 0, 0, columns)
-    got_0, send_1, *outs = event(got_0, send_1, *outs)
-    got_1 = shift(send_1, "c", 1)
-    outs = put(token, keep_1, outs, 0, cut, columns)
+    cuts = (cut, columns - cut)
+    sends = multiply_last(token, left_last, total, lasts, ranges, False, cuts, "multiply_1")
+    got_0, got_1 = [shift(send, "c", 1) for send in sends]
+    (keep,) = multiply_last(token, left_last, total, lasts, ranges, True, (columns,), "multiply_2")
+    outs = put(token, keep, [], 0, 0, columns)
+    got_0, *outs = event(got_0, *outs)
     outs = put(token, got_0, outs, 1, 0, columns)
     got_1, *outs = event(got_1, *outs)
     return tuple(put(token, got_1, outs, 1, cut, columns))

time: 90.1 us -> 89 us (0.988)
  Pallas kernels: 10.9 us -> 8.42 us
    pallas_call x1, Pallas kernels: 4.9 us -> 3.02 us  [multiply_part(): pl.pallas_call(functools.partial(part_kernel, ranges, 256), out_shape=jax...]
    ppermute x21, waiting for transfers between devices: 27.4 us -> 28.3 us  [shift(): return lax.ppermute(x, axis, [(i, (i + by) % n) for i in range(n)])]
    pallas_call x4 -> x3, Pallas kernels: 3.72 us -> 3.1 us  [put(): pl.pallas_call(functools.partial(put_kernel, got, at), out_shape=(shape,...]
  transfers between devices with their start and end apart: 22 -> 22, of which waited for: 10 -> 11; matrix products, arithmetic and copies ran while one was open for 4% -> 4% of each run, Pallas kernels for 10% -> 8%
where the time goes in v5:
time: 89 us; the launch traced here: 88.7 us
  starting transfers between devices  44.3 us (50%)
  waiting for transfers between devices  30.2 us (34%)
  Pallas kernels  8.42 us (9%)
  other arithmetic  3.36 us (4%)
  between operations  2.26 us (3%)
    ppermute x21, starting transfers between devices, shift(): return lax.ppermute(x, axis, [(i, (i + by) % n) for i in range(n)])  37.5 us
    ppermute x21, waiting for transfers between devices, shift(): return lax.ppermute(x, axis, [(i, (i + by) % n) for i in range(n)])  28.3 us
    all_to_all x1, starting transfers between devices, shards(): lax.all_to_all(left, ('y', 'z'), split_axis=0, concat_axis=0, tiled=True)  6.76 us
    pallas_call x3, Pallas kernels, put(): pl.pallas_call(functools.partial(put_kernel, got, at), out_shape=(shape,...  3.1 us
    pallas_call x1, Pallas kernels, multiply_part(): pl.pallas_call(functools.partial(part_kernel, ranges, 256), out_shape=jax...  3.02 us
    all_to_all x1, waiting for transfers between devices, shards(): lax.all_to_all(left, ('y', 'z'), split_axis=0, concat_axis=0, tiled=True)  1.92 us
  transfers between devices with their start and end apart: 22, of which 11 were waited for; matrix products, arithmetic and copies ran while one was open for 4% of the time, Pallas kernels for 8%

profile of v5, /device:TPU:1, one launch (start us, length us, event | category | flops | bytes accessed | tf_op | source)
XLA Modules:
  0.0 88.7 jit_solution(12671725704336868730)
XLA Ops:
  0.6 3.3 %collective-permute-start = (bf16[8,4,3584]{2,1,0:T(4,128)(2,1)}, bf16[8,4,3584]{2,1,0:T(4,128)(2,1)S(1)}, u32[]{:S(2)}, u32[]{:S(2)}) collective-permute-start(bf16[8,4,3584]{2,1,0:T(4,128)(2,1)} %param.8), channel_id=1, source_target_pairs={{0,8},{8,0},{1,9},{9,1},{2,10},{10,2},{3,11},{11,3},{4,12},{12,4},... | collective-permute-start | bytes 688136 | tf_op jit(solution)/shard_map/ppermute | solution.py:22
  5.4 0.9 %select_bitcast_fusion = (bf16[4,8192]{1,0:T(4,128)(2,1)S(1)}, bf16[4,8192]{1,0:T(4,128)(2,1)S(1)}) fusion(pred[]{:T(512)S(6)} %eq.3, bf16[1,4,8192]{2,1,0:T(4,128)(2,1)} %param.6, f32[]{:T(128)} %bitcast, bf16[1,4,8192]{2,1,0:T(4,128)(2,1)} %param.7), kind=kLoop, calls=%fused_computation.14 | loop fusion | flops 262144 | bytes 262149 | tf_op jit(solution)/shard_map/jit(_where)/select_n | solution.py:179
  6.9 1.0 %broadcast_select_fusion = (bf16[4,8,3584]{2,1,0:T(8,128)(2,1)S(1)}, bf16[4,8,3584]{2,1,0:T(8,128)(2,1)S(1)}) fusion(bf16[4,8,3584]{2,1,0:T(8,128)(2,1)S(1)} %bitcast.28, bf16[4,8,3584]{2,1,0:T(8,128)(2,1)} %bitcast.27, pred[]{:T(512)S(6)} %eq.3, bf16[4,8,3584]{2,1,0:T(8,128)(2,1)} %bitcast.26, bf16[4,8,3584]{2,1,0:T(8,128)(2,1)S(1)} %bitcast.29), kind=kLoop, calls=%fused_computation.9 | loop fusion | flops 229376 | bytes 1376257 | tf_op jit(solution)/shard_map/jit(_where)/select_n | solution.py:181
  8.2 2.6 %collective-permute-start.3 = (bf16[64,3584]{1,0:T(8,128)(2,1)S(1)}, bf16[64,3584]{1,0:T(8,128)(2,1)S(1)}, u32[]{:S(2)}, u32[]{:S(2)}) collective-permute-start(bf16[64,3584]{1,0:T(8,128)(2,1)S(1)} %maximum_bitcast_fusion.refs_0_), channel_id=1, source_target_pairs={{0,192},{64,0},{128,64},{192,128},{1,193},{65,1},{129,65},{193,129... | collective-permute-start | bytes 1376264 | tf_op jit(solution)/shard_map/ppermute | solution.py:22
  11.6 6.8 %all-to-all-start = ((bf16[16,8,512]{2,1,0:T(8,128)(2,1)}), bf16[16,8,512]{2,1,0:T(8,128)(2,1)S(1)}, u32[]{:S(2)}, u32[]{:S(2)}) async-start(bf16[16,8,512]{2,1,0:T(8,128)(2,1)} %bitcast.10), calls=%async_computation | async-start | bytes 262144 | tf_op jit(solution)/shard_map/all_to_all | solution.py:209
  18.4 3.7 %collective-permute-done.2.refs_5_ = bf16[64,3584]{1,0:T(8,128)(2,1)S(1)} collective-permute-done((bf16[64,3584]{1,0:T(8,128)(2,1)S(1)}, bf16[64,3584]{1,0:T(8,128)(2,1)S(1)}, u32[]{:S(2)}, u32[]{:S(2)}) %collective-permute-start.2) | collective-permute-done | bytes 458784 | tf_op jit(solution)/shard_map/ppermute | solution.py:22
  22.1 1.5 %collective-permute-done.4.refs_1_ = bf16[64,3584]{1,0:T(8,128)(2,1)S(1)} collective-permute-done((bf16[64,3584]{1,0:T(8,128)(2,1)S(1)}, bf16[64,3584]{1,0:T(8,128)(2,1)S(1)}, u32[]{:S(2)}, u32[]{:S(2)}) %collective-permute-start.4) | collective-permute-done | bytes 458784 | tf_op jit(solution)/shard_map/ppermute | solution.py:22
  23.7 1.9 %all-to-all-done = bf16[16,8,512]{2,1,0:T(8,128)(2,1)S(1)} async-done(((bf16[16,8,512]{2,1,0:T(8,128)(2,1)}), bf16[16,8,512]{2,1,0:T(8,128)(2,1)S(1)}, u32[]{:S(2)}, u32[]{:S(2)}) %all-to-all-start) | async-done | bytes 131104 | tf_op jit(solution)/shard_map/all_to_all | solution.py:209
  27.7 5.5 %collective-permute-start.7 = (bf16[16,8,512]{2,1,0:T(8,128)(2,1)S(1)}, bf16[16,8,512]{2,1,0:T(8,128)(2,1)S(1)}, u32[]{:S(2)}, u32[]{:S(2)}) collective-permute-start(bf16[16,8,512]{2,1,0:T(8,128)(2,1)S(1)} %all-to-all-done), channel_id=1, source_target_pairs={{0,4},{4,0},{1,5},{5,1},{2,6},{6,2},{3,7},{7,3},{8,12},{12,8},{9,1... | collective-permute-start | bytes 393224 | tf_op jit(solution)/shard_map/ppermute | solution.py:22
  33.3 11.4 %collective-permute-done.7 = bf16[16,8,512]{2,1,0:T(8,128)(2,1)S(1)} collective-permute-done((bf16[16,8,512]{2,1,0:T(8,128)(2,1)S(1)}, bf16[16,8,512]{2,1,0:T(8,128)(2,1)S(1)}, u32[]{:S(2)}, u32[]{:S(2)}) %collective-permute-start.7) | collective-permute-done | bytes 131104 | tf_op jit(solution)/shard_map/ppermute | solution.py:22
  44.9 2.5 %collective-permute-start.14 = (bf16[96,3584]{1,0:T(8,128)(2,1)S(1)}, bf16[96,3584]{1,0:T(8,128)(2,1)S(1)}, u32[]{:S(2)}, u32[]{:S(2)}) collective-permute-start(bf16[96,3584]{1,0:T(8,128)(2,1)S(1)} %get-tuple-element.107), channel_id=1, source_target_pairs={{0,192},{64,0},{128,64},{192,128},{1,193},{65,1},{129,65},{193,129... | collective-permute-start | bytes 2064392 | tf_op jit(solution)/shard_map/ppermute | solution.py:22
  47.4 1.3 %collective-permute-start.12 = (bf16[2,16,8,512]{3,2,1,0:T(8,128)(2,1)S(1)}, bf16[2,16,8,512]{3,2,1,0:T(8,128)(2,1)S(1)}, u32[]{:S(2)}, u32[]{:S(2)}) collective-permute-start(bf16[2,16,8,512]{3,2,1,0:T(8,128)(2,1)S(1)} %pad_maximum_fusion.7.refs_0_), channel_id=1, source_target_pairs={{0,1},{1,2},{2,3},{3,0},{4,5},{5,6},{6,7},{7,4},{8,9},{9,10},{10,1... | collective-permute-start | bytes 786440 | tf_op jit(solution)/shard_map/ppermute | solution.py:22
  48.7 1.5 %collective-permute-start.13 = (bf16[2,16,8,512]{3,2,1,0:T(8,128)(2,1)S(1)}, bf16[2,16,8,512]{3,2,1,0:T(8,128)(2,1)S(1)}, u32[]{:S(2)}, u32[]{:S(2)}) collective-permute-start(bf16[2,16,8,512]{3,2,1,0:T(8,128)(2,1)S(1)} %pad_maximum_fusion.7.refs_0_), channel_id=1, source_target_pairs={{0,3},{1,0},{2,1},{3,2},{4,7},{5,4},{6,5},{7,6},{8,11},{9,8},{10,9... | collective-permute-start | bytes 786440 | tf_op jit(solution)/shard_map/ppermute | solution.py:22
  50.2 3.8 %collective-permute-done.12.refs_1_ = bf16[2,16,8,512]{3,2,1,0:T(8,128)(2,1)S(1)} collective-permute-done((bf16[2,16,8,512]{3,2,1,0:T(8,128)(2,1)S(1)}, bf16[2,16,8,512]{3,2,1,0:T(8,128)(2,1)S(1)}, u32[]{:S(2)}, u32[]{:S(2)}) %collective-permute-start.12) | collective-permute-done | bytes 262176 | tf_op jit(solution)/shard_map/ppermute | solution.py:22
  54.2 3.0 %collective-permute-done.11.refs_9_ = bf16[64,3584]{1,0:T(8,128)(2,1)S(1)} collective-permute-done((bf16[64,3584]{1,0:T(8,128)(2,1)S(1)}, bf16[64,3584]{1,0:T(8,128)(2,1)S(1)}, u32[]{:S(2)}, u32[]{:S(2)}) %collective-permute-start.11) | collective-permute-done | bytes 458784 | tf_op jit(solution)/shard_map/ppermute | solution.py:22
  57.2 2.8 %collective-permute-done.15.refs_6_ = bf16[96,3584]{1,0:T(8,128)(2,1)S(1)} collective-permute-done((bf16[96,3584]{1,0:T(8,128)(2,1)S(1)}, bf16[96,3584]{1,0:T(8,128)(2,1)S(1)}, u32[]{:S(2)}, u32[]{:S(2)}) %collective-permute-start.15) | collective-permute-done | bytes 688160 | tf_op jit(solution)/shard_map/ppermute | solution.py:22
  60.0 2.7 %collective-permute-start.18 = (bf16[2,16,8,512]{3,2,1,0:T(8,128)(2,1)S(1)}, bf16[2,16,8,512]{3,2,1,0:T(8,128)(2,1)S(1)}, u32[]{:S(2)}, u32[]{:S(2)}) collective-permute-start(bf16[2,16,8,512]{3,2,1,0:T(8,128)(2,1)S(1)} %pad_maximum_fusion.7.refs_0_), channel_id=1, source_target_pairs={{0,2},{1,3},{2,0},{3,1},{4,6},{5,7},{6,4},{7,5},{8,10},{9,11},{10,... | collective-permute-start | bytes 786440 | tf_op jit(solution)/shard_map/ppermute | solution.py:22
  63.3 1.2 %collective-permute-start.17 = (bf16[96,3584]{1,0:T(8,128)(2,1)S(1)}, bf16[96,3584]{1,0:T(8,128)(2,1)S(1)}, u32[]{:S(2)}, u32[]{:S(2)}) collective-permute-start(bf16[96,3584]{1,0:T(8,128)(2,1)S(1)} %get-tuple-element.104), channel_id=1, source_target_pairs={{0,64},{64,128},{128,192},{192,0},{1,65},{65,129},{129,193},{193,1... | collective-permute-start | bytes 2064392 | tf_op jit(solution)/shard_map/ppermute | solution.py:22
  64.5 5.2 %collective-permute-start.10 = (bf16[64,3584]{1,0:T(8,128)(2,1)S(1)}, bf16[64,3584]{1,0:T(8,128)(2,1)S(1)}, u32[]{:S(2)}, u32[]{:S(2)}) collective-permute-start(bf16[64,3584]{1,0:T(8,128)(2,1)S(1)} %pad_maximum_fusion.6), channel_id=1, source_target_pairs={{0,48},{16,0},{32,16},{48,32},{1,49},{17,1},{33,17},{49,33},{2,50}... | collective-permute-start | bytes 1376264 | tf_op jit(solution)/shard_map/ppermute | solution.py:22
  69.7 1.0 %arrange_left.1 = (bf16[512,768]{1,0:T(8,128)(2,1)S(1)}, bf16[512,256]{1,0:T(8,128)(2,1)S(1)}) custom-call(s32[4]{0:T(128)S(1)} %pad_add_fusion.place_ref, bf16[2,16,8,512]{3,2,1,0:T(8,128)(2,1)S(1)} %pad_maximum_fusion.7.refs_0_, bf16[2,16,8,512]{3,2,1,0:T(8,128)(2,1)S(1)} %collective-permute-done.12.refs_1_, ...), custom_call_target="tpu_custom_call" | custom-call | bytes 6291456 | tf_op jit(solution)/shard_map/arrange_left/pallas_call | solution.py:48
  70.7 3.0 %multiply_0.1.total_ref = f32[512,3584]{1,0:T(8,128)S(1)} custom-call(bf16[512,768]{1,0:T(8,128)(2,1)S(1)} %get-tuple-element.78.left_ref, bf16[64,3584]{1,0:T(8,128)(2,1)S(1)} %maximum_bitcast_fusion.refs_0_, bf16[64,3584]{1,0:T(8,128)(2,1)S(1)} %collective-permute-done.4.refs_1_, bf16[64,3584]{1,0:T(8,128)(2,1)S(1)} %collective-permute-done.3.refs_2_, ...), custom_call_target="tpu_custom_call" | custom-call | flops 2818572288 | bytes 1048576 | tf_op jit(solution)/shard_map/multiply_0/pallas_call | solution.py:82
  73.7 1.4 %collective-permute-done.10.refs_2_ = bf16[64,3584]{1,0:T(8,128)(2,1)S(1)} collective-permute-done((bf16[64,3584]{1,0:T(8,128)(2,1)S(1)}, bf16[64,3584]{1,0:T(8,128)(2,1)S(1)}, u32[]{:S(2)}, u32[]{:S(2)}) %collective-permute-start.10) | collective-permute-done | bytes 458784 | tf_op jit(solution)/shard_map/ppermute | solution.py:22
  75.8 8.4 %collective-permute-start.20 = (bf16[256,1792]{1,0:T(8,128)(2,1)S(1)}, bf16[256,1792]{1,0:T(8,128)(2,1)S(1)}, u32[]{:S(2)}, u32[]{:S(2)}) collective-permute-start(bf16[256,1792]{1,0:T(8,128)(2,1)S(1)} %get-tuple-element.87), channel_id=1, source_target_pairs={{0,8},{8,0},{1,9},{9,1},{2,10},{10,2},{3,11},{11,3},{4,12},{12,4},... | collective-permute-start | bytes 2752520 | tf_op jit(solution)/shard_map/ppermute | solution.py:22
  84.9 1.2 %put_0_0.1 = (bf16[256,3584]{1,0:T(8,128)(2,1)}, bf16[256,3584]{1,0:T(8,128)(2,1)}) custom-call(s32[1]{0:T(128)} %bitcast.7.core_ref, bf16[256,3584]{1,0:T(8,128)(2,1)S(1)} %multiply_2.1.part_ref), custom_call_target="tpu_custom_call" | custom-call | bytes 4194304 | tf_op jit(solution)/shard_map/put_0_0/pallas_call | solution.py:145
  (44 shorter events, 8.7 us)
Async XLA Ops:
  0.6 5.8 %collective-permute-start = (bf16[8,4,3584]{2,1,0:T(4,128)(2,1)}, bf16[8,4,3584]{2,1,0:T(4,128)(2,1)S(1)}, u32[]{:S(2)}, u32[]{:S(2)}) collective-permute-start(bf16[8,4,3584]{2,1,0:T(4,128)(2,1)} %param.8), channel_id=1, source_target_pairs={{0,8},{8,0},{1,9},{9,1},{2,10},{10,2},{3,11},{11,3},{4,12},{12,4},... | collective-permute-start | bytes 688136 | tf_op jit(solution)/shard_map/ppermute | solution.py:22
  4.0 2.4 %collective-permute-start.1 = (bf16[8,4,3584]{2,1,0:T(4,128)(2,1)}, bf16[8,4,3584]{2,1,0:T(4,128)(2,1)S(1)}, u32[]{:S(2)}, u32[]{:S(2)}) collective-permute-start(bf16[8,4,3584]{2,1,0:T(4,128)(2,1)} %param.9), channel_id=1, source_target_pairs={{0,8},{8,0},{1,9},{9,1},{2,10},{10,2},{3,11},{11,3},{4,12},{12,4},... | collective-permute-start | bytes 688136 | tf_op jit(solution)/shard_map/ppermute | solution.py:22
  6.4 4.5 %collective-permute-start.6 = (bf16[4,8192]{1,0:T(4,128)(2,1)S(1)}, bf16[4,8192]{1,0:T(4,128)(2,1)S(1)}, u32[]{:S(2)}, u32[]{:S(2)}) collective-permute-start(bf16[4,8192]{1,0:T(4,128)(2,1)S(1)} %get-tuple-element.58), channel_id=1, source_target_pairs={{0,8},{8,0},{1,9},{9,1},{2,10},{10,2},{3,11},{11,3},{4,12},{12,4},... | collective-permute-start | bytes 196616 | tf_op jit(solution)/shard_map/ppermute | solution.py:22
  8.1 14.0 %collective-permute-start.2 = (bf16[64,3584]{1,0:T(8,128)(2,1)S(1)}, bf16[64,3584]{1,0:T(8,128)(2,1)S(1)}, u32[]{:S(2)}, u32[]{:S(2)}) collective-permute-start(bf16[64,3584]{1,0:T(8,128)(2,1)S(1)} %maximum_bitcast_fusion.refs_0_), channel_id=1, source_target_pairs={{0,16},{16,32},{32,48},{48,0},{1,17},{17,33},{33,49},{49,1},{2,18}... | collective-permute-start | bytes 1376264 | tf_op jit(solution)/shard_map/ppermute | solution.py:22
  8.2 13.9 %collective-permute-start.3 = (bf16[64,3584]{1,0:T(8,128)(2,1)S(1)}, bf16[64,3584]{1,0:T(8,128)(2,1)S(1)}, u32[]{:S(2)}, u32[]{:S(2)}) collective-permute-start(bf16[64,3584]{1,0:T(8,128)(2,1)S(1)} %maximum_bitcast_fusion.refs_0_), channel_id=1, source_target_pairs={{0,192},{64,0},{128,64},{192,128},{1,193},{65,1},{129,65},{193,129... | collective-permute-start | bytes 1376264 | tf_op jit(solution)/shard_map/ppermute | solution.py:22
  10.9 12.7 %collective-permute-start.4 = (bf16[64,3584]{1,0:T(8,128)(2,1)S(1)}, bf16[64,3584]{1,0:T(8,128)(2,1)S(1)}, u32[]{:S(2)}, u32[]{:S(2)}) collective-permute-start(bf16[64,3584]{1,0:T(8,128)(2,1)S(1)} %maximum_bitcast_fusion.refs_0_), channel_id=1, source_target_pairs={{0,64},{64,128},{128,192},{192,0},{1,65},{65,129},{129,193},{193,1... | collective-permute-start | bytes 1376264 | tf_op jit(solution)/shard_map/ppermute | solution.py:22
  11.6 14.0 %all-to-all-start = ((bf16[16,8,512]{2,1,0:T(8,128)(2,1)}), bf16[16,8,512]{2,1,0:T(8,128)(2,1)S(1)}, u32[]{:S(2)}, u32[]{:S(2)}) async-start(bf16[16,8,512]{2,1,0:T(8,128)(2,1)} %bitcast.10), calls=%async_computation | async-start | bytes 262144 | tf_op jit(solution)/shard_map/all_to_all | solution.py:209
  25.7 19.1 %collective-permute-start.8 = (bf16[96,3584]{1,0:T(8,128)(2,1)S(1)}, bf16[96,3584]{1,0:T(8,128)(2,1)S(1)}, u32[]{:S(2)}, u32[]{:S(2)}) collective-permute-start(bf16[96,3584]{1,0:T(8,128)(2,1)S(1)} %get-tuple-element.62), channel_id=1, source_target_pairs={{0,192},{64,0},{128,64},{192,128},{1,193},{65,1},{129,65},{193,129... | collective-permute-start | bytes 2064392 | tf_op jit(solution)/shard_map/ppermute | solution.py:22
  26.6 18.2 %collective-permute-start.9 = (bf16[96,3584]{1,0:T(8,128)(2,1)S(1)}, bf16[96,3584]{1,0:T(8,128)(2,1)S(1)}, u32[]{:S(2)}, u32[]{:S(2)}) collective-permute-start(bf16[96,3584]{1,0:T(8,128)(2,1)S(1)} %get-tuple-element.108), channel_id=1, source_target_pairs={{0,64},{64,128},{128,192},{192,0},{1,65},{65,129},{129,193},{193,1... | collective-permute-start | bytes 2064392 | tf_op jit(solution)/shard_map/ppermute | solution.py:22
  27.1 17.6 %collective-permute-start.5 = (bf16[64,3584]{1,0:T(8,128)(2,1)S(1)}, bf16[64,3584]{1,0:T(8,128)(2,1)S(1)}, u32[]{:S(2)}, u32[]{:S(2)}) collective-permute-start(bf16[64,3584]{1,0:T(8,128)(2,1)S(1)} %collective-permute-done.2.refs_5_), channel_id=1, source_target_pairs={{0,16},{16,32},{32,48},{48,0},{1,17},{17,33},{33,49},{49,1},{2,18}... | collective-permute-start | bytes 1376264 | tf_op jit(solution)/shard_map/ppermute | solution.py:22
  27.7 17.0 %collective-permute-start.7 = (bf16[16,8,512]{2,1,0:T(8,128)(2,1)S(1)}, bf16[16,8,512]{2,1,0:T(8,128)(2,1)S(1)}, u32[]{:S(2)}, u32[]{:S(2)}) collective-permute-start(bf16[16,8,512]{2,1,0:T(8,128)(2,1)S(1)} %all-to-all-done), channel_id=1, source_target_pairs={{0,4},{4,0},{1,5},{5,1},{2,6},{6,2},{3,7},{7,3},{8,12},{12,8},{9,1... | collective-permute-start | bytes 393224 | tf_op jit(solution)/shard_map/ppermute | solution.py:22
  44.9 12.3 %collective-permute-start.14 = (bf16[96,3584]{1,0:T(8,128)(2,1)S(1)}, bf16[96,3584]{1,0:T(8,128)(2,1)S(1)}, u32[]{:S(2)}, u32[]{:S(2)}) collective-permute-start(bf16[96,3584]{1,0:T(8,128)(2,1)S(1)} %get-tuple-element.107), channel_id=1, source_target_pairs={{0,192},{64,0},{128,64},{192,128},{1,193},{65,1},{129,65},{193,129... | collective-permute-start | bytes 2064392 | tf_op jit(solution)/shard_map/ppermute | solution.py:22
  47.4 12.6 %collective-permute-start.15 = (bf16[96,3584]{1,0:T(8,128)(2,1)S(1)}, bf16[96,3584]{1,0:T(8,128)(2,1)S(1)}, u32[]{:S(2)}, u32[]{:S(2)}) collective-permute-start(bf16[96,3584]{1,0:T(8,128)(2,1)S(1)} %get-tuple-element.106), channel_id=1, source_target_pairs={{0,64},{64,128},{128,192},{192,0},{1,65},{65,129},{129,193},{193,1... | collective-permute-start | bytes 2064392 | tf_op jit(solution)/shard_map/ppermute | solution.py:22
  47.4 9.8 %collective-permute-start.11 = (bf16[64,3584]{1,0:T(8,128)(2,1)S(1)}, bf16[64,3584]{1,0:T(8,128)(2,1)S(1)}, u32[]{:S(2)}, u32[]{:S(2)}) collective-permute-start(bf16[64,3584]{1,0:T(8,128)(2,1)S(1)} %collective-permute-done.5.refs_8_), channel_id=1, source_target_pairs={{0,16},{16,32},{32,48},{48,0},{1,17},{17,33},{33,49},{49,1},{2,18}... | collective-permute-start | bytes 1376264 | tf_op jit(solution)/shard_map/ppermute | solution.py:22
  47.4 6.5 %collective-permute-start.12 = (bf16[2,16,8,512]{3,2,1,0:T(8,128)(2,1)S(1)}, bf16[2,16,8,512]{3,2,1,0:T(8,128)(2,1)S(1)}, u32[]{:S(2)}, u32[]{:S(2)}) collective-permute-start(bf16[2,16,8,512]{3,2,1,0:T(8,128)(2,1)S(1)} %pad_maximum_fusion.7.refs_0_), channel_id=1, source_target_pairs={{0,1},{1,2},{2,3},{3,0},{4,5},{5,6},{6,7},{7,4},{8,9},{9,10},{10,1... | collective-permute-start | bytes 786440 | tf_op jit(solution)/shard_map/ppermute | solution.py:22
  48.7 5.5 %collective-permute-start.13 = (bf16[2,16,8,512]{3,2,1,0:T(8,128)(2,1)S(1)}, bf16[2,16,8,512]{3,2,1,0:T(8,128)(2,1)S(1)}, u32[]{:S(2)}, u32[]{:S(2)}) collective-permute-start(bf16[2,16,8,512]{3,2,1,0:T(8,128)(2,1)S(1)} %pad_maximum_fusion.7.refs_0_), channel_id=1, source_target_pairs={{0,3},{1,0},{2,1},{3,2},{4,7},{5,4},{6,5},{7,6},{8,11},{9,8},{10,9... | collective-permute-start | bytes 786440 | tf_op jit(solution)/shard_map/ppermute | solution.py:22
  60.0 9.7 %collective-permute-start.18 = (bf16[2,16,8,512]{3,2,1,0:T(8,128)(2,1)S(1)}, bf16[2,16,8,512]{3,2,1,0:T(8,128)(2,1)S(1)}, u32[]{:S(2)}, u32[]{:S(2)}) collective-permute-start(bf16[2,16,8,512]{3,2,1,0:T(8,128)(2,1)S(1)} %pad_maximum_fusion.7.refs_0_), channel_id=1, source_target_pairs={{0,2},{1,3},{2,0},{3,1},{4,6},{5,7},{6,4},{7,5},{8,10},{9,11},{10,... | collective-permute-start | bytes 786440 | tf_op jit(solution)/shard_map/ppermute | solution.py:22
  62.9 12.2 %collective-permute-start.16 = (bf16[96,3584]{1,0:T(8,128)(2,1)S(1)}, bf16[96,3584]{1,0:T(8,128)(2,1)S(1)}, u32[]{:S(2)}, u32[]{:S(2)}) collective-permute-start(bf16[96,3584]{1,0:T(8,128)(2,1)S(1)} %get-tuple-element.105), channel_id=1, source_target_pairs={{0,192},{64,0},{128,64},{192,128},{1,193},{65,1},{129,65},{193,129... | collective-permute-start | bytes 2064392 | tf_op jit(solution)/shard_map/ppermute | solution.py:22
  63.3 11.9 %collective-permute-start.17 = (bf16[96,3584]{1,0:T(8,128)(2,1)S(1)}, bf16[96,3584]{1,0:T(8,128)(2,1)S(1)}, u32[]{:S(2)}, u32[]{:S(2)}) collective-permute-start(bf16[96,3584]{1,0:T(8,128)(2,1)S(1)} %get-tuple-element.104), channel_id=1, source_target_pairs={{0,64},{64,128},{128,192},{192,0},{1,65},{65,129},{129,193},{193,1... | collective-permute-start | bytes 2064392 | tf_op jit(solution)/shard_map/ppermute | solution.py:22
  64.5 10.6 %collective-permute-start.10 = (bf16[64,3584]{1,0:T(8,128)(2,1)S(1)}, bf16[64,3584]{1,0:T(8,128)(2,1)S(1)}, u32[]{:S(2)}, u32[]{:S(2)}) collective-permute-start(bf16[64,3584]{1,0:T(8,128)(2,1)S(1)} %pad_maximum_fusion.6), channel_id=1, source_target_pairs={{0,48},{16,0},{32,16},{48,32},{1,49},{17,1},{33,17},{49,33},{2,50}... | collective-permute-start | bytes 1376264 | tf_op jit(solution)/shard_map/ppermute | solution.py:22
  75.8 10.5 %collective-permute-start.20 = (bf16[256,1792]{1,0:T(8,128)(2,1)S(1)}, bf16[256,1792]{1,0:T(8,128)(2,1)S(1)}, u32[]{:S(2)}, u32[]{:S(2)}) collective-permute-start(bf16[256,1792]{1,0:T(8,128)(2,1)S(1)} %get-tuple-element.87), channel_id=1, source_target_pairs={{0,8},{8,0},{1,9},{9,1},{2,10},{10,2},{3,11},{11,3},{4,12},{12,4},... | collective-permute-start | bytes 2752520 | tf_op jit(solution)/shard_map/ppermute | solution.py:22
  84.2 3.4 %collective-permute-start.19 = (bf16[256,1792]{1,0:T(8,128)(2,1)S(1)}, bf16[256,1792]{1,0:T(8,128)(2,1)S(1)}, u32[]{:S(2)}, u32[]{:S(2)}) collective-permute-start(bf16[256,1792]{1,0:T(8,128)(2,1)S(1)} %get-tuple-element.86), channel_id=1, source_target_pairs={{0,8},{8,0},{1,9},{9,1},{2,10},{10,2},{3,11},{11,3},{4,12},{12,4},... | collective-permute-start | bytes 2752520 | tf_op jit(solution)/shard_map/ppermute | solution.py:22

commit v6 on v5

--- a/solution.py
+++ b/solution.py
@@ -24,7 +24,7 @@
 
 def left_kernel(place_ref, *refs):
     *left_refs, out_ref, last_ref, held = refs
-    x, y, z, h = place_ref[0], place_ref[1], place_ref[2], place_ref[3]
+    x, y, z = place_ref[0], place_ref[1], place_ref[2]
     for r, left_ref in enumerate(left_refs):
         held[r] = left_ref[...].astype(held.dtype)
     for k, order in enumerate(ORDER):
@@ -33,7 +33,7 @@
             chip = lax.rem(y + Y - from_y, Y) * Z + lax.rem(z + Z - d, Z)
             for at_h in range(H):
                 for at_x in range(X):
-                    parts.append(held[lax.rem(x + X - at_x, X), lax.rem(h + at_h, H), chip])
+                    parts.append(held[lax.rem(x + X - at_x, X), at_h * Y * Z + chip])
         block = jnp.concatenate(parts, axis=0).T.astype(out_ref.dtype)
         if k < len(ORDER) - 1:
             out_ref[:, k * block.shape[1] : (k + 1) * block.shape[1]] = block
@@ -43,7 +43,7 @@
 
 def arrange_left(place, lefts):
     rows = lefts[0].shape[-1]
-    size = H * X * lefts[0].shape[2]
+    size = H * X * lefts[0].shape[1]
     vmem = pl.BlockSpec(memory_space=pltpu.VMEM)
     return pl.pallas_call(
         left_kernel,
@@ -162,7 +162,7 @@
 def shards(gate_left, up_left, gate_right, up_right, fitness_order, member_scale):
     y, z, core = lax.axis_index("y"), lax.axis_index("z"), lax.axis_index("c")
     first = core == 0
-    place = jnp.stack([lax.axis_index("x"), y, z, lax.axis_index("h")]).astype(jnp.int32)
+    place = jnp.stack([lax.axis_index("x"), y, z]).astype(jnp.int32)
     token = core.reshape(1).astype(jnp.int32)
     total = Y * Z * C * H * X
     rank, columns = gate_right.shape[1:]
@@ -195,45 +195,38 @@
     n = own.shape[0]
     half = n // 2
 
-    def both(block, up=None, down=None):
-        if up is not None:
-            up, down = join(block, up, down)
-        else:
-            up = down = block
+    def both(block, *passing):
+        up = jnp.concatenate([block] + [pair[0][:half] for pair in passing], axis=0) if passing else block
+        down = jnp.concatenate([block] + [pair[1][half:n] for pair in passing], axis=0) if passing else block
         return shift(up, "y", 1), shift(down, "y", -1)
 
-    def join(block, up, down):
-        return jnp.concatenate([block, up[:half]], axis=0), jnp.concatenate([block, down[half:n]], axis=0)
-
     left = left.reshape(C * rank, Y * Z, -1).transpose(1, 0, 2)
-    left = lax.all_to_all(left, ("y", "z"), split_axis=0, concat_axis=0, tiled=True)
+    left = jnp.concatenate([left, left], axis=0)
+    left = lax.all_to_all(left, ("h", "y", "z"), split_axis=0, concat_axis=0, tiled=True)
     own, = event(own)
     up0, down0 = both(own)
     z1 = shift(own, "z", 1)
     z1, down0, up0 = event(z1, down0, up0)
 
-    up1, down1 = join(z1, up0, down0)
-    up1 = shift(up1, "y", 1)
+    up1, down1 = both(z1)
     z2 = shift(z1, "z", 1)
-    left, down1 = event(left, down1)
-    down1 = shift(down1, "y", -1)
-    left_h = shift(left, "h", 1)
-    z2, left, left_h, down1, up1 = event(z2, left, left_h, down1, up1)
-
-    up2, down2 = both(z2, up1, down1)
+    left, = event(left)
+    left_1 = shift(left, "x", 1)
+    z2, left, left_1, down1, up1 = event(z2, left, left_1, down1, up1)
+
+    up2, down2 = both(z2, (up1, down1), (up0, down0))
     z3 = shift(z2, "z", 1)
-    left = jnp.stack([left, left_h])
-    left_1, left_3 = shift(left, "x", 1), shift(left, "x", 3)
-    z3, left, left_1, left_3, down2, up2 = event(z3, left, left_1, left_3, down2, up2)
-
-    up3, down3 = both(z3, up2, down2)
-    far3 = shift(jnp.concatenate([up1[n:], down1[n:]], axis=0), "z", 3)
-    left, left_last = arrange_left(place, [left, left_1, shift(left, "x", 2), left_3])
-
-    def slot(block, up, down, up_next, down_next):
-        return [(block, 0, n), (up, 0, n), (down, 0, n), (up_next, n, half), (down_next, n, half)]
-
-    pieces = slot(own, up0, down0, up1, down1) + slot(z1, up1, down1, up2, down2)
+    left_2, left_3 = shift(left, "x", 2), shift(left, "x", 3)
+    z3, left_2, left_3, down2, up2 = event(z3, left_2, left_3, down2, up2)
+
+    up3, down3 = both(z3, (up2, down2))
+    far3 = shift(jnp.concatenate([up2[n + half :], down2[n + half :]], axis=0), "z", 3)
+    left, left_last = arrange_left(place, [left, left_1, left_2, left_3])
+
+    def slot(block, up, down, row):
+        return [(block, 0, n), (up, 0, n), (down, 0, n), (up2, row, half), (down2, row, half)]
+
+    pieces = slot(own, up0, down0, n + half) + slot(z1, up1, down1, n)
     pieces += [(part, 0, n) for part in (z2, up2, down2, z3)]
     total = multiply_part(left, pieces, "multiply_0")
     far3, down3, up3, total = event(far3, down3, up3, total)

time: 89 us -> 87.6 us (0.984)
  starting transfers between devices: 44.3 us -> 35.4 us
  waiting for transfers between devices: 30.2 us -> 37.8 us
    ppermute x21 -> x20, starting transfers between devices: 37.5 us -> 25.4 us  [shift(): return lax.ppermute(x, axis, [(i, (i + by) % n) for i in range(n)])]
    all_to_all x1, waiting for transfers between devices: 1.92 us -> 6.9 us  [shards(): lax.all_to_all(left, ('h', 'y', 'z'), split_axis=0, concat_axis=0, tiled=...]
    all_to_all x1, starting transfers between devices: 6.76 us -> 10.1 us  [shards(): lax.all_to_all(left, ('h', 'y', 'z'), split_axis=0, concat_axis=0, tiled=...]
    ppermute x21 -> x20, waiting for transfers between devices: 28.3 us -> 30.9 us  [shift(): return lax.ppermute(x, axis, [(i, (i + by) % n) for i in range(n)])]
  transfers between devices with their start and end apart: 22 -> 21, of which waited for: 11 -> 14; matrix products, arithmetic and copies ran while one was open for 4% -> 4% of each run, Pallas kernels for 8% -> 8%
where the time goes in v6:
time: 87.6 us; the launch traced here: 87.4 us
  waiting for transfers between devices  37.8 us (43%)
  starting transfers between devices  35.4 us (40%)
  Pallas kernels  8.41 us (10%)
  other arithmetic  3.33 us (4%)
  between operations  2.25 us (3%)
    ppermute x20, waiting for transfers between devices, shift(): return lax.ppermute(x, axis, [(i, (i + by) % n) for i in range(n)])  30.9 us
    ppermute x20, starting transfers between devices, shift(): return lax.ppermute(x, axis, [(i, (i + by) % n) for i in range(n)])  25.4 us
    all_to_all x1, starting transfers between devices, shards(): lax.all_to_all(left, ('h', 'y', 'z'), split_axis=0, concat_axis=0, tiled=...  10.1 us
    all_to_all x1, waiting for transfers between devices, shards(): lax.all_to_all(left, ('h', 'y', 'z'), split_axis=0, concat_axis=0, tiled=...  6.9 us
    pallas_call x3, Pallas kernels, put(): pl.pallas_call(functools.partial(put_kernel, got, at), out_shape=(shape,...  3.1 us
    pallas_call x1, Pallas kernels, multiply_part(): pl.pallas_call(functools.partial(part_kernel, ranges, 256), out_shape=jax...  3.02 us
  transfers between devices with their start and end apart: 21, of which 14 were waited for; matrix products, arithmetic and copies ran while one was open for 4% of the time, Pallas kernels for 8%

profile of v6, /device:TPU:1, one launch (start us, length us, event | category | flops | bytes accessed | tf_op | source)
XLA Modules:
  0.0 87.4 jit_solution(11011663452303453515)
XLA Ops:
  0.6 3.3 %collective-permute-start = (bf16[8,4,3584]{2,1,0:T(4,128)(2,1)}, bf16[8,4,3584]{2,1,0:T(4,128)(2,1)S(1)}, u32[]{:S(2)}, u32[]{:S(2)}) collective-permute-start(bf16[8,4,3584]{2,1,0:T(4,128)(2,1)} %param.8), channel_id=1, source_target_pairs={{0,8},{8,0},{1,9},{9,1},{2,10},{10,2},{3,11},{11,3},{4,12},{12,4},... | collective-permute-start | bytes 688136 | tf_op jit(solution)/shard_map/ppermute | solution.py:22
  8.2 2.6 %collective-permute-start.3 = (bf16[64,3584]{1,0:T(8,128)(2,1)S(1)}, bf16[64,3584]{1,0:T(8,128)(2,1)S(1)}, u32[]{:S(2)}, u32[]{:S(2)}) collective-permute-start(bf16[64,3584]{1,0:T(8,128)(2,1)S(1)} %maximum_bitcast_fusion.refs_0_), channel_id=1, source_target_pairs={{0,192},{64,0},{128,64},{192,128},{1,193},{65,1},{129,65},{193,129... | collective-permute-start | bytes 1376264 | tf_op jit(solution)/shard_map/ppermute | solution.py:22
  11.7 10.1 %all-to-all-start = ((bf16[32,8,512]{2,1,0:T(8,128)(2,1)}), bf16[32,8,512]{2,1,0:T(8,128)(2,1)S(1)}, u32[]{:S(2)}, u32[]{:S(2)}) async-start(bf16[32,8,512]{2,1,0:T(8,128)(2,1)} %pad_maximum_fusion.5), calls=%async_computation | async-start | bytes 524288 | tf_op jit(solution)/shard_map/all_to_all | solution.py:205
  22.1 1.4 %collective-permute-done.4.refs_1_ = bf16[64,3584]{1,0:T(8,128)(2,1)S(1)} collective-permute-done((bf16[64,3584]{1,0:T(8,128)(2,1)S(1)}, bf16[64,3584]{1,0:T(8,128)(2,1)S(1)}, u32[]{:S(2)}, u32[]{:S(2)}) %collective-permute-start.4) | collective-permute-done | bytes 458784 | tf_op jit(solution)/shard_map/ppermute | solution.py:22
  23.5 1.6 %collective-permute-start.5 = (bf16[64,3584]{1,0:T(8,128)(2,1)S(1)}, bf16[64,3584]{1,0:T(8,128)(2,1)S(1)}, u32[]{:S(2)}, u32[]{:S(2)}) collective-permute-start(bf16[64,3584]{1,0:T(8,128)(2,1)S(1)} %collective-permute-done.2.refs_5_), channel_id=1, source_target_pairs={{0,16},{16,32},{32,48},{48,0},{1,17},{17,33},{33,49},{49,1},{2,18}... | collective-permute-start | bytes 1376264 | tf_op jit(solution)/shard_map/ppermute | solution.py:22
  25.5 1.1 %collective-permute-start.9 = (bf16[64,3584]{1,0:T(8,128)(2,1)S(1)}, bf16[64,3584]{1,0:T(8,128)(2,1)S(1)}, u32[]{:S(2)}, u32[]{:S(2)}) collective-permute-start(bf16[64,3584]{1,0:T(8,128)(2,1)S(1)} %collective-permute-done.2.refs_5_), channel_id=1, source_target_pairs={{0,64},{64,128},{128,192},{192,0},{1,65},{65,129},{129,193},{193,1... | collective-permute-start | bytes 1376264 | tf_op jit(solution)/shard_map/ppermute | solution.py:22
  26.6 6.9 %all-to-all-done.refs_0_ = bf16[32,8,512]{2,1,0:T(8,128)(2,1)S(1)} async-done(((bf16[32,8,512]{2,1,0:T(8,128)(2,1)}), bf16[32,8,512]{2,1,0:T(8,128)(2,1)S(1)}, u32[]{:S(2)}, u32[]{:S(2)}) %all-to-all-start) | async-done | bytes 262176 | tf_op jit(solution)/shard_map/all_to_all | solution.py:205
  33.5 1.2 %collective-permute-start.7 = (bf16[32,8,512]{2,1,0:T(8,128)(2,1)S(1)}, bf16[32,8,512]{2,1,0:T(8,128)(2,1)S(1)}, u32[]{:S(2)}, u32[]{:S(2)}) collective-permute-start(bf16[32,8,512]{2,1,0:T(8,128)(2,1)S(1)} %all-to-all-done.refs_0_), channel_id=1, source_target_pairs={{0,1},{1,2},{2,3},{3,0},{4,5},{5,6},{6,7},{7,4},{8,9},{9,10},{10,1... | collective-permute-start | bytes 786440 | tf_op jit(solution)/shard_map/ppermute | solution.py:22
  34.7 5.5 %collective-permute-done.7.refs_1_ = bf16[32,8,512]{2,1,0:T(8,128)(2,1)S(1)} collective-permute-done((bf16[32,8,512]{2,1,0:T(8,128)(2,1)S(1)}, bf16[32,8,512]{2,1,0:T(8,128)(2,1)S(1)}, u32[]{:S(2)}, u32[]{:S(2)}) %collective-permute-start.7) | collective-permute-done | bytes 262176 | tf_op jit(solution)/shard_map/ppermute | solution.py:22
  40.8 1.7 %collective-permute-start.13 = (bf16[128,3584]{1,0:T(8,128)(2,1)S(1)}, bf16[128,3584]{1,0:T(8,128)(2,1)S(1)}, u32[]{:S(2)}, u32[]{:S(2)}) collective-permute-start(bf16[128,3584]{1,0:T(8,128)(2,1)S(1)} %get-tuple-element.103), channel_id=1, source_target_pairs={{0,192},{64,0},{128,64},{192,128},{1,193},{65,1},{129,65},{193,129... | collective-permute-start | bytes 2752520 | tf_op jit(solution)/shard_map/ppermute | solution.py:22
  42.7 2.7 %collective-permute-start.11 = (bf16[32,8,512]{2,1,0:T(8,128)(2,1)S(1)}, bf16[32,8,512]{2,1,0:T(8,128)(2,1)S(1)}, u32[]{:S(2)}, u32[]{:S(2)}) collective-permute-start(bf16[32,8,512]{2,1,0:T(8,128)(2,1)S(1)} %all-to-all-done.refs_0_), channel_id=1, source_target_pairs={{0,2},{1,3},{2,0},{3,1},{4,6},{5,7},{6,4},{7,5},{8,10},{9,11},{10,... | collective-permute-start | bytes 786440 | tf_op jit(solution)/shard_map/ppermute | solution.py:22
  46.3 3.1 %collective-permute-done.11.refs_2_ = bf16[32,8,512]{2,1,0:T(8,128)(2,1)S(1)} collective-permute-done((bf16[32,8,512]{2,1,0:T(8,128)(2,1)S(1)}, bf16[32,8,512]{2,1,0:T(8,128)(2,1)S(1)}, u32[]{:S(2)}, u32[]{:S(2)}) %collective-permute-start.11) | collective-permute-done | bytes 262176 | tf_op jit(solution)/shard_map/ppermute | solution.py:22
  49.4 5.6 %collective-permute-done.12.refs_3_ = bf16[32,8,512]{2,1,0:T(8,128)(2,1)S(1)} collective-permute-done((bf16[32,8,512]{2,1,0:T(8,128)(2,1)S(1)}, bf16[32,8,512]{2,1,0:T(8,128)(2,1)S(1)}, u32[]{:S(2)}, u32[]{:S(2)}) %collective-permute-start.12) | collective-permute-done | bytes 262176 | tf_op jit(solution)/shard_map/ppermute | solution.py:22
  55.0 4.2 %collective-permute-done.13.refs_4_ = bf16[128,3584]{1,0:T(8,128)(2,1)S(1)} collective-permute-done((bf16[128,3584]{1,0:T(8,128)(2,1)S(1)}, bf16[128,3584]{1,0:T(8,128)(2,1)S(1)}, u32[]{:S(2)}, u32[]{:S(2)}) %collective-permute-start.13) | collective-permute-done | bytes 917536 | tf_op jit(solution)/shard_map/ppermute | solution.py:22
  59.2 3.1 %collective-permute-done.14.refs_3_ = bf16[128,3584]{1,0:T(8,128)(2,1)S(1)} collective-permute-done((bf16[128,3584]{1,0:T(8,128)(2,1)S(1)}, bf16[128,3584]{1,0:T(8,128)(2,1)S(1)}, u32[]{:S(2)}, u32[]{:S(2)}) %collective-permute-start.14) | collective-permute-done | bytes 917536 | tf_op jit(solution)/shard_map/ppermute | solution.py:22
  63.1 1.2 %collective-permute-start.17 = (bf16[96,3584]{1,0:T(8,128)(2,1)S(1)}, bf16[96,3584]{1,0:T(8,128)(2,1)S(1)}, u32[]{:S(2)}, u32[]{:S(2)}) collective-permute-start(bf16[96,3584]{1,0:T(8,128)(2,1)S(1)} %get-tuple-element.100), channel_id=1, source_target_pairs={{0,64},{64,128},{128,192},{192,0},{1,65},{65,129},{129,193},{193,1... | collective-permute-start | bytes 2064392 | tf_op jit(solution)/shard_map/ppermute | solution.py:22
  64.3 2.0 %collective-permute-start.15 = (bf16[64,3584]{1,0:T(8,128)(2,1)S(1)}, bf16[64,3584]{1,0:T(8,128)(2,1)S(1)}, u32[]{:S(2)}, u32[]{:S(2)}) collective-permute-start(bf16[64,3584]{1,0:T(8,128)(2,1)S(1)} %pad_maximum_fusion.4), channel_id=1, source_target_pairs={{0,48},{16,0},{32,16},{48,32},{1,49},{17,1},{33,17},{49,33},{2,50}... | collective-permute-start | bytes 1376264 | tf_op jit(solution)/shard_map/ppermute | solution.py:22
  66.3 1.0 %arrange_left.1 = (bf16[512,768]{1,0:T(8,128)(2,1)S(1)}, bf16[512,256]{1,0:T(8,128)(2,1)S(1)}) custom-call(s32[3]{0:T(128)S(1)} %pad_add_fusion.place_ref, bf16[32,8,512]{2,1,0:T(8,128)(2,1)S(1)} %all-to-all-done.refs_0_, bf16[32,8,512]{2,1,0:T(8,128)(2,1)S(1)} %collective-permute-done.7.refs_1_, bf16[32,8,512]{2,1,0:T(8,128)(2,1)S(1)} %collective-permute-done.11.refs_2_, ...), custom_call_target="tpu_custom_call" | custom-call | bytes 6291456 | tf_op jit(solution)/shard_map/arrange_left/pallas_call | solution.py:48
  67.3 3.0 %multiply_0.1.total_ref = f32[512,3584]{1,0:T(8,128)S(1)} custom-call(bf16[512,768]{1,0:T(8,128)(2,1)S(1)} %get-tuple-element.74.left_ref, bf16[64,3584]{1,0:T(8,128)(2,1)S(1)} %maximum_bitcast_fusion.refs_0_, bf16[64,3584]{1,0:T(8,128)(2,1)S(1)} %collective-permute-done.4.refs_1_, bf16[64,3584]{1,0:T(8,128)(2,1)S(1)} %collective-permute-done.3.refs_2_, ...), custom_call_target="tpu_custom_call" | custom-call | flops 2818572288 | bytes 1048576 | tf_op jit(solution)/shard_map/multiply_0/pallas_call | solution.py:82
  70.3 1.7 %collective-permute-done.15.refs_2_ = bf16[64,3584]{1,0:T(8,128)(2,1)S(1)} collective-permute-done((bf16[64,3584]{1,0:T(8,128)(2,1)S(1)}, bf16[64,3584]{1,0:T(8,128)(2,1)S(1)}, u32[]{:S(2)}, u32[]{:S(2)}) %collective-permute-start.15) | collective-permute-done | bytes 458784 | tf_op jit(solution)/shard_map/ppermute | solution.py:22
  72.0 3.6 %collective-permute-done.16.refs_1_ = bf16[96,3584]{1,0:T(8,128)(2,1)S(1)} collective-permute-done((bf16[96,3584]{1,0:T(8,128)(2,1)S(1)}, bf16[96,3584]{1,0:T(8,128)(2,1)S(1)}, u32[]{:S(2)}, u32[]{:S(2)}) %collective-permute-start.16) | collective-permute-done | bytes 688160 | tf_op jit(solution)/shard_map/ppermute | solution.py:22
  75.6 1.5 %collective-permute-done.17.refs_0_ = bf16[96,3584]{1,0:T(8,128)(2,1)S(1)} collective-permute-done((bf16[96,3584]{1,0:T(8,128)(2,1)S(1)}, bf16[96,3584]{1,0:T(8,128)(2,1)S(1)}, u32[]{:S(2)}, u32[]{:S(2)}) %collective-permute-start.17) | collective-permute-done | bytes 688160 | tf_op jit(solution)/shard_map/ppermute | solution.py:22
  77.7 5.1 %collective-permute-start.19 = (bf16[256,1792]{1,0:T(8,128)(2,1)S(1)}, bf16[256,1792]{1,0:T(8,128)(2,1)S(1)}, u32[]{:S(2)}, u32[]{:S(2)}) collective-permute-start(bf16[256,1792]{1,0:T(8,128)(2,1)S(1)} %get-tuple-element.83), channel_id=1, source_target_pairs={{0,8},{8,0},{1,9},{9,1},{2,10},{10,2},{3,11},{11,3},{4,12},{12,4},... | collective-permute-start | bytes 2752520 | tf_op jit(solution)/shard_map/ppermute | solution.py:22
  83.6 1.2 %put_0_0.1 = (bf16[256,3584]{1,0:T(8,128)(2,1)}, bf16[256,3584]{1,0:T(8,128)(2,1)}) custom-call(s32[1]{0:T(128)} %bitcast.6.core_ref, bf16[256,3584]{1,0:T(8,128)(2,1)S(1)} %multiply_2.1.part_ref), custom_call_target="tpu_custom_call" | custom-call | bytes 4194304 | tf_op jit(solution)/shard_map/put_0_0/pallas_call | solution.py:145
  (41 shorter events, 10.5 us)
Async XLA Ops:
  0.6 5.8 %collective-permute-start = (bf16[8,4,3584]{2,1,0:T(4,128)(2,1)}, bf16[8,4,3584]{2,1,0:T(4,128)(2,1)S(1)}, u32[]{:S(2)}, u32[]{:S(2)}) collective-permute-start(bf16[8,4,3584]{2,1,0:T(4,128)(2,1)} %param.8), channel_id=1, source_target_pairs={{0,8},{8,0},{1,9},{9,1},{2,10},{10,2},{3,11},{11,3},{4,12},{12,4},... | collective-permute-start | bytes 688136 | tf_op jit(solution)/shard_map/ppermute | solution.py:22
  4.0 2.4 %collective-permute-start.1 = (bf16[8,4,3584]{2,1,0:T(4,128)(2,1)}, bf16[8,4,3584]{2,1,0:T(4,128)(2,1)S(1)}, u32[]{:S(2)}, u32[]{:S(2)}) collective-permute-start(bf16[8,4,3584]{2,1,0:T(4,128)(2,1)} %param.9), channel_id=1, source_target_pairs={{0,8},{8,0},{1,9},{9,1},{2,10},{10,2},{3,11},{11,3},{4,12},{12,4},... | collective-permute-start | bytes 688136 | tf_op jit(solution)/shard_map/ppermute | solution.py:22
  6.4 4.4 %collective-permute-start.6 = (bf16[4,8192]{1,0:T(4,128)(2,1)S(1)}, bf16[4,8192]{1,0:T(4,128)(2,1)S(1)}, u32[]{:S(2)}, u32[]{:S(2)}) collective-permute-start(bf16[4,8192]{1,0:T(4,128)(2,1)S(1)} %get-tuple-element.56), channel_id=1, source_target_pairs={{0,8},{8,0},{1,9},{9,1},{2,10},{10,2},{3,11},{11,3},{4,12},{12,4},... | collective-permute-start | bytes 196616 | tf_op jit(solution)/shard_map/ppermute | solution.py:22
  8.1 14.0 %collective-permute-start.2 = (bf16[64,3584]{1,0:T(8,128)(2,1)S(1)}, bf16[64,3584]{1,0:T(8,128)(2,1)S(1)}, u32[]{:S(2)}, u32[]{:S(2)}) collective-permute-start(bf16[64,3584]{1,0:T(8,128)(2,1)S(1)} %maximum_bitcast_fusion.refs_0_), channel_id=1, source_target_pairs={{0,16},{16,32},{32,48},{48,0},{1,17},{17,33},{33,49},{49,1},{2,18}... | collective-permute-start | bytes 1376264 | tf_op jit(solution)/shard_map/ppermute | solution.py:22
  8.2 13.9 %collective-permute-start.3 = (bf16[64,3584]{1,0:T(8,128)(2,1)S(1)}, bf16[64,3584]{1,0:T(8,128)(2,1)S(1)}, u32[]{:S(2)}, u32[]{:S(2)}) collective-permute-start(bf16[64,3584]{1,0:T(8,128)(2,1)S(1)} %maximum_bitcast_fusion.refs_0_), channel_id=1, source_target_pairs={{0,192},{64,0},{128,64},{192,128},{1,193},{65,1},{129,65},{193,129... | collective-permute-start | bytes 1376264 | tf_op jit(solution)/shard_map/ppermute | solution.py:22
  10.8 12.6 %collective-permute-start.4 = (bf16[64,3584]{1,0:T(8,128)(2,1)S(1)}, bf16[64,3584]{1,0:T(8,128)(2,1)S(1)}, u32[]{:S(2)}, u32[]{:S(2)}) collective-permute-start(bf16[64,3584]{1,0:T(8,128)(2,1)S(1)} %maximum_bitcast_fusion.refs_0_), channel_id=1, source_target_pairs={{0,64},{64,128},{128,192},{192,0},{1,65},{65,129},{129,193},{193,1... | collective-permute-start | bytes 1376264 | tf_op jit(solution)/shard_map/ppermute | solution.py:22
  11.7 21.8 %all-to-all-start = ((bf16[32,8,512]{2,1,0:T(8,128)(2,1)}), bf16[32,8,512]{2,1,0:T(8,128)(2,1)S(1)}, u32[]{:S(2)}, u32[]{:S(2)}) async-start(bf16[32,8,512]{2,1,0:T(8,128)(2,1)} %pad_maximum_fusion.5), calls=%async_computation | async-start | bytes 524288 | tf_op jit(solution)/shard_map/all_to_all | solution.py:205
  23.5 17.1 %collective-permute-start.5 = (bf16[64,3584]{1,0:T(8,128)(2,1)S(1)}, bf16[64,3584]{1,0:T(8,128)(2,1)S(1)}, u32[]{:S(2)}, u32[]{:S(2)}) collective-permute-start(bf16[64,3584]{1,0:T(8,128)(2,1)S(1)} %collective-permute-done.2.refs_5_), channel_id=1, source_target_pairs={{0,16},{16,32},{32,48},{48,0},{1,17},{17,33},{33,49},{49,1},{2,18}... | collective-permute-start | bytes 1376264 | tf_op jit(solution)/shard_map/ppermute | solution.py:22
  25.1 15.5 %collective-permute-start.8 = (bf16[64,3584]{1,0:T(8,128)(2,1)S(1)}, bf16[64,3584]{1,0:T(8,128)(2,1)S(1)}, u32[]{:S(2)}, u32[]{:S(2)}) collective-permute-start(bf16[64,3584]{1,0:T(8,128)(2,1)S(1)} %collective-permute-done.2.refs_5_), channel_id=1, source_target_pairs={{0,192},{64,0},{128,64},{192,128},{1,193},{65,1},{129,65},{193,129... | collective-permute-start | bytes 1376264 | tf_op jit(solution)/shard_map/ppermute | solution.py:22
  25.5 15.1 %collective-permute-start.9 = (bf16[64,3584]{1,0:T(8,128)(2,1)S(1)}, bf16[64,3584]{1,0:T(8,128)(2,1)S(1)}, u32[]{:S(2)}, u32[]{:S(2)}) collective-permute-start(bf16[64,3584]{1,0:T(8,128)(2,1)S(1)} %collective-permute-done.2.refs_5_), channel_id=1, source_target_pairs={{0,64},{64,128},{128,192},{192,0},{1,65},{65,129},{129,193},{193,1... | collective-permute-start | bytes 1376264 | tf_op jit(solution)/shard_map/ppermute | solution.py:22
  33.5 6.7 %collective-permute-start.7 = (bf16[32,8,512]{2,1,0:T(8,128)(2,1)S(1)}, bf16[32,8,512]{2,1,0:T(8,128)(2,1)S(1)}, u32[]{:S(2)}, u32[]{:S(2)}) collective-permute-start(bf16[32,8,512]{2,1,0:T(8,128)(2,1)S(1)} %all-to-all-done.refs_0_), channel_id=1, source_target_pairs={{0,1},{1,2},{2,3},{3,0},{4,5},{5,6},{6,7},{7,4},{8,9},{9,10},{10,1... | collective-permute-start | bytes 786440 | tf_op jit(solution)/shard_map/ppermute | solution.py:22
  40.8 18.4 %collective-permute-start.13 = (bf16[128,3584]{1,0:T(8,128)(2,1)S(1)}, bf16[128,3584]{1,0:T(8,128)(2,1)S(1)}, u32[]{:S(2)}, u32[]{:S(2)}) collective-permute-start(bf16[128,3584]{1,0:T(8,128)(2,1)S(1)} %get-tuple-element.103), channel_id=1, source_target_pairs={{0,192},{64,0},{128,64},{192,128},{1,193},{65,1},{129,65},{193,129... | collective-permute-start | bytes 2752520 | tf_op jit(solution)/shard_map/ppermute | solution.py:22
  42.5 19.8 %collective-permute-start.14 = (bf16[128,3584]{1,0:T(8,128)(2,1)S(1)}, bf16[128,3584]{1,0:T(8,128)(2,1)S(1)}, u32[]{:S(2)}, u32[]{:S(2)}) collective-permute-start(bf16[128,3584]{1,0:T(8,128)(2,1)S(1)} %get-tuple-element.102), channel_id=1, source_target_pairs={{0,64},{64,128},{128,192},{192,0},{1,65},{65,129},{129,193},{193,1... | collective-permute-start | bytes 2752520 | tf_op jit(solution)/shard_map/ppermute | solution.py:22
  42.5 12.5 %collective-permute-start.10 = (bf16[64,3584]{1,0:T(8,128)(2,1)S(1)}, bf16[64,3584]{1,0:T(8,128)(2,1)S(1)}, u32[]{:S(2)}, u32[]{:S(2)}) collective-permute-start(bf16[64,3584]{1,0:T(8,128)(2,1)S(1)} %collective-permute-done.5.refs_8_), channel_id=1, source_target_pairs={{0,16},{16,32},{32,48},{48,0},{1,17},{17,33},{33,49},{49,1},{2,18}... | collective-permute-start | bytes 1376264 | tf_op jit(solution)/shard_map/ppermute | solution.py:22
  42.7 6.7 %collective-permute-start.11 = (bf16[32,8,512]{2,1,0:T(8,128)(2,1)S(1)}, bf16[32,8,512]{2,1,0:T(8,128)(2,1)S(1)}, u32[]{:S(2)}, u32[]{:S(2)}) collective-permute-start(bf16[32,8,512]{2,1,0:T(8,128)(2,1)S(1)} %all-to-all-done.refs_0_), channel_id=1, source_target_pairs={{0,2},{1,3},{2,0},{3,1},{4,6},{5,7},{6,4},{7,5},{8,10},{9,11},{10,... | collective-permute-start | bytes 786440 | tf_op jit(solution)/shard_map/ppermute | solution.py:22
  45.4 9.6 %collective-permute-start.12 = (bf16[32,8,512]{2,1,0:T(8,128)(2,1)S(1)}, bf16[32,8,512]{2,1,0:T(8,128)(2,1)S(1)}, u32[]{:S(2)}, u32[]{:S(2)}) collective-permute-start(bf16[32,8,512]{2,1,0:T(8,128)(2,1)S(1)} %all-to-all-done.refs_0_), channel_id=1, source_target_pairs={{0,3},{1,0},{2,1},{3,2},{4,7},{5,4},{6,5},{7,6},{8,11},{9,8},{10,9... | collective-permute-start | bytes 786440 | tf_op jit(solution)/shard_map/ppermute | solution.py:22
  62.5 13.1 %collective-permute-start.16 = (bf16[96,3584]{1,0:T(8,128)(2,1)S(1)}, bf16[96,3584]{1,0:T(8,128)(2,1)S(1)}, u32[]{:S(2)}, u32[]{:S(2)}) collective-permute-start(bf16[96,3584]{1,0:T(8,128)(2,1)S(1)} %get-tuple-element.101), channel_id=1, source_target_pairs={{0,192},{64,0},{128,64},{192,128},{1,193},{65,1},{129,65},{193,129... | collective-permute-start | bytes 2064392 | tf_op jit(solution)/shard_map/ppermute | solution.py:22
  63.1 14.0 %collective-permute-start.17 = (bf16[96,3584]{1,0:T(8,128)(2,1)S(1)}, bf16[96,3584]{1,0:T(8,128)(2,1)S(1)}, u32[]{:S(2)}, u32[]{:S(2)}) collective-permute-start(bf16[96,3584]{1,0:T(8,128)(2,1)S(1)} %get-tuple-element.100), channel_id=1, source_target_pairs={{0,64},{64,128},{128,192},{192,0},{1,65},{65,129},{129,193},{193,1... | collective-permute-start | bytes 2064392 | tf_op jit(solution)/shard_map/ppermute | solution.py:22
  64.3 7.7 %collective-permute-start.15 = (bf16[64,3584]{1,0:T(8,128)(2,1)S(1)}, bf16[64,3584]{1,0:T(8,128)(2,1)S(1)}, u32[]{:S(2)}, u32[]{:S(2)}) collective-permute-start(bf16[64,3584]{1,0:T(8,128)(2,1)S(1)} %pad_maximum_fusion.4), channel_id=1, source_target_pairs={{0,48},{16,0},{32,16},{48,32},{1,49},{17,1},{33,17},{49,33},{2,50}... | collective-permute-start | bytes 1376264 | tf_op jit(solution)/shard_map/ppermute | solution.py:22
  77.7 7.2 %collective-permute-start.19 = (bf16[256,1792]{1,0:T(8,128)(2,1)S(1)}, bf16[256,1792]{1,0:T(8,128)(2,1)S(1)}, u32[]{:S(2)}, u32[]{:S(2)}) collective-permute-start(bf16[256,1792]{1,0:T(8,128)(2,1)S(1)} %get-tuple-element.83), channel_id=1, source_target_pairs={{0,8},{8,0},{1,9},{9,1},{2,10},{10,2},{3,11},{11,3},{4,12},{12,4},... | collective-permute-start | bytes 2752520 | tf_op jit(solution)/shard_map/ppermute | solution.py:22
  82.9 3.4 %collective-permute-start.18 = (bf16[256,1792]{1,0:T(8,128)(2,1)S(1)}, bf16[256,1792]{1,0:T(8,128)(2,1)S(1)}, u32[]{:S(2)}, u32[]{:S(2)}) collective-permute-start(bf16[256,1792]{1,0:T(8,128)(2,1)S(1)} %get-tuple-element.82), channel_id=1, source_target_pairs={{0,8},{8,0},{1,9},{9,1},{2,10},{10,2},{3,11},{11,3},{4,12},{12,4},... | collective-permute-start | bytes 2752520 | tf_op jit(solution)/shard_map/ppermute | solution.py:22

commit v7 on v6

--- a/solution.py
+++ b/solution.py
@@ -195,10 +195,8 @@
     n = own.shape[0]
     half = n // 2
 
-    def both(block, *passing):
-        up = jnp.concatenate([block] + [pair[0][:half] for pair in passing], axis=0) if passing else block
-        down = jnp.concatenate([block] + [pair[1][half:n] for pair in passing], axis=0) if passing else block
-        return shift(up, "y", 1), shift(down, "y", -1)
+    def both(block):
+        return shift(block, "y", 1), shift(block, "y", -1)
 
     left = left.reshape(C * rank, Y * Z, -1).transpose(1, 0, 2)
     left = jnp.concatenate([left, left], axis=0)
@@ -214,20 +212,24 @@
     left_1 = shift(left, "x", 1)
     z2, left, left_1, down1, up1 = event(z2, left, left_1, down1, up1)
 
-    up2, down2 = both(z2, (up1, down1), (up0, down0))
-    z3 = shift(z2, "z", 1)
+    few = n // 4
+    up2 = shift(jnp.concatenate([z2[: n - few], up1[:half], up0[:half]], axis=0), "y", 1)
+    down2 = shift(jnp.concatenate([z2[few:], down1[half:], down0[half:]], axis=0), "y", -1)
+    z3 = shift(jnp.concatenate([z2, up1[n - few :], down1[:few]], axis=0), "z", 1)
     left_2, left_3 = shift(left, "x", 2), shift(left, "x", 3)
     z3, left_2, left_3, down2, up2 = event(z3, left_2, left_3, down2, up2)
 
-    up3, down3 = both(z3, (up2, down2))
-    far3 = shift(jnp.concatenate([up2[n + half :], down2[n + half :]], axis=0), "z", 3)
+    up3 = shift(jnp.concatenate([z3[:n], up2[:half]], axis=0), "y", 1)
+    down3 = shift(jnp.concatenate([z3[:n], down2[half - few : n - few]], axis=0), "y", -1)
+    row = n - few
+    far3 = shift(jnp.concatenate([up2[row + half :], down2[row + half :]], axis=0), "z", 3)
     left, left_last = arrange_left(place, [left, left_1, left_2, left_3])
 
-    def slot(block, up, down, row):
-        return [(block, 0, n), (up, 0, n), (down, 0, n), (up2, row, half), (down2, row, half)]
-
-    pieces = slot(own, up0, down0, n + half) + slot(z1, up1, down1, n)
-    pieces += [(part, 0, n) for part in (z2, up2, down2, z3)]
+    def slot(block, up, down, at):
+        return [(block, 0, n), (up, 0, n), (down, 0, n), (up2, at, half), (down2, at, half)]
+
+    pieces = slot(own, up0, down0, row + half) + slot(z1, up1, down1, row)
+    pieces += [(z2, 0, n), (up2, 0, row), (z3, n, few), (z3, n + few, few), (down2, 0, row), (z3, 0, n)]
     total = multiply_part(left, pieces, "multiply_0")
     far3, down3, up3, total = event(far3, down3, up3, total)
 

time: 87.6 us -> 85.7 us (0.978)
  waiting for transfers between devices: 37.8 us -> 30 us
  starting transfers between devices: 35.4 us -> 40 us
    ppermute x20, waiting for transfers between devices: 30.9 us -> 23.1 us  [shift(): return lax.ppermute(x, axis, [(i, (i + by) % n) for i in range(n)])]
    ppermute x20, starting transfers between devices: 25.4 us -> 29.9 us  [shift(): return lax.ppermute(x, axis, [(i, (i + by) % n) for i in range(n)])]
  transfers between devices with their start and end apart: 21 -> 21, of which waited for: 14 -> 13; matrix products, arithmetic and copies ran while one was open for 4% -> 4% of each run, Pallas kernels for 8% -> 8%
where the time goes in v7:
time: 85.7 us; the launch traced here: 85 us
  starting transfers between devices  40 us (47%)
  waiting for transfers between devices  30 us (35%)
  Pallas kernels  8.41 us (10%)
  other arithmetic  3.36 us (4%)
  between operations  2.35 us (3%)
  local copies, waits for them, and re-layouts  0.94 us (1%)
    ppermute x20, starting transfers between devices, shift(): return lax.ppermute(x, axis, [(i, (i + by) % n) for i in range(n)])  29.9 us
    ppermute x20, waiting for transfers between devices, shift(): return lax.ppermute(x, axis, [(i, (i + by) % n) for i in range(n)])  23.1 us
    all_to_all x1, starting transfers between devices, shards(): lax.all_to_all(left, ('h', 'y', 'z'), split_axis=0, concat_axis=0, tiled=...  10.1 us
    all_to_all x1, waiting for transfers between devices, shards(): lax.all_to_all(left, ('h', 'y', 'z'), split_axis=0, concat_axis=0, tiled=...  6.9 us
    pallas_call x3, Pallas kernels, put(): pl.pallas_call(functools.partial(put_kernel, got, at), out_shape=(shape,...  3.1 us
    pallas_call x1, Pallas kernels, multiply_part(): pl.pallas_call(functools.partial(part_kernel, ranges, 256), out_shape=jax...  3.02 us
  transfers between devices with their start and end apart: 21, of which 13 were waited for; matrix products, arithmetic and copies ran while one was open for 4% of the time, Pallas kernels for 8%

profile of v7, /device:TPU:1, one launch (start us, length us, event | category | flops | bytes accessed | tf_op | source)
XLA Modules:
  0.0 85.0 jit_solution(12238821833700446711)
XLA Ops:
  0.6 3.3 %collective-permute-start = (bf16[8,4,3584]{2,1,0:T(4,128)(2,1)}, bf16[8,4,3584]{2,1,0:T(4,128)(2,1)S(1)}, u32[]{:S(2)}, u32[]{:S(2)}) collective-permute-start(bf16[8,4,3584]{2,1,0:T(4,128)(2,1)} %param.8), channel_id=1, source_target_pairs={{0,8},{8,0},{1,9},{9,1},{2,10},{10,2},{3,11},{11,3},{4,12},{12,4},... | collective-permute-start | bytes 688136 | tf_op jit(solution)/shard_map/ppermute | solution.py:22
  6.9 1.0 %broadcast_select_fusion = (bf16[4,8,3584]{2,1,0:T(8,128)(2,1)S(1)}, bf16[4,8,3584]{2,1,0:T(8,128)(2,1)S(1)}) fusion(bf16[4,8,3584]{2,1,0:T(8,128)(2,1)S(1)} %bitcast.25, bf16[4,8,3584]{2,1,0:T(8,128)(2,1)} %bitcast.24, pred[]{:T(512)S(6)} %eq.3, bf16[4,8,3584]{2,1,0:T(8,128)(2,1)} %bitcast.23, bf16[4,8,3584]{2,1,0:T(8,128)(2,1)S(1)} %bitcast.26), kind=kLoop, calls=%fused_computation.8 | loop fusion | flops 229376 | bytes 1376257 | tf_op jit(solution)/shard_map/jit(_where)/select_n | solution.py:181
  8.2 2.6 %collective-permute-start.3 = (bf16[64,3584]{1,0:T(8,128)(2,1)S(1)}, bf16[64,3584]{1,0:T(8,128)(2,1)S(1)}, u32[]{:S(2)}, u32[]{:S(2)}) collective-permute-start(bf16[64,3584]{1,0:T(8,128)(2,1)S(1)} %maximum_bitcast_fusion.refs_0_), channel_id=1, source_target_pairs={{0,192},{64,0},{128,64},{192,128},{1,193},{65,1},{129,65},{193,129... | collective-permute-start | bytes 1376264 | tf_op jit(solution)/shard_map/ppermute | solution.py:22
  11.7 10.1 %all-to-all-start = ((bf16[32,8,512]{2,1,0:T(8,128)(2,1)}), bf16[32,8,512]{2,1,0:T(8,128)(2,1)S(1)}, u32[]{:S(2)}, u32[]{:S(2)}) async-start(bf16[32,8,512]{2,1,0:T(8,128)(2,1)} %pad_maximum_fusion.6), calls=%async_computation | async-start | bytes 524288 | tf_op jit(solution)/shard_map/all_to_all | solution.py:203
  22.1 1.4 %collective-permute-done.4.refs_1_ = bf16[64,3584]{1,0:T(8,128)(2,1)S(1)} collective-permute-done((bf16[64,3584]{1,0:T(8,128)(2,1)S(1)}, bf16[64,3584]{1,0:T(8,128)(2,1)S(1)}, u32[]{:S(2)}, u32[]{:S(2)}) %collective-permute-start.4) | collective-permute-done | bytes 458784 | tf_op jit(solution)/shard_map/ppermute | solution.py:22
  23.5 1.6 %collective-permute-start.5 = (bf16[64,3584]{1,0:T(8,128)(2,1)S(1)}, bf16[64,3584]{1,0:T(8,128)(2,1)S(1)}, u32[]{:S(2)}, u32[]{:S(2)}) collective-permute-start(bf16[64,3584]{1,0:T(8,128)(2,1)S(1)} %collective-permute-done.2.refs_5_), channel_id=1, source_target_pairs={{0,16},{16,32},{32,48},{48,0},{1,17},{17,33},{33,49},{49,1},{2,18}... | collective-permute-start | bytes 1376264 | tf_op jit(solution)/shard_map/ppermute | solution.py:22
  25.5 1.0 %collective-permute-start.9 = (bf16[64,3584]{1,0:T(8,128)(2,1)S(1)}, bf16[64,3584]{1,0:T(8,128)(2,1)S(1)}, u32[]{:S(2)}, u32[]{:S(2)}) collective-permute-start(bf16[64,3584]{1,0:T(8,128)(2,1)S(1)} %collective-permute-done.2.refs_5_), channel_id=1, source_target_pairs={{0,64},{64,128},{128,192},{192,0},{1,65},{65,129},{129,193},{193,1... | collective-permute-start | bytes 1376264 | tf_op jit(solution)/shard_map/ppermute | solution.py:22
  26.6 6.9 %all-to-all-done.refs_0_ = bf16[32,8,512]{2,1,0:T(8,128)(2,1)S(1)} async-done(((bf16[32,8,512]{2,1,0:T(8,128)(2,1)}), bf16[32,8,512]{2,1,0:T(8,128)(2,1)S(1)}, u32[]{:S(2)}, u32[]{:S(2)}) %all-to-all-start) | async-done | bytes 262176 | tf_op jit(solution)/shard_map/all_to_all | solution.py:203
  33.5 1.2 %collective-permute-start.7 = (bf16[32,8,512]{2,1,0:T(8,128)(2,1)S(1)}, bf16[32,8,512]{2,1,0:T(8,128)(2,1)S(1)}, u32[]{:S(2)}, u32[]{:S(2)}) collective-permute-start(bf16[32,8,512]{2,1,0:T(8,128)(2,1)S(1)} %all-to-all-done.refs_0_), channel_id=1, source_target_pairs={{0,1},{1,2},{2,3},{3,0},{4,5},{5,6},{6,7},{7,4},{8,9},{9,10},{10,1... | collective-permute-start | bytes 786440 | tf_op jit(solution)/shard_map/ppermute | solution.py:22
  34.7 5.5 %collective-permute-done.7.refs_1_ = bf16[32,8,512]{2,1,0:T(8,128)(2,1)S(1)} collective-permute-done((bf16[32,8,512]{2,1,0:T(8,128)(2,1)S(1)}, bf16[32,8,512]{2,1,0:T(8,128)(2,1)S(1)}, u32[]{:S(2)}, u32[]{:S(2)}) %collective-permute-start.7) | collective-permute-done | bytes 262176 | tf_op jit(solution)/shard_map/ppermute | solution.py:22
  42.0 2.3 %collective-permute-start.13 = (bf16[112,3584]{1,0:T(8,128)(2,1)S(1)}, bf16[112,3584]{1,0:T(8,128)(2,1)S(1)}, u32[]{:S(2)}, u32[]{:S(2)}) collective-permute-start(bf16[112,3584]{1,0:T(8,128)(2,1)S(1)} %pad_maximum_fusion), channel_id=1, source_target_pairs={{0,192},{64,0},{128,64},{192,128},{1,193},{65,1},{129,65},{193,129... | collective-permute-start | bytes 2408456 | tf_op jit(solution)/shard_map/ppermute | solution.py:22
  44.7 2.7 %collective-permute-start.11 = (bf16[32,8,512]{2,1,0:T(8,128)(2,1)S(1)}, bf16[32,8,512]{2,1,0:T(8,128)(2,1)S(1)}, u32[]{:S(2)}, u32[]{:S(2)}) collective-permute-start(bf16[32,8,512]{2,1,0:T(8,128)(2,1)S(1)} %all-to-all-done.refs_0_), channel_id=1, source_target_pairs={{0,2},{1,3},{2,0},{3,1},{4,6},{5,7},{6,4},{7,5},{8,10},{9,11},{10,... | collective-permute-start | bytes 786440 | tf_op jit(solution)/shard_map/ppermute | solution.py:22
  48.3 3.1 %collective-permute-done.11.refs_2_ = bf16[32,8,512]{2,1,0:T(8,128)(2,1)S(1)} collective-permute-done((bf16[32,8,512]{2,1,0:T(8,128)(2,1)S(1)}, bf16[32,8,512]{2,1,0:T(8,128)(2,1)S(1)}, u32[]{:S(2)}, u32[]{:S(2)}) %collective-permute-start.11) | collective-permute-done | bytes 262176 | tf_op jit(solution)/shard_map/ppermute | solution.py:22
  51.4 5.8 %collective-permute-done.12.refs_3_ = bf16[32,8,512]{2,1,0:T(8,128)(2,1)S(1)} collective-permute-done((bf16[32,8,512]{2,1,0:T(8,128)(2,1)S(1)}, bf16[32,8,512]{2,1,0:T(8,128)(2,1)S(1)}, u32[]{:S(2)}, u32[]{:S(2)}) %collective-permute-start.12) | collective-permute-done | bytes 262176 | tf_op jit(solution)/shard_map/ppermute | solution.py:22
  57.2 1.2 %collective-permute-done.10.refs_9_ = bf16[96,3584]{1,0:T(8,128)(2,1)S(1)} collective-permute-done((bf16[96,3584]{1,0:T(8,128)(2,1)S(1)}, bf16[96,3584]{1,0:T(8,128)(2,1)S(1)}, u32[]{:S(2)}, u32[]{:S(2)}) %collective-permute-start.10) | collective-permute-done | bytes 688160 | tf_op jit(solution)/shard_map/ppermute | solution.py:22
  58.6 2.1 %collective-permute-start.16 = (bf16[96,3584]{1,0:T(8,128)(2,1)S(1)}, bf16[96,3584]{1,0:T(8,128)(2,1)S(1)}, u32[]{:S(2)}, u32[]{:S(2)}) collective-permute-start(bf16[96,3584]{1,0:T(8,128)(2,1)S(1)} %get-tuple-element.101), channel_id=1, source_target_pairs={{0,192},{64,0},{128,64},{192,128},{1,193},{65,1},{129,65},{193,129... | collective-permute-start | bytes 2064392 | tf_op jit(solution)/shard_map/ppermute | solution.py:22
  60.8 2.6 %collective-permute-start.15 = (bf16[64,3584]{1,0:T(8,128)(2,1)S(1)}, bf16[64,3584]{1,0:T(8,128)(2,1)S(1)}, u32[]{:S(2)}, u32[]{:S(2)}) collective-permute-start(bf16[64,3584]{1,0:T(8,128)(2,1)S(1)} %pad_maximum_fusion.5), channel_id=1, source_target_pairs={{0,48},{16,0},{32,16},{48,32},{1,49},{17,1},{33,17},{49,33},{2,50}... | collective-permute-start | bytes 1376264 | tf_op jit(solution)/shard_map/ppermute | solution.py:22
  63.4 1.0 %arrange_left.1 = (bf16[512,768]{1,0:T(8,128)(2,1)S(1)}, bf16[512,256]{1,0:T(8,128)(2,1)S(1)}) custom-call(s32[3]{0:T(128)S(1)} %pad_add_fusion.place_ref, bf16[32,8,512]{2,1,0:T(8,128)(2,1)S(1)} %all-to-all-done.refs_0_, bf16[32,8,512]{2,1,0:T(8,128)(2,1)S(1)} %collective-permute-done.7.refs_1_, bf16[32,8,512]{2,1,0:T(8,128)(2,1)S(1)} %collective-permute-done.11.refs_2_, ...), custom_call_target="tpu_custom_call" | custom-call | bytes 6291456 | tf_op jit(solution)/shard_map/arrange_left/pallas_call | solution.py:48
  64.4 3.0 %multiply_0.1.total_ref = f32[512,3584]{1,0:T(8,128)S(1)} custom-call(bf16[512,768]{1,0:T(8,128)(2,1)S(1)} %get-tuple-element.74.left_ref, bf16[64,3584]{1,0:T(8,128)(2,1)S(1)} %maximum_bitcast_fusion.refs_0_, bf16[64,3584]{1,0:T(8,128)(2,1)S(1)} %collective-permute-done.4.refs_1_, bf16[64,3584]{1,0:T(8,128)(2,1)S(1)} %copy-done.5, ...), custom_call_target="tpu_custom_call" | custom-call | flops 2818572288 | bytes 1048576 | tf_op jit(solution)/shard_map/multiply_0/pallas_call | solution.py:82
  67.4 1.6 %collective-permute-done.15.refs_2_ = bf16[64,3584]{1,0:T(8,128)(2,1)S(1)} collective-permute-done((bf16[64,3584]{1,0:T(8,128)(2,1)S(1)}, bf16[64,3584]{1,0:T(8,128)(2,1)S(1)}, u32[]{:S(2)}, u32[]{:S(2)}) %collective-permute-start.15) | collective-permute-done | bytes 458784 | tf_op jit(solution)/shard_map/ppermute | solution.py:22
  69.0 2.1 %collective-permute-done.16.refs_1_ = bf16[96,3584]{1,0:T(8,128)(2,1)S(1)} collective-permute-done((bf16[96,3584]{1,0:T(8,128)(2,1)S(1)}, bf16[96,3584]{1,0:T(8,128)(2,1)S(1)}, u32[]{:S(2)}, u32[]{:S(2)}) %collective-permute-start.16) | collective-permute-done | bytes 688160 | tf_op jit(solution)/shard_map/ppermute | solution.py:22
  71.1 1.2 %collective-permute-done.17.refs_0_ = bf16[96,3584]{1,0:T(8,128)(2,1)S(1)} collective-permute-done((bf16[96,3584]{1,0:T(8,128)(2,1)S(1)}, bf16[96,3584]{1,0:T(8,128)(2,1)S(1)}, u32[]{:S(2)}, u32[]{:S(2)}) %collective-permute-start.17) | collective-permute-done | bytes 688160 | tf_op jit(solution)/shard_map/ppermute | solution.py:22
  73.0 7.5 %collective-permute-start.19 = (bf16[256,1792]{1,0:T(8,128)(2,1)S(1)}, bf16[256,1792]{1,0:T(8,128)(2,1)S(1)}, u32[]{:S(2)}, u32[]{:S(2)}) collective-permute-start(bf16[256,1792]{1,0:T(8,128)(2,1)S(1)} %get-tuple-element.83), channel_id=1, source_target_pairs={{0,8},{8,0},{1,9},{9,1},{2,10},{10,2},{3,11},{11,3},{4,12},{12,4},... | collective-permute-start | bytes 2752520 | tf_op jit(solution)/shard_map/ppermute | solution.py:22
  81.3 1.2 %put_0_0.1 = (bf16[256,3584]{1,0:T(8,128)(2,1)}, bf16[256,3584]{1,0:T(8,128)(2,1)}) custom-call(s32[1]{0:T(128)} %bitcast.6.core_ref, bf16[256,3584]{1,0:T(8,128)(2,1)S(1)} %multiply_2.1.part_ref), custom_call_target="tpu_custom_call" | custom-call | bytes 4194304 | tf_op jit(solution)/shard_map/put_0_0/pallas_call | solution.py:145
  (62 shorter events, 10.4 us)
Async XLA Ops:
  0.6 5.8 %collective-permute-start = (bf16[8,4,3584]{2,1,0:T(4,128)(2,1)}, bf16[8,4,3584]{2,1,0:T(4,128)(2,1)S(1)}, u32[]{:S(2)}, u32[]{:S(2)}) collective-permute-start(bf16[8,4,3584]{2,1,0:T(4,128)(2,1)} %param.8), channel_id=1, source_target_pairs={{0,8},{8,0},{1,9},{9,1},{2,10},{10,2},{3,11},{11,3},{4,12},{12,4},... | collective-permute-start | bytes 688136 | tf_op jit(solution)/shard_map/ppermute | solution.py:22
  4.0 2.4 %collective-permute-start.1 = (bf16[8,4,3584]{2,1,0:T(4,128)(2,1)}, bf16[8,4,3584]{2,1,0:T(4,128)(2,1)S(1)}, u32[]{:S(2)}, u32[]{:S(2)}) collective-permute-start(bf16[8,4,3584]{2,1,0:T(4,128)(2,1)} %param.9), channel_id=1, source_target_pairs={{0,8},{8,0},{1,9},{9,1},{2,10},{10,2},{3,11},{11,3},{4,12},{12,4},... | collective-permute-start | bytes 688136 | tf_op jit(solution)/shard_map/ppermute | solution.py:22
  6.4 4.4 %collective-permute-start.6 = (bf16[4,8192]{1,0:T(4,128)(2,1)S(1)}, bf16[4,8192]{1,0:T(4,128)(2,1)S(1)}, u32[]{:S(2)}, u32[]{:S(2)}) collective-permute-start(bf16[4,8192]{1,0:T(4,128)(2,1)S(1)} %get-tuple-element.56), channel_id=1, source_target_pairs={{0,8},{8,0},{1,9},{9,1},{2,10},{10,2},{3,11},{11,3},{4,12},{12,4},... | collective-permute-start | bytes 196616 | tf_op jit(solution)/shard_map/ppermute | solution.py:22
  8.1 14.0 %collective-permute-start.2 = (bf16[64,3584]{1,0:T(8,128)(2,1)S(1)}, bf16[64,3584]{1,0:T(8,128)(2,1)S(1)}, u32[]{:S(2)}, u32[]{:S(2)}) collective-permute-start(bf16[64,3584]{1,0:T(8,128)(2,1)S(1)} %maximum_bitcast_fusion.refs_0_), channel_id=1, source_target_pairs={{0,16},{16,32},{32,48},{48,0},{1,17},{17,33},{33,49},{49,1},{2,18}... | collective-permute-start | bytes 1376264 | tf_op jit(solution)/shard_map/ppermute | solution.py:22
  8.2 13.9 %collective-permute-start.3 = (bf16[64,3584]{1,0:T(8,128)(2,1)S(1)}, bf16[64,3584]{1,0:T(8,128)(2,1)S(1)}, u32[]{:S(2)}, u32[]{:S(2)}) collective-permute-start(bf16[64,3584]{1,0:T(8,128)(2,1)S(1)} %maximum_bitcast_fusion.refs_0_), channel_id=1, source_target_pairs={{0,192},{64,0},{128,64},{192,128},{1,193},{65,1},{129,65},{193,129... | collective-permute-start | bytes 1376264 | tf_op jit(solution)/shard_map/ppermute | solution.py:22
  10.8 12.6 %collective-permute-start.4 = (bf16[64,3584]{1,0:T(8,128)(2,1)S(1)}, bf16[64,3584]{1,0:T(8,128)(2,1)S(1)}, u32[]{:S(2)}, u32[]{:S(2)}) collective-permute-start(bf16[64,3584]{1,0:T(8,128)(2,1)S(1)} %maximum_bitcast_fusion.refs_0_), channel_id=1, source_target_pairs={{0,64},{64,128},{128,192},{192,0},{1,65},{65,129},{129,193},{193,1... | collective-permute-start | bytes 1376264 | tf_op jit(solution)/shard_map/ppermute | solution.py:22
  11.7 21.8 %all-to-all-start = ((bf16[32,8,512]{2,1,0:T(8,128)(2,1)}), bf16[32,8,512]{2,1,0:T(8,128)(2,1)S(1)}, u32[]{:S(2)}, u32[]{:S(2)}) async-start(bf16[32,8,512]{2,1,0:T(8,128)(2,1)} %pad_maximum_fusion.6), calls=%async_computation | async-start | bytes 524288 | tf_op jit(solution)/shard_map/all_to_all | solution.py:203
  22.1 18.7 %copy-start.4 = (bf16[64,3584]{1,0:T(8,128)(2,1)}, bf16[64,3584]{1,0:T(8,128)(2,1)S(1)}, u32[]{:S(2)}) copy-start(bf16[64,3584]{1,0:T(8,128)(2,1)S(1)} %collective-permute-done.3.refs_2_) | copy-start | bytes 1376260
  23.5 17.1 %collective-permute-start.5 = (bf16[64,3584]{1,0:T(8,128)(2,1)S(1)}, bf16[64,3584]{1,0:T(8,128)(2,1)S(1)}, u32[]{:S(2)}, u32[]{:S(2)}) collective-permute-start(bf16[64,3584]{1,0:T(8,128)(2,1)S(1)} %collective-permute-done.2.refs_5_), channel_id=1, source_target_pairs={{0,16},{16,32},{32,48},{48,0},{1,17},{17,33},{33,49},{49,1},{2,18}... | collective-permute-start | bytes 1376264 | tf_op jit(solution)/shard_map/ppermute | solution.py:22
  25.1 15.5 %collective-permute-start.8 = (bf16[64,3584]{1,0:T(8,128)(2,1)S(1)}, bf16[64,3584]{1,0:T(8,128)(2,1)S(1)}, u32[]{:S(2)}, u32[]{:S(2)}) collective-permute-start(bf16[64,3584]{1,0:T(8,128)(2,1)S(1)} %collective-permute-done.2.refs_5_), channel_id=1, source_target_pairs={{0,192},{64,0},{128,64},{192,128},{1,193},{65,1},{129,65},{193,129... | collective-permute-start | bytes 1376264 | tf_op jit(solution)/shard_map/ppermute | solution.py:22
  25.5 15.1 %collective-permute-start.9 = (bf16[64,3584]{1,0:T(8,128)(2,1)S(1)}, bf16[64,3584]{1,0:T(8,128)(2,1)S(1)}, u32[]{:S(2)}, u32[]{:S(2)}) collective-permute-start(bf16[64,3584]{1,0:T(8,128)(2,1)S(1)} %collective-permute-done.2.refs_5_), channel_id=1, source_target_pairs={{0,64},{64,128},{128,192},{192,0},{1,65},{65,129},{129,193},{193,1... | collective-permute-start | bytes 1376264 | tf_op jit(solution)/shard_map/ppermute | solution.py:22
  33.5 6.7 %collective-permute-start.7 = (bf16[32,8,512]{2,1,0:T(8,128)(2,1)S(1)}, bf16[32,8,512]{2,1,0:T(8,128)(2,1)S(1)}, u32[]{:S(2)}, u32[]{:S(2)}) collective-permute-start(bf16[32,8,512]{2,1,0:T(8,128)(2,1)S(1)} %all-to-all-done.refs_0_), channel_id=1, source_target_pairs={{0,1},{1,2},{2,3},{3,0},{4,5},{5,6},{6,7},{7,4},{8,9},{9,10},{10,1... | collective-permute-start | bytes 786440 | tf_op jit(solution)/shard_map/ppermute | solution.py:22
  41.5 16.8 %collective-permute-start.14 = (bf16[112,3584]{1,0:T(8,128)(2,1)S(1)}, bf16[112,3584]{1,0:T(8,128)(2,1)S(1)}, u32[]{:S(2)}, u32[]{:S(2)}) collective-permute-start(bf16[112,3584]{1,0:T(8,128)(2,1)S(1)} %pad_maximum_fusion.1), channel_id=1, source_target_pairs={{0,64},{64,128},{128,192},{192,0},{1,65},{65,129},{129,193},{193,1... | collective-permute-start | bytes 2408456 | tf_op jit(solution)/shard_map/ppermute | solution.py:22
  42.0 16.3 %collective-permute-start.13 = (bf16[112,3584]{1,0:T(8,128)(2,1)S(1)}, bf16[112,3584]{1,0:T(8,128)(2,1)S(1)}, u32[]{:S(2)}, u32[]{:S(2)}) collective-permute-start(bf16[112,3584]{1,0:T(8,128)(2,1)S(1)} %pad_maximum_fusion), channel_id=1, source_target_pairs={{0,192},{64,0},{128,64},{192,128},{1,193},{65,1},{129,65},{193,129... | collective-permute-start | bytes 2408456 | tf_op jit(solution)/shard_map/ppermute | solution.py:22
  44.4 14.0 %collective-permute-start.10 = (bf16[96,3584]{1,0:T(8,128)(2,1)S(1)}, bf16[96,3584]{1,0:T(8,128)(2,1)S(1)}, u32[]{:S(2)}, u32[]{:S(2)}) collective-permute-start(bf16[96,3584]{1,0:T(8,128)(2,1)S(1)} %pad_maximum_fusion.4), channel_id=1, source_target_pairs={{0,16},{16,32},{32,48},{48,0},{1,17},{17,33},{33,49},{49,1},{2,18}... | collective-permute-start | bytes 2064392 | tf_op jit(solution)/shard_map/ppermute | solution.py:22
  44.7 6.7 %collective-permute-start.11 = (bf16[32,8,512]{2,1,0:T(8,128)(2,1)S(1)}, bf16[32,8,512]{2,1,0:T(8,128)(2,1)S(1)}, u32[]{:S(2)}, u32[]{:S(2)}) collective-permute-start(bf16[32,8,512]{2,1,0:T(8,128)(2,1)S(1)} %all-to-all-done.refs_0_), channel_id=1, source_target_pairs={{0,2},{1,3},{2,0},{3,1},{4,6},{5,7},{6,4},{7,5},{8,10},{9,11},{10,... | collective-permute-start | bytes 786440 | tf_op jit(solution)/shard_map/ppermute | solution.py:22
  47.4 9.8 %collective-permute-start.12 = (bf16[32,8,512]{2,1,0:T(8,128)(2,1)S(1)}, bf16[32,8,512]{2,1,0:T(8,128)(2,1)S(1)}, u32[]{:S(2)}, u32[]{:S(2)}) collective-permute-start(bf16[32,8,512]{2,1,0:T(8,128)(2,1)S(1)} %all-to-all-done.refs_0_), channel_id=1, source_target_pairs={{0,3},{1,0},{2,1},{3,2},{4,7},{5,4},{6,5},{7,6},{8,11},{9,8},{10,9... | collective-permute-start | bytes 786440 | tf_op jit(solution)/shard_map/ppermute | solution.py:22
  58.5 5.9 %copy-start.1 = (bf16[64,3584]{1,0:T(8,128)(2,1)S(1)}, bf16[64,3584]{1,0:T(8,128)(2,1)}, u32[]{:S(2)}) copy-start(bf16[64,3584]{1,0:T(8,128)(2,1)} %copy-done) | copy-start | bytes 1376260
  58.5 5.9 %copy-start.3 = (bf16[64,3584]{1,0:T(8,128)(2,1)S(1)}, bf16[64,3584]{1,0:T(8,128)(2,1)}, u32[]{:S(2)}) copy-start(bf16[64,3584]{1,0:T(8,128)(2,1)} %copy-done.2) | copy-start | bytes 1376260
  58.6 12.4 %collective-permute-start.16 = (bf16[96,3584]{1,0:T(8,128)(2,1)S(1)}, bf16[96,3584]{1,0:T(8,128)(2,1)S(1)}, u32[]{:S(2)}, u32[]{:S(2)}) collective-permute-start(bf16[96,3584]{1,0:T(8,128)(2,1)S(1)} %get-tuple-element.101), channel_id=1, source_target_pairs={{0,192},{64,0},{128,64},{192,128},{1,193},{65,1},{129,65},{193,129... | collective-permute-start | bytes 2064392 | tf_op jit(solution)/shard_map/ppermute | solution.py:22
  60.7 11.6 %collective-permute-start.17 = (bf16[96,3584]{1,0:T(8,128)(2,1)S(1)}, bf16[96,3584]{1,0:T(8,128)(2,1)S(1)}, u32[]{:S(2)}, u32[]{:S(2)}) collective-permute-start(bf16[96,3584]{1,0:T(8,128)(2,1)S(1)} %get-tuple-element.100), channel_id=1, source_target_pairs={{0,64},{64,128},{128,192},{192,0},{1,65},{65,129},{129,193},{193,1... | collective-permute-start | bytes 2064392 | tf_op jit(solution)/shard_map/ppermute | solution.py:22
  60.8 8.3 %collective-permute-start.15 = (bf16[64,3584]{1,0:T(8,128)(2,1)S(1)}, bf16[64,3584]{1,0:T(8,128)(2,1)S(1)}, u32[]{:S(2)}, u32[]{:S(2)}) collective-permute-start(bf16[64,3584]{1,0:T(8,128)(2,1)S(1)} %pad_maximum_fusion.5), channel_id=1, source_target_pairs={{0,48},{16,0},{32,16},{48,32},{1,49},{17,1},{33,17},{49,33},{2,50}... | collective-permute-start | bytes 1376264 | tf_op jit(solution)/shard_map/ppermute | solution.py:22
  73.0 9.6 %collective-permute-start.19 = (bf16[256,1792]{1,0:T(8,128)(2,1)S(1)}, bf16[256,1792]{1,0:T(8,128)(2,1)S(1)}, u32[]{:S(2)}, u32[]{:S(2)}) collective-permute-start(bf16[256,1792]{1,0:T(8,128)(2,1)S(1)} %get-tuple-element.83), channel_id=1, source_target_pairs={{0,8},{8,0},{1,9},{9,1},{2,10},{10,2},{3,11},{11,3},{4,12},{12,4},... | collective-permute-start | bytes 2752520 | tf_op jit(solution)/shard_map/ppermute | solution.py:22
  80.5 3.4 %collective-permute-start.18 = (bf16[256,1792]{1,0:T(8,128)(2,1)S(1)}, bf16[256,1792]{1,0:T(8,128)(2,1)S(1)}, u32[]{:S(2)}, u32[]{:S(2)}) collective-permute-start(bf16[256,1792]{1,0:T(8,128)(2,1)S(1)} %get-tuple-element.82), channel_id=1, source_target_pairs={{0,8},{8,0},{1,9},{9,1},{2,10},{10,2},{3,11},{11,3},{4,12},{12,4},... | collective-permute-start | bytes 2752520 | tf_op jit(solution)/shard_map/ppermute | solution.py:22
  (6 other events, 13.6 us)

commit v8 on v7

--- a/solution.py
+++ b/solution.py
@@ -217,7 +217,7 @@
     down2 = shift(jnp.concatenate([z2[few:], down1[half:], down0[half:]], axis=0), "y", -1)
     z3 = shift(jnp.concatenate([z2, up1[n - few :], down1[:few]], axis=0), "z", 1)
     left_2, left_3 = shift(left, "x", 2), shift(left, "x", 3)
-    z3, left_2, left_3, down2, up2 = event(z3, left_2, left_3, down2, up2)
+    z3, left_2, left_3, up2, down2 = event(z3, left_2, left_3, up2, down2)
 
     up3 = shift(jnp.concatenate([z3[:n], up2[:half]], axis=0), "y", 1)
     down3 = shift(jnp.concatenate([z3[:n], down2[half - few : n - few]], axis=0), "y", -1)
@@ -233,7 +233,7 @@
     total = multiply_part(left, pieces, "multiply_0")
     far3, down3, up3, total = event(far3, down3, up3, total)
 
-    cut = columns // 2
+    cut = columns // 1792 * 1280
     lasts = [up3, down3, far3]
     ranges = [(0, n, half), (1, n, half), (0, 0, n), (1, 0, n), (2, 0, n)]
     cuts = (cut, columns - cut)

time: 85.7 us -> 86.5 us (level)
  waiting for transfers between devices: 30 us -> 34.5 us
  starting transfers between devices: 40 us -> 35.8 us
    ppermute x20, waiting for transfers between devices: 23.1 us -> 27.6 us  [shift(): return lax.ppermute(x, axis, [(i, (i + by) % n) for i in range(n)])]
    ppermute x20, starting transfers between devices: 29.9 us -> 25.8 us  [shift(): return lax.ppermute(x, axis, [(i, (i + by) % n) for i in range(n)])]
where the time goes in v8:
time: 86.5 us; the launch traced here: 86.2 us
  starting transfers between devices  35.8 us (41%)
  waiting for transfers between devices  34.5 us (40%)
  Pallas kernels  8.43 us (10%)
  other arithmetic  3.36 us (4%)
  between operations  2.37 us (3%)
  local copies, waits for them, and re-layouts  1.74 us (2%)
    ppermute x20, waiting for transfers between devices, shift(): return lax.ppermute(x, axis, [(i, (i + by) % n) for i in range(n)])  27.6 us
    ppermute x20, starting transfers between devices, shift(): return lax.ppermute(x, axis, [(i, (i + by) % n) for i in range(n)])  25.8 us
    all_to_all x1, starting transfers between devices, shards(): lax.all_to_all(left, ('h', 'y', 'z'), split_axis=0, concat_axis=0, tiled=...  10.1 us
    all_to_all x1, waiting for transfers between devices, shards(): lax.all_to_all(left, ('h', 'y', 'z'), split_axis=0, concat_axis=0, tiled=...  6.9 us
    pallas_call x3, Pallas kernels, put(): pl.pallas_call(functools.partial(put_kernel, got, at), out_shape=(shape,...  3.12 us
    pallas_call x1, Pallas kernels, multiply_part(): pl.pallas_call(functools.partial(part_kernel, ranges, 256), out_shape=jax...  3.02 us
  transfers between devices with their start and end apart: 21, of which 13 were waited for; matrix products, arithmetic and copies ran while one was open for 4% of the time, Pallas kernels for 8%

profile of v8, /device:TPU:1, one launch (start us, length us, event | category | flops | bytes accessed | tf_op | source)
XLA Modules:
  0.0 86.2 jit_solution(11192400306192428148)
XLA Ops:
  0.6 3.3 %collective-permute-start = (bf16[8,4,3584]{2,1,0:T(4,128)(2,1)}, bf16[8,4,3584]{2,1,0:T(4,128)(2,1)S(1)}, u32[]{:S(2)}, u32[]{:S(2)}) collective-permute-start(bf16[8,4,3584]{2,1,0:T(4,128)(2,1)} %param.8), channel_id=1, source_target_pairs={{0,8},{8,0},{1,9},{9,1},{2,10},{10,2},{3,11},{11,3},{4,12},{12,4},... | collective-permute-start | bytes 688136 | tf_op jit(solution)/shard_map/ppermute | solution.py:22
  8.2 2.6 %collective-permute-start.3 = (bf16[64,3584]{1,0:T(8,128)(2,1)S(1)}, bf16[64,3584]{1,0:T(8,128)(2,1)S(1)}, u32[]{:S(2)}, u32[]{:S(2)}) collective-permute-start(bf16[64,3584]{1,0:T(8,128)(2,1)S(1)} %maximum_bitcast_fusion.refs_0_), channel_id=1, source_target_pairs={{0,192},{64,0},{128,64},{192,128},{1,193},{65,1},{129,65},{193,129... | collective-permute-start | bytes 1376264 | tf_op jit(solution)/shard_map/ppermute | solution.py:22
  11.7 10.1 %all-to-all-start = ((bf16[32,8,512]{2,1,0:T(8,128)(2,1)}), bf16[32,8,512]{2,1,0:T(8,128)(2,1)S(1)}, u32[]{:S(2)}, u32[]{:S(2)}) async-start(bf16[32,8,512]{2,1,0:T(8,128)(2,1)} %pad_maximum_fusion.6), calls=%async_computation | async-start | bytes 524288 | tf_op jit(solution)/shard_map/all_to_all | solution.py:203
  22.1 1.4 %collective-permute-done.4.refs_1_ = bf16[64,3584]{1,0:T(8,128)(2,1)S(1)} collective-permute-done((bf16[64,3584]{1,0:T(8,128)(2,1)S(1)}, bf16[64,3584]{1,0:T(8,128)(2,1)S(1)}, u32[]{:S(2)}, u32[]{:S(2)}) %collective-permute-start.4) | collective-permute-done | bytes 458784 | tf_op jit(solution)/shard_map/ppermute | solution.py:22
  23.5 1.6 %collective-permute-start.5 = (bf16[64,3584]{1,0:T(8,128)(2,1)S(1)}, bf16[64,3584]{1,0:T(8,128)(2,1)S(1)}, u32[]{:S(2)}, u32[]{:S(2)}) collective-permute-start(bf16[64,3584]{1,0:T(8,128)(2,1)S(1)} %collective-permute-done.2.refs_5_), channel_id=1, source_target_pairs={{0,16},{16,32},{32,48},{48,0},{1,17},{17,33},{33,49},{49,1},{2,18}... | collective-permute-start | bytes 1376264 | tf_op jit(solution)/shard_map/ppermute | solution.py:22
  25.5 1.1 %collective-permute-start.9 = (bf16[64,3584]{1,0:T(8,128)(2,1)S(1)}, bf16[64,3584]{1,0:T(8,128)(2,1)S(1)}, u32[]{:S(2)}, u32[]{:S(2)}) collective-permute-start(bf16[64,3584]{1,0:T(8,128)(2,1)S(1)} %collective-permute-done.2.refs_5_), channel_id=1, source_target_pairs={{0,64},{64,128},{128,192},{192,0},{1,65},{65,129},{129,193},{193,1... | collective-permute-start | bytes 1376264 | tf_op jit(solution)/shard_map/ppermute | solution.py:22
  26.6 6.9 %all-to-all-done.refs_0_ = bf16[32,8,512]{2,1,0:T(8,128)(2,1)S(1)} async-done(((bf16[32,8,512]{2,1,0:T(8,128)(2,1)}), bf16[32,8,512]{2,1,0:T(8,128)(2,1)S(1)}, u32[]{:S(2)}, u32[]{:S(2)}) %all-to-all-start) | async-done | bytes 262176 | tf_op jit(solution)/shard_map/all_to_all | solution.py:203
  33.5 1.2 %collective-permute-start.7 = (bf16[32,8,512]{2,1,0:T(8,128)(2,1)S(1)}, bf16[32,8,512]{2,1,0:T(8,128)(2,1)S(1)}, u32[]{:S(2)}, u32[]{:S(2)}) collective-permute-start(bf16[32,8,512]{2,1,0:T(8,128)(2,1)S(1)} %all-to-all-done.refs_0_), channel_id=1, source_target_pairs={{0,1},{1,2},{2,3},{3,0},{4,5},{5,6},{6,7},{7,4},{8,9},{9,10},{10,1... | collective-permute-start | bytes 786440 | tf_op jit(solution)/shard_map/ppermute | solution.py:22
  34.7 5.5 %collective-permute-done.7.refs_1_ = bf16[32,8,512]{2,1,0:T(8,128)(2,1)S(1)} collective-permute-done((bf16[32,8,512]{2,1,0:T(8,128)(2,1)S(1)}, bf16[32,8,512]{2,1,0:T(8,128)(2,1)S(1)}, u32[]{:S(2)}, u32[]{:S(2)}) %collective-permute-start.7) | collective-permute-done | bytes 262176 | tf_op jit(solution)/shard_map/ppermute | solution.py:22
  41.5 1.6 %collective-permute-start.14 = (bf16[112,3584]{1,0:T(8,128)(2,1)S(1)}, bf16[112,3584]{1,0:T(8,128)(2,1)S(1)}, u32[]{:S(2)}, u32[]{:S(2)}) collective-permute-start(bf16[112,3584]{1,0:T(8,128)(2,1)S(1)} %pad_maximum_fusion.1), channel_id=1, source_target_pairs={{0,192},{64,0},{128,64},{192,128},{1,193},{65,1},{129,65},{193,129... | collective-permute-start | bytes 2408456 | tf_op jit(solution)/shard_map/ppermute | solution.py:22
  44.3 2.8 %collective-permute-start.11 = (bf16[32,8,512]{2,1,0:T(8,128)(2,1)S(1)}, bf16[32,8,512]{2,1,0:T(8,128)(2,1)S(1)}, u32[]{:S(2)}, u32[]{:S(2)}) collective-permute-start(bf16[32,8,512]{2,1,0:T(8,128)(2,1)S(1)} %all-to-all-done.refs_0_), channel_id=1, source_target_pairs={{0,2},{1,3},{2,0},{3,1},{4,6},{5,7},{6,4},{7,5},{8,10},{9,11},{10,... | collective-permute-start | bytes 786440 | tf_op jit(solution)/shard_map/ppermute | solution.py:22
  48.0 3.1 %collective-permute-done.11.refs_2_ = bf16[32,8,512]{2,1,0:T(8,128)(2,1)S(1)} collective-permute-done((bf16[32,8,512]{2,1,0:T(8,128)(2,1)S(1)}, bf16[32,8,512]{2,1,0:T(8,128)(2,1)S(1)}, u32[]{:S(2)}, u32[]{:S(2)}) %collective-permute-start.11) | collective-permute-done | bytes 262176 | tf_op jit(solution)/shard_map/ppermute | solution.py:22
  51.1 5.8 %collective-permute-done.12.refs_3_ = bf16[32,8,512]{2,1,0:T(8,128)(2,1)S(1)} collective-permute-done((bf16[32,8,512]{2,1,0:T(8,128)(2,1)S(1)}, bf16[32,8,512]{2,1,0:T(8,128)(2,1)S(1)}, u32[]{:S(2)}, u32[]{:S(2)}) %collective-permute-start.12) | collective-permute-done | bytes 262176 | tf_op jit(solution)/shard_map/ppermute | solution.py:22
  56.9 2.2 %collective-permute-done.10.refs_9_ = bf16[96,3584]{1,0:T(8,128)(2,1)S(1)} collective-permute-done((bf16[96,3584]{1,0:T(8,128)(2,1)S(1)}, bf16[96,3584]{1,0:T(8,128)(2,1)S(1)}, u32[]{:S(2)}, u32[]{:S(2)}) %collective-permute-start.10) | collective-permute-done | bytes 688160 | tf_op jit(solution)/shard_map/ppermute | solution.py:22
  59.2 1.6 %collective-permute-done.13.refs_3_ = bf16[112,3584]{1,0:T(8,128)(2,1)S(1)} collective-permute-done((bf16[112,3584]{1,0:T(8,128)(2,1)S(1)}, bf16[112,3584]{1,0:T(8,128)(2,1)S(1)}, u32[]{:S(2)}, u32[]{:S(2)}) %collective-permute-start.13) | collective-permute-done | bytes 802848 | tf_op jit(solution)/shard_map/ppermute | solution.py:22
  62.5 2.0 %collective-permute-start.15 = (bf16[64,3584]{1,0:T(8,128)(2,1)S(1)}, bf16[64,3584]{1,0:T(8,128)(2,1)S(1)}, u32[]{:S(2)}, u32[]{:S(2)}) collective-permute-start(bf16[64,3584]{1,0:T(8,128)(2,1)S(1)} %pad_maximum_fusion.5), channel_id=1, source_target_pairs={{0,48},{16,0},{32,16},{48,32},{1,49},{17,1},{33,17},{49,33},{2,50}... | collective-permute-start | bytes 1376264 | tf_op jit(solution)/shard_map/ppermute | solution.py:22
  64.5 1.0 %arrange_left.1 = (bf16[512,768]{1,0:T(8,128)(2,1)S(1)}, bf16[512,256]{1,0:T(8,128)(2,1)S(1)}) custom-call(s32[3]{0:T(128)S(1)} %pad_add_fusion.place_ref, bf16[32,8,512]{2,1,0:T(8,128)(2,1)S(1)} %all-to-all-done.refs_0_, bf16[32,8,512]{2,1,0:T(8,128)(2,1)S(1)} %collective-permute-done.7.refs_1_, bf16[32,8,512]{2,1,0:T(8,128)(2,1)S(1)} %collective-permute-done.11.refs_2_, ...), custom_call_target="tpu_custom_call" | custom-call | bytes 6291456 | tf_op jit(solution)/shard_map/arrange_left/pallas_call | solution.py:48
  65.6 3.0 %multiply_0.1.total_ref = f32[512,3584]{1,0:T(8,128)S(1)} custom-call(bf16[512,768]{1,0:T(8,128)(2,1)S(1)} %get-tuple-element.74.left_ref, bf16[64,3584]{1,0:T(8,128)(2,1)S(1)} %maximum_bitcast_fusion.refs_0_, bf16[64,3584]{1,0:T(8,128)(2,1)S(1)} %copy-done.5, bf16[64,3584]{1,0:T(8,128)(2,1)S(1)} %collective-permute-done.3.refs_2_, ...), custom_call_target="tpu_custom_call" | custom-call | flops 2818572288 | bytes 1048576 | tf_op jit(solution)/shard_map/multiply_0/pallas_call | solution.py:82
  68.6 1.7 %collective-permute-done.15.refs_2_ = bf16[64,3584]{1,0:T(8,128)(2,1)S(1)} collective-permute-done((bf16[64,3584]{1,0:T(8,128)(2,1)S(1)}, bf16[64,3584]{1,0:T(8,128)(2,1)S(1)}, u32[]{:S(2)}, u32[]{:S(2)}) %collective-permute-start.15) | collective-permute-done | bytes 458784 | tf_op jit(solution)/shard_map/ppermute | solution.py:22
  70.2 3.6 %collective-permute-done.16.refs_1_ = bf16[96,3584]{1,0:T(8,128)(2,1)S(1)} collective-permute-done((bf16[96,3584]{1,0:T(8,128)(2,1)S(1)}, bf16[96,3584]{1,0:T(8,128)(2,1)S(1)}, u32[]{:S(2)}, u32[]{:S(2)}) %collective-permute-start.16) | collective-permute-done | bytes 688160 | tf_op jit(solution)/shard_map/ppermute | solution.py:22
  73.8 1.3 %collective-permute-done.17.refs_0_ = bf16[96,3584]{1,0:T(8,128)(2,1)S(1)} collective-permute-done((bf16[96,3584]{1,0:T(8,128)(2,1)S(1)}, bf16[96,3584]{1,0:T(8,128)(2,1)S(1)}, u32[]{:S(2)}, u32[]{:S(2)}) %collective-permute-start.17) | collective-permute-done | bytes 688160 | tf_op jit(solution)/shard_map/ppermute | solution.py:22
  75.8 5.7 %collective-permute-start.19 = (bf16[256,2560]{1,0:T(8,128)(2,1)S(1)}, bf16[256,2560]{1,0:T(8,128)(2,1)S(1)}, u32[]{:S(2)}, u32[]{:S(2)}) collective-permute-start(bf16[256,2560]{1,0:T(8,128)(2,1)S(1)} %get-tuple-element.83), channel_id=1, source_target_pairs={{0,8},{8,0},{1,9},{9,1},{2,10},{10,2},{3,11},{11,3},{4,12},{12,4},... | collective-permute-start | bytes 3932168 | tf_op jit(solution)/shard_map/ppermute | solution.py:22
  82.2 1.2 %put_0_0.1 = (bf16[256,3584]{1,0:T(8,128)(2,1)}, bf16[256,3584]{1,0:T(8,128)(2,1)}) custom-call(s32[1]{0:T(128)} %bitcast.6.core_ref, bf16[256,3584]{1,0:T(8,128)(2,1)S(1)} %multiply_2.1.part_ref), custom_call_target="tpu_custom_call" | custom-call | bytes 4194304 | tf_op jit(solution)/shard_map/put_0_0/pallas_call | solution.py:145
  84.2 1.1 %put_1_0.1 = (bf16[256,3584]{1,0:T(8,128)(2,1)}, bf16[256,3584]{1,0:T(8,128)(2,1)}) custom-call(s32[1]{0:T(128)} %bitcast.6.core_ref, bf16[256,2560]{1,0:T(8,128)(2,1)S(1)} %collective-permute-done.19.part_ref, bf16[256,3584]{1,0:T(8,128)(2,1)} %get-tuple-element.88.refs_0_, ...), custom_call_target="tpu_custom_call", output_to_operand_aliasing={{0}: (2, {}), {1}: (3, {})} | custom-call | bytes 4194304 | tf_op jit(solution)/shard_map/put_1_0/pallas_call | solution.py:145
  (62 shorter events, 12.3 us)
Async XLA Ops:
  0.6 5.8 %collective-permute-start = (bf16[8,4,3584]{2,1,0:T(4,128)(2,1)}, bf16[8,4,3584]{2,1,0:T(4,128)(2,1)S(1)}, u32[]{:S(2)}, u32[]{:S(2)}) collective-permute-start(bf16[8,4,3584]{2,1,0:T(4,128)(2,1)} %param.8), channel_id=1, source_target_pairs={{0,8},{8,0},{1,9},{9,1},{2,10},{10,2},{3,11},{11,3},{4,12},{12,4},... | collective-permute-start | bytes 688136 | tf_op jit(solution)/shard_map/ppermute | solution.py:22
  4.0 2.4 %collective-permute-start.1 = (bf16[8,4,3584]{2,1,0:T(4,128)(2,1)}, bf16[8,4,3584]{2,1,0:T(4,128)(2,1)S(1)}, u32[]{:S(2)}, u32[]{:S(2)}) collective-permute-start(bf16[8,4,3584]{2,1,0:T(4,128)(2,1)} %param.9), channel_id=1, source_target_pairs={{0,8},{8,0},{1,9},{9,1},{2,10},{10,2},{3,11},{11,3},{4,12},{12,4},... | collective-permute-start | bytes 688136 | tf_op jit(solution)/shard_map/ppermute | solution.py:22
  6.4 4.4 %collective-permute-start.6 = (bf16[4,8192]{1,0:T(4,128)(2,1)S(1)}, bf16[4,8192]{1,0:T(4,128)(2,1)S(1)}, u32[]{:S(2)}, u32[]{:S(2)}) collective-permute-start(bf16[4,8192]{1,0:T(4,128)(2,1)S(1)} %get-tuple-element.56), channel_id=1, source_target_pairs={{0,8},{8,0},{1,9},{9,1},{2,10},{10,2},{3,11},{11,3},{4,12},{12,4},... | collective-permute-start | bytes 196616 | tf_op jit(solution)/shard_map/ppermute | solution.py:22
  8.1 14.0 %collective-permute-start.2 = (bf16[64,3584]{1,0:T(8,128)(2,1)S(1)}, bf16[64,3584]{1,0:T(8,128)(2,1)S(1)}, u32[]{:S(2)}, u32[]{:S(2)}) collective-permute-start(bf16[64,3584]{1,0:T(8,128)(2,1)S(1)} %maximum_bitcast_fusion.refs_0_), channel_id=1, source_target_pairs={{0,16},{16,32},{32,48},{48,0},{1,17},{17,33},{33,49},{49,1},{2,18}... | collective-permute-start | bytes 1376264 | tf_op jit(solution)/shard_map/ppermute | solution.py:22
  8.2 13.9 %collective-permute-start.3 = (bf16[64,3584]{1,0:T(8,128)(2,1)S(1)}, bf16[64,3584]{1,0:T(8,128)(2,1)S(1)}, u32[]{:S(2)}, u32[]{:S(2)}) collective-permute-start(bf16[64,3584]{1,0:T(8,128)(2,1)S(1)} %maximum_bitcast_fusion.refs_0_), channel_id=1, source_target_pairs={{0,192},{64,0},{128,64},{192,128},{1,193},{65,1},{129,65},{193,129... | collective-permute-start | bytes 1376264 | tf_op jit(solution)/shard_map/ppermute | solution.py:22
  10.8 12.6 %collective-permute-start.4 = (bf16[64,3584]{1,0:T(8,128)(2,1)S(1)}, bf16[64,3584]{1,0:T(8,128)(2,1)S(1)}, u32[]{:S(2)}, u32[]{:S(2)}) collective-permute-start(bf16[64,3584]{1,0:T(8,128)(2,1)S(1)} %maximum_bitcast_fusion.refs_0_), channel_id=1, source_target_pairs={{0,64},{64,128},{128,192},{192,0},{1,65},{65,129},{129,193},{193,1... | collective-permute-start | bytes 1376264 | tf_op jit(solution)/shard_map/ppermute | solution.py:22
  11.7 21.8 %all-to-all-start = ((bf16[32,8,512]{2,1,0:T(8,128)(2,1)}), bf16[32,8,512]{2,1,0:T(8,128)(2,1)S(1)}, u32[]{:S(2)}, u32[]{:S(2)}) async-start(bf16[32,8,512]{2,1,0:T(8,128)(2,1)} %pad_maximum_fusion.6), calls=%async_computation | async-start | bytes 524288 | tf_op jit(solution)/shard_map/all_to_all | solution.py:203
  23.5 17.3 %copy-start.4 = (bf16[64,3584]{1,0:T(8,128)(2,1)}, bf16[64,3584]{1,0:T(8,128)(2,1)S(1)}, u32[]{:S(2)}) copy-start(bf16[64,3584]{1,0:T(8,128)(2,1)S(1)} %collective-permute-done.4.refs_1_) | copy-start | bytes 1376260
  23.5 17.1 %collective-permute-start.5 = (bf16[64,3584]{1,0:T(8,128)(2,1)S(1)}, bf16[64,3584]{1,0:T(8,128)(2,1)S(1)}, u32[]{:S(2)}, u32[]{:S(2)}) collective-permute-start(bf16[64,3584]{1,0:T(8,128)(2,1)S(1)} %collective-permute-done.2.refs_5_), channel_id=1, source_target_pairs={{0,16},{16,32},{32,48},{48,0},{1,17},{17,33},{33,49},{49,1},{2,18}... | collective-permute-start | bytes 1376264 | tf_op jit(solution)/shard_map/ppermute | solution.py:22
  25.1 15.5 %collective-permute-start.8 = (bf16[64,3584]{1,0:T(8,128)(2,1)S(1)}, bf16[64,3584]{1,0:T(8,128)(2,1)S(1)}, u32[]{:S(2)}, u32[]{:S(2)}) collective-permute-start(bf16[64,3584]{1,0:T(8,128)(2,1)S(1)} %collective-permute-done.2.refs_5_), channel_id=1, source_target_pairs={{0,192},{64,0},{128,64},{192,128},{1,193},{65,1},{129,65},{193,129... | collective-permute-start | bytes 1376264 | tf_op jit(solution)/shard_map/ppermute | solution.py:22
  25.5 15.1 %collective-permute-start.9 = (bf16[64,3584]{1,0:T(8,128)(2,1)S(1)}, bf16[64,3584]{1,0:T(8,128)(2,1)S(1)}, u32[]{:S(2)}, u32[]{:S(2)}) collective-permute-start(bf16[64,3584]{1,0:T(8,128)(2,1)S(1)} %collective-permute-done.2.refs_5_), channel_id=1, source_target_pairs={{0,64},{64,128},{128,192},{192,0},{1,65},{65,129},{129,193},{193,1... | collective-permute-start | bytes 1376264 | tf_op jit(solution)/shard_map/ppermute | solution.py:22
  33.5 6.7 %collective-permute-start.7 = (bf16[32,8,512]{2,1,0:T(8,128)(2,1)S(1)}, bf16[32,8,512]{2,1,0:T(8,128)(2,1)S(1)}, u32[]{:S(2)}, u32[]{:S(2)}) collective-permute-start(bf16[32,8,512]{2,1,0:T(8,128)(2,1)S(1)} %all-to-all-done.refs_0_), channel_id=1, source_target_pairs={{0,1},{1,2},{2,3},{3,0},{4,5},{5,6},{6,7},{7,4},{8,9},{9,10},{10,1... | collective-permute-start | bytes 786440 | tf_op jit(solution)/shard_map/ppermute | solution.py:22
  41.5 17.6 %collective-permute-start.14 = (bf16[112,3584]{1,0:T(8,128)(2,1)S(1)}, bf16[112,3584]{1,0:T(8,128)(2,1)S(1)}, u32[]{:S(2)}, u32[]{:S(2)}) collective-permute-start(bf16[112,3584]{1,0:T(8,128)(2,1)S(1)} %pad_maximum_fusion.1), channel_id=1, source_target_pairs={{0,192},{64,0},{128,64},{192,128},{1,193},{65,1},{129,65},{193,129... | collective-permute-start | bytes 2408456 | tf_op jit(solution)/shard_map/ppermute | solution.py:22
  43.3 17.5 %collective-permute-start.13 = (bf16[112,3584]{1,0:T(8,128)(2,1)S(1)}, bf16[112,3584]{1,0:T(8,128)(2,1)S(1)}, u32[]{:S(2)}, u32[]{:S(2)}) collective-permute-start(bf16[112,3584]{1,0:T(8,128)(2,1)S(1)} %pad_maximum_fusion), channel_id=1, source_target_pairs={{0,64},{64,128},{128,192},{192,0},{1,65},{65,129},{129,193},{193,1... | collective-permute-start | bytes 2408456 | tf_op jit(solution)/shard_map/ppermute | solution.py:22
  44.2 15.0 %collective-permute-start.10 = (bf16[96,3584]{1,0:T(8,128)(2,1)S(1)}, bf16[96,3584]{1,0:T(8,128)(2,1)S(1)}, u32[]{:S(2)}, u32[]{:S(2)}) collective-permute-start(bf16[96,3584]{1,0:T(8,128)(2,1)S(1)} %pad_maximum_fusion.4), channel_id=1, source_target_pairs={{0,16},{16,32},{32,48},{48,0},{1,17},{17,33},{33,49},{49,1},{2,18}... | collective-permute-start | bytes 2064392 | tf_op jit(solution)/shard_map/ppermute | solution.py:22
  44.3 6.8 %collective-permute-start.11 = (bf16[32,8,512]{2,1,0:T(8,128)(2,1)S(1)}, bf16[32,8,512]{2,1,0:T(8,128)(2,1)S(1)}, u32[]{:S(2)}, u32[]{:S(2)}) collective-permute-start(bf16[32,8,512]{2,1,0:T(8,128)(2,1)S(1)} %all-to-all-done.refs_0_), channel_id=1, source_target_pairs={{0,2},{1,3},{2,0},{3,1},{4,6},{5,7},{6,4},{7,5},{8,10},{9,11},{10,... | collective-permute-start | bytes 786440 | tf_op jit(solution)/shard_map/ppermute | solution.py:22
  47.1 9.8 %collective-permute-start.12 = (bf16[32,8,512]{2,1,0:T(8,128)(2,1)S(1)}, bf16[32,8,512]{2,1,0:T(8,128)(2,1)S(1)}, u32[]{:S(2)}, u32[]{:S(2)}) collective-permute-start(bf16[32,8,512]{2,1,0:T(8,128)(2,1)S(1)} %all-to-all-done.refs_0_), channel_id=1, source_target_pairs={{0,3},{1,0},{2,1},{3,2},{4,7},{5,4},{6,5},{7,6},{8,11},{9,8},{10,9... | collective-permute-start | bytes 786440 | tf_op jit(solution)/shard_map/ppermute | solution.py:22
  60.8 4.7 %copy-start.1 = (bf16[64,3584]{1,0:T(8,128)(2,1)S(1)}, bf16[64,3584]{1,0:T(8,128)(2,1)}, u32[]{:S(2)}) copy-start(bf16[64,3584]{1,0:T(8,128)(2,1)} %copy-done) | copy-start | bytes 1376260
  60.8 4.7 %copy-start.3 = (bf16[64,3584]{1,0:T(8,128)(2,1)S(1)}, bf16[64,3584]{1,0:T(8,128)(2,1)}, u32[]{:S(2)}) copy-start(bf16[64,3584]{1,0:T(8,128)(2,1)} %copy-done.2) | copy-start | bytes 1376260
  61.0 12.9 %collective-permute-start.16 = (bf16[96,3584]{1,0:T(8,128)(2,1)S(1)}, bf16[96,3584]{1,0:T(8,128)(2,1)S(1)}, u32[]{:S(2)}, u32[]{:S(2)}) collective-permute-start(bf16[96,3584]{1,0:T(8,128)(2,1)S(1)} %get-tuple-element.101), channel_id=1, source_target_pairs={{0,192},{64,0},{128,64},{192,128},{1,193},{65,1},{129,65},{193,129... | collective-permute-start | bytes 2064392 | tf_op jit(solution)/shard_map/ppermute | solution.py:22
  61.7 13.4 %collective-permute-start.17 = (bf16[96,3584]{1,0:T(8,128)(2,1)S(1)}, bf16[96,3584]{1,0:T(8,128)(2,1)S(1)}, u32[]{:S(2)}, u32[]{:S(2)}) collective-permute-start(bf16[96,3584]{1,0:T(8,128)(2,1)S(1)} %get-tuple-element.100), channel_id=1, source_target_pairs={{0,64},{64,128},{128,192},{192,0},{1,65},{65,129},{129,193},{193,1... | collective-permute-start | bytes 2064392 | tf_op jit(solution)/shard_map/ppermute | solution.py:22
  62.5 7.7 %collective-permute-start.15 = (bf16[64,3584]{1,0:T(8,128)(2,1)S(1)}, bf16[64,3584]{1,0:T(8,128)(2,1)S(1)}, u32[]{:S(2)}, u32[]{:S(2)}) collective-permute-start(bf16[64,3584]{1,0:T(8,128)(2,1)S(1)} %pad_maximum_fusion.5), channel_id=1, source_target_pairs={{0,48},{16,0},{32,16},{48,32},{1,49},{17,1},{33,17},{49,33},{2,50}... | collective-permute-start | bytes 1376264 | tf_op jit(solution)/shard_map/ppermute | solution.py:22
  75.8 8.4 %collective-permute-start.19 = (bf16[256,2560]{1,0:T(8,128)(2,1)S(1)}, bf16[256,2560]{1,0:T(8,128)(2,1)S(1)}, u32[]{:S(2)}, u32[]{:S(2)}) collective-permute-start(bf16[256,2560]{1,0:T(8,128)(2,1)S(1)} %get-tuple-element.83), channel_id=1, source_target_pairs={{0,8},{8,0},{1,9},{9,1},{2,10},{10,2},{3,11},{11,3},{4,12},{12,4},... | collective-permute-start | bytes 3932168 | tf_op jit(solution)/shard_map/ppermute | solution.py:22
  81.5 3.7 %collective-permute-start.18 = (bf16[256,1024]{1,0:T(8,128)(2,1)S(1)}, bf16[256,1024]{1,0:T(8,128)(2,1)S(1)}, u32[]{:S(2)}, u32[]{:S(2)}) collective-permute-start(bf16[256,1024]{1,0:T(8,128)(2,1)S(1)} %get-tuple-element.82), channel_id=1, source_target_pairs={{0,8},{8,0},{1,9},{9,1},{2,10},{10,2},{3,11},{11,3},{4,12},{12,4},... | collective-permute-start | bytes 1572872 | tf_op jit(solution)/shard_map/ppermute | solution.py:22
  (6 other events, 10.7 us)
